TPU v7x, 32 devices: a whole 2x2x4 slice. The times are simulated.
32 devices in a mesh: seq: 4 (over z), heads: 8 (over y, x, core).
Axes of the slice: x: 2, y: 2, z: 4, core: 2. Of those that a mesh axis runs over, the one named last changes fastest.
Arguments:
- hidden_in: bfloat16 [1024, 4, 2048], P(('seq', 'heads')), may hold values from -6 to 6
- grad_out: bfloat16 [1024, 4, 2048], P(('seq', 'heads')), may hold values from -6 to 6
- lengths: int32 [4], replicated, may hold values from 512 to 1024, as said below
- norm_gain: bfloat16 [3, 2048], P(None, 'seq'), may hold values from 0.5 to 1.5
- w_z: bfloat16 [3, 2048, 4096], P(None, 'seq', 'heads'), may hold values from -0.125 to 0.125
- w_x: bfloat16 [3, 2048, 4096], P(None, 'seq', 'heads'), may hold values from -0.125 to 0.125
- w_bc: bfloat16 [3, 2048, 256], P(None, 'seq'), may hold values from -0.125 to 0.125
- w_dt: bfloat16 [3, 2048, 64], P(None, 'seq', 'heads'), may hold values from -0.125 to 0.125
- conv_x: float32 [3, 4, 4096], P(None, None, 'heads'), may hold values from -3 to 3
- conv_x_bias: float32 [3, 4096], P(None, 'heads'), may hold values from -2 to 2
- conv_bc: float32 [3, 4, 256], replicated, may hold values from -3 to 3
- conv_bc_bias: float32 [3, 256], replicated, may hold values from -2 to 2
- dt_bias: float32 [3, 64], P(None, 'heads'), may hold values from -7 to -2
- a_log: float32 [3, 64], P(None, 'heads'), may hold values from -2 to 1
- d_skip: float32 [3, 64], P(None, 'heads'), may hold values from 0.5 to 1.5
- y_gain: float32 [3, 4096], P(None, 'heads'), may hold values from 0.5 to 1.5
- w_out: bfloat16 [3, 4096, 2048], P(None, 'heads', 'seq'), may hold values from -0.09375 to 0.09375
Outputs:
- hidden_out: float32 [1024, 4, 2048], P(('seq', 'heads'))
- grad_in: float32 [1024, 4, 2048], P(('seq', 'heads'))
- d_norm_gain: float32 [3, 2048], P(None, 'seq')
- d_w_z: float32 [3, 2048, 4096], P(None, 'seq', 'heads')
- d_w_x: float32 [3, 2048, 4096], P(None, 'seq', 'heads')
- d_w_bc: float32 [3, 2048, 256], P(None, 'seq')
- d_w_dt: float32 [3, 2048, 64], P(None, 'seq', 'heads')
- d_conv_x: float32 [3, 4, 4096], P(None, None, 'heads')
- d_conv_x_bias: float32 [3, 4096], P(None, 'heads')
- d_conv_bc: float32 [3, 4, 256], replicated
- d_conv_bc_bias: float32 [3, 256], replicated
- d_dt_bias: float32 [3, 64], P(None, 'heads')
- d_a_log: float32 [3, 64], P(None, 'heads')
- d_d_skip: float32 [3, 64], P(None, 'heads')
- d_y_gain: float32 [3, 4096], P(None, 'heads')
- d_w_out: float32 [3, 4096, 2048], P(None, 'heads', 'seq')
Inputs may be any that keep to these rules, and one draw needn't show every extreme that they name: `lengths`: one of the 4 sequences fills all 1024 positions; positions at or past a sequence's length are padding.
All inputs are finite; a program needn't handle non-finite values.
Results may differ from a plain program's by a relative error of at most 0.035.
Values may be sent and summed in bfloat16 or wider, within the bound.
No kernel may reach another device: no remote copies, remote signals or barrier semaphores. Data moves between devices by JAX's collectives and lax.ppermute only.
A program may use at most 256 MiB of HBM per device.

v0:
```python
import jax
import jax.numpy as jnp
from jax import lax
from jax.sharding import PartitionSpec as P

EPSILON = 1e-05
PRECISE = lax.Precision.HIGHEST


def shifted(x, axis, by):
    count = lax.axis_size(axis)
    pairs = [(i, i + by) for i in range(count) if 0 <= i + by < count]
    return lax.ppermute(x, axis, pairs)


def carried_in(x, axis, combine, identity):
    count, here = (lax.axis_size(axis), lax.axis_index(axis))
    everything = jax.tree.map(
        lambda part, kind: lax.all_gather(part.astype(kind), axis), x, (jnp.bfloat16, jnp.bfloat16)
    )
    start = jax.tree.map(
        lambda part, zero: jnp.broadcast_to(jnp.asarray(zero, part.dtype), part.shape), x, identity
    )

    def hop(k, before):
        reached = k < here
        new = combine(
            before, jax.tree.map(lambda part, own: part[k].astype(own.dtype), everything, x)
        )
        return jax.tree.map(lambda a, b: jnp.where(reached, a, b), new, before)

    return lax.fori_loop(0, count, hop, start)


def prefix(x, axis, join, neutral):
    count = lax.axis_size(axis)
    place = lax.axis_index(axis)
    ahead = count - 1 - place
    gathered = jax.tree.map(
        lambda a, kind: lax.all_gather(a.astype(kind), axis),
        x,
        jax.tree.map(lambda a: jnp.bfloat16 if a.dtype == jnp.float32 else a.dtype, x),
    )
    state = jax.tree.map(lambda a, e: jnp.zeros_like(a) + jnp.asarray(e, a.dtype), x, neutral)

    def one(hop, state):
        source = count - 1 - hop
        return join(
            state,
            jax.tree.map(
                lambda a, own: lax.dynamic_index_in_dim(a, source, 0, False).astype(own.dtype),
                gathered,
                x,
            ),
        )

    return lax.fori_loop(0, ahead, one, state)


def norm_rows(x_res, gain_row):
    factor = lax.rsqrt(jnp.mean(x_res * x_res, axis=-1, keepdims=True) + EPSILON)
    return x_res * factor * gain_row


def conv_act(feed_ext, kernel_w, kernel_b, valid_rows):
    length = valid_rows.shape[0]
    running = kernel_b
    for offset in range(kernel_w.shape[0]):
        running = running + kernel_w[offset] * feed_ext[offset : offset + length]
    return jax.nn.silu(running) * valid_rows[:, :, None]


def rates(raw_dt, bias_dt, log_rate, valid_rows):
    stepped = jax.nn.softplus(raw_dt + bias_dt) * valid_rows[:, :, None]
    rising = jnp.cumsum(jnp.exp(log_rate) * stepped, axis=0)
    return (stepped, rising)


def mixing(scores, rising, stepped):
    length = rising.shape[0]
    causal = jnp.arange(length)[:, None] >= jnp.arange(length)[None, :]
    levels = jnp.transpose(rising, (1, 2, 0))
    spread_gap = jnp.where(causal, levels[:, :, None, :] - levels[:, :, :, None], 0.0)
    decays = jnp.where(causal, jnp.exp(spread_gap), 0.0)
    return scores[:, None] * decays * jnp.transpose(stepped, (1, 2, 0))[:, :, None, :]


def block_state(value_heads, key_rows, rising, stepped):
    closing = rising[-1]
    weighting = jnp.exp(rising - closing[None]) * stepped
    return (
        jnp.exp(-closing),
        jnp.einsum("smh,smhp,smn->mhpn", weighting, value_heads, key_rows, precision=PRECISE),
    )


def gated_rows(diagonal, rising, carried, value_heads, query_rows, gate_rows, skip_gain):
    offdiag = jnp.exp(-rising)[..., None] * jnp.einsum(
        "tmn,mhpn->tmhp", query_rows, carried, precision=PRECISE
    )
    joined = diagonal + offdiag + skip_gain[:, None] * value_heads
    joined = joined.reshape(joined.shape[0], joined.shape[1], -1)
    return joined * jax.nn.silu(gate_rows)


def link(earlier, later):
    return (earlier[0] * later[0], later[0][:, :, None, None] * earlier[1] + later[1])


def stack_sets(groups):
    return tuple(
        (jnp.stack([member[place] for member in groups]) for place in range(len(groups[0])))
    )


def shards(
    hidden_in,
    grad_out,
    lengths,
    norm_gain,
    w_z,
    w_x,
    w_bc,
    w_dt,
    conv_x,
    conv_x_bias,
    conv_bc,
    conv_bc_bias,
    dt_bias,
    a_log,
    d_skip,
    y_gain,
    w_out,
):
    layers = w_z.shape[0]
    heads_here = w_dt.shape[2]
    inner_here = w_z.shape[2]
    head_size = inner_here // heads_here
    state_size = w_bc.shape[2] // 2
    kernel = conv_x.shape[1]
    own_rows = hidden_in.shape[0]
    batches = hidden_in.shape[1]
    model_width = hidden_in.shape[2]
    block_rows = own_rows * lax.axis_size("heads")
    inner_all = inner_here * lax.axis_size("heads")
    seq_rows = model_width // lax.axis_size("seq")
    places = lax.axis_index("seq") * block_rows + jnp.arange(block_rows)
    valid_rows = (places[:, None] < lengths[None, :]).astype(jnp.float32)

    def gather_weights(layer_index):
        return (
            lax.all_gather(w_z[layer_index], "seq", axis=0, tiled=True),
            lax.all_gather(w_x[layer_index], "seq", axis=0, tiled=True),
            lax.all_gather(w_bc[layer_index], "seq", axis=0, tiled=True),
            lax.all_gather(w_dt[layer_index], "seq", axis=0, tiled=True),
            lax.all_gather(w_out[layer_index], "seq", axis=1, tiled=True),
            lax.all_gather(norm_gain[layer_index], "seq", axis=0, tiled=True),
        )

    x_res = hidden_in.astype(jnp.float32)
    stored = []
    for layer_index in range(layers):
        gathered = gather_weights(layer_index)
        gate_w, mixed_w, shared_w, raw_w, out_w, gain_row = gathered
        gain_wide = gain_row.astype(jnp.float32)
        normed = norm_rows(x_res, gain_wide).astype(jnp.bfloat16)
        block_in = lax.all_gather(normed, "heads", axis=0, tiled=True)
        gate_rows = jnp.einsum("tmd,dc->tmc", block_in, gate_w, preferred_element_type=jnp.float32)
        mixed = jnp.einsum("tmd,dc->tmc", block_in, mixed_w, preferred_element_type=jnp.float32)
        shared = jnp.einsum("tmd,dc->tmc", block_in, shared_w, preferred_element_type=jnp.float32)
        raw_dt = jnp.einsum("tmd,dc->tmc", block_in, raw_w, preferred_element_type=jnp.float32)
        feed = jnp.concatenate([mixed, shared], axis=-1)
        rim_rows = shifted(feed[block_rows - kernel + 1 :], "seq", 1)
        feed_ext = jnp.concatenate([rim_rows, feed], axis=0)
        kernel_w = jnp.concatenate([conv_x[layer_index], conv_bc[layer_index]], axis=-1)
        kernel_b = jnp.concatenate([conv_x_bias[layer_index], conv_bc_bias[layer_index]], axis=-1)
        active = conv_act(feed_ext, kernel_w, kernel_b, valid_rows)
        value_low = (
            active[..., :inner_here]
            .astype(jnp.bfloat16)
            .reshape(block_rows, batches, heads_here, head_size)
        )
        key_low = active[..., inner_here : inner_here + state_size].astype(jnp.bfloat16)
        query_low = active[..., inner_here + state_size :].astype(jnp.bfloat16)
        stepped, rising = rates(raw_dt, dt_bias[layer_index], a_log[layer_index], valid_rows)
        scores = jnp.einsum("tmn,smn->mts", query_low, key_low, preferred_element_type=jnp.float32)
        mix_low = mixing(scores, rising, stepped).astype(jnp.bfloat16)
        diagonal = jnp.einsum(
            "mhts,smhp->tmhp", mix_low, value_low, preferred_element_type=jnp.float32
        )
        value_heads = value_low.astype(jnp.float32)
        key_rows = key_low.astype(jnp.float32)
        query_rows = query_low.astype(jnp.float32)
        fading, local_state = block_state(value_heads, key_rows, rising, stepped)
        ignored, carried = carried_in(
            (fading, local_state), "seq", link, (jnp.ones_like(fading), jnp.zeros_like(local_state))
        )
        gated = gated_rows(
            diagonal, rising, carried, value_heads, query_rows, gate_rows, d_skip[layer_index]
        )
        squares = lax.psum(jnp.sum(gated * gated, axis=-1), "heads")
        factor = lax.rsqrt(squares / inner_all + EPSILON)[..., None]
        normal_out = (gated * factor * y_gain[layer_index]).astype(jnp.bfloat16)

        def project(first_row, row_count, normal_out=normal_out, out_w=out_w):
            return jnp.einsum("tmc,cd->tmd", normal_out, out_w, preferred_element_type=jnp.float32)

        branch = lax.psum_scatter(
            project(jnp.int32(0), lax.axis_size("heads") * own_rows).astype(jnp.bfloat16),
            "heads",
            scatter_dimension=0,
            tiled=True,
        ).astype(jnp.float32)
        stored.append(
            {
                "gathered": gathered,
                "x_res": x_res,
                "block_in": block_in,
                "gate_rows": gate_rows,
                "raw_dt": raw_dt,
                "feed_ext": feed_ext,
                "kernel_w": kernel_w,
                "kernel_b": kernel_b,
                "value_low": value_low,
                "value_heads": value_heads,
                "key_rows": key_rows,
                "query_rows": query_rows,
                "stepped": stepped,
                "rising": rising,
                "scores": scores,
                "mix_low": mix_low,
                "diagonal": diagonal,
                "fading": fading,
                "carried": carried,
                "gated": gated,
                "factor": factor,
                "normal_out": normal_out,
            }
        )
        x_res = x_res + branch
    grad_res = grad_out.astype(jnp.float32)
    sharded_grads = [None] * layers
    local_sets = [None] * layers
    shared_sets = [None] * layers
    reduced_sets = [None] * layers
    for layer_index in reversed(range(layers)):
        saved = stored[layer_index]
        gate_w, mixed_w, shared_w, raw_w, out_w, gain_row = gather_weights(layer_index)
        gain_wide = gain_row.astype(jnp.float32)
        grad_low = grad_res.astype(jnp.bfloat16)
        grad_block = lax.all_gather(grad_low, "heads", axis=0, tiled=True)
        d_normal = jnp.einsum("tmd,cd->tmc", grad_block, out_w, preferred_element_type=jnp.float32)
        d_out_w = jnp.einsum(
            "tmc,tmd->cd", saved["normal_out"], grad_block, preferred_element_type=jnp.float32
        )
        gated = saved["gated"]
        factor = saved["factor"]
        scaled = d_normal * y_gain[layer_index]
        cross = lax.psum(jnp.sum(scaled * gated, axis=-1), "heads")[..., None]
        d_gated = factor * scaled - gated * (factor * factor * factor) * cross / inner_all
        d_y_gain = jnp.sum(d_normal * gated * factor, axis=(0, 1))
        rising = saved["rising"]
        stepped = saved["stepped"]
        value_heads = saved["value_heads"]
        key_rows = saved["key_rows"]
        query_rows = saved["query_rows"]
        ignored, back_rows = jax.vjp(
            gated_rows,
            saved["diagonal"],
            rising,
            saved["carried"],
            value_heads,
            query_rows,
            saved["gate_rows"],
            d_skip[layer_index],
        )
        d_diagonal, d_rise_a, d_carried, d_value_a, d_query_a, d_gate, d_skip_here = back_rows(
            d_gated
        )
        ignored, d_after = prefix(
            (saved["fading"], d_carried),
            "seq",
            link,
            (jnp.ones_like(saved["fading"]), jnp.zeros_like(d_carried)),
        )
        d_fading = jnp.sum(d_after * saved["carried"], axis=(2, 3))
        ignored, back_state = jax.vjp(block_state, value_heads, key_rows, rising, stepped)
        d_value_b, d_key_b, d_rise_b, d_step_b = back_state((d_fading, d_after))
        d_diag_low = d_diagonal.astype(jnp.bfloat16)
        d_mix = jnp.einsum(
            "tmhp,smhp->mhts", d_diag_low, saved["value_low"], preferred_element_type=jnp.float32
        )
        d_value_c = jnp.einsum(
            "mhts,tmhp->smhp", saved["mix_low"], d_diag_low, preferred_element_type=jnp.float32
        )
        ignored, back_mix = jax.vjp(mixing, saved["scores"], rising, stepped)
        d_scores, d_rise_c, d_step_c = back_mix(d_mix)
        d_query_c = jnp.einsum("mts,smn->tmn", d_scores, key_rows, precision=PRECISE)
        d_key_c = jnp.einsum("mts,tmn->smn", d_scores, query_rows, precision=PRECISE)
        ignored, back_rates = jax.vjp(
            lambda raw_in, bias_in, rate_in: rates(raw_in, bias_in, rate_in, valid_rows),
            saved["raw_dt"],
            dt_bias[layer_index],
            a_log[layer_index],
        )
        d_raw, d_bias_dt, d_log_rate = back_rates(
            (d_step_b + d_step_c, d_rise_a + d_rise_b + d_rise_c)
        )
        d_values = (d_value_a + d_value_b + d_value_c).reshape(block_rows, batches, inner_here)
        d_active = jnp.concatenate([d_values, d_key_b + d_key_c, d_query_a + d_query_c], axis=-1)
        ignored, back_conv = jax.vjp(
            lambda feed_in, weight_in, bias_in: conv_act(feed_in, weight_in, bias_in, valid_rows),
            saved["feed_ext"],
            saved["kernel_w"],
            saved["kernel_b"],
        )
        d_feed_ext, d_kernel_w, d_kernel_b = back_conv(d_active)
        rim_back = shifted(d_feed_ext[: kernel - 1], "seq", -1)
        d_feed = d_feed_ext[kernel - 1 :]
        d_feed = jnp.concatenate(
            [d_feed[: block_rows - kernel + 1], d_feed[block_rows - kernel + 1 :] + rim_back],
            axis=0,
        )
        d_gate_low = d_gate.astype(jnp.bfloat16)
        d_mixed_low = d_feed[..., :inner_here].astype(jnp.bfloat16)
        d_shared = d_feed[..., inner_here:]
        d_raw_low = d_raw.astype(jnp.bfloat16)
        shared_wide = shared_w.astype(jnp.float32)

        def spread(
            first_row,
            row_count,
            gate_w=gate_w,
            mixed_w=mixed_w,
            raw_w=raw_w,
            d_gate_low=d_gate_low,
            d_mixed_low=d_mixed_low,
            d_raw_low=d_raw_low,
            d_shared=d_shared,
            shared_wide=shared_wide,
        ):
            running = jnp.einsum(
                "tmc,dc->tmd", d_gate_low, gate_w, preferred_element_type=jnp.float32
            )
            running = running + jnp.einsum(
                "tmc,dc->tmd", d_mixed_low, mixed_w, preferred_element_type=jnp.float32
            )
            running = running + jnp.einsum(
                "tmc,dc->tmd", d_raw_low, raw_w, preferred_element_type=jnp.float32
            )
            return running + jnp.einsum("tmc,dc->tmd", d_shared, shared_wide, precision=PRECISE)

        d_normed = lax.psum_scatter(
            spread(jnp.int32(0), lax.axis_size("heads") * own_rows).astype(jnp.bfloat16),
            "heads",
            scatter_dimension=0,
            tiled=True,
        ).astype(jnp.float32)
        ignored, back_norm = jax.vjp(norm_rows, saved["x_res"], gain_wide)
        d_x_res, d_gain = back_norm(d_normed)
        grad_res = grad_res + d_x_res
        block_in = saved["block_in"]
        d_gate_w = jnp.einsum(
            "tmd,tmc->dc", block_in, d_gate_low, preferred_element_type=jnp.float32
        )
        d_mixed_w = jnp.einsum(
            "tmd,tmc->dc", block_in, d_mixed_low, preferred_element_type=jnp.float32
        )
        d_raw_w = jnp.einsum("tmd,tmc->dc", block_in, d_raw_low, preferred_element_type=jnp.float32)
        d_shared_w = jnp.einsum(
            "tmd,tmc->dc", block_in.astype(jnp.float32), d_shared, precision=PRECISE
        )
        sharded_grads[layer_index] = (
            lax.psum_scatter(
                d_gate_w.astype(jnp.bfloat16), "seq", scatter_dimension=0, tiled=True
            ).astype(jnp.float32),
            lax.psum_scatter(
                d_mixed_w.astype(jnp.bfloat16), "seq", scatter_dimension=0, tiled=True
            ).astype(jnp.float32),
            lax.psum_scatter(
                d_raw_w.astype(jnp.bfloat16), "seq", scatter_dimension=0, tiled=True
            ).astype(jnp.float32),
            lax.psum_scatter(
                d_out_w.astype(jnp.bfloat16), "seq", scatter_dimension=1, tiled=True
            ).astype(jnp.float32),
        )
        shared_sets[layer_index] = (
            d_gain,
            d_shared_w,
            d_kernel_w[:, inner_here:],
            d_kernel_b[inner_here:],
        )
        local_sets[layer_index] = (
            d_kernel_w[:, :inner_here],
            d_kernel_b[:inner_here],
            d_bias_dt,
            d_log_rate,
            d_skip_here,
            d_y_gain,
        )
        reduced_sets[layer_index] = (
            lax.psum(local_sets[layer_index], "seq"),
            lax.psum(shared_sets[layer_index], ("seq", "heads")),
        )
    local_total = stack_sets([member[0] for member in reduced_sets])
    shared_total = stack_sets([member[1] for member in reduced_sets])
    weight_total = stack_sets(sharded_grads)
    seq_start = lax.axis_index("seq") * seq_rows
    gain_grad = lax.dynamic_slice_in_dim(shared_total[0], seq_start, seq_rows, 1)
    shared_grad = lax.dynamic_slice_in_dim(shared_total[1], seq_start, seq_rows, 1)
    conv_grad = shared_total[2]
    conv_bias_grad = shared_total[3]
    return (
        x_res,
        grad_res,
        gain_grad,
        weight_total[0],
        weight_total[1],
        shared_grad,
        weight_total[2],
        local_total[0],
        local_total[1],
        conv_grad,
        conv_bias_grad,
        local_total[2],
        local_total[3],
        local_total[4],
        local_total[5],
        weight_total[3],
    )


def solution(mesh):
    placed = (
        P(("seq", "heads"), None, None),
        P(("seq", "heads"), None, None),
        P(),
        P(None, "seq"),
        P(None, "seq", "heads"),
        P(None, "seq", "heads"),
        P(None, "seq", None),
        P(None, "seq", "heads"),
        P(None, None, "heads"),
        P(None, "heads"),
        P(),
        P(),
        P(None, "heads"),
        P(None, "heads"),
        P(None, "heads"),
        P(None, "heads"),
        P(None, "heads", "seq"),
    )
    return jax.shard_map(
        shards,
        mesh=mesh,
        in_specs=placed,
        out_specs=(
            P(("seq", "heads"), None, None),
            P(("seq", "heads"), None, None),
            P(None, "seq"),
            P(None, "seq", "heads"),
            P(None, "seq", "heads"),
            P(None, "seq", None),
            P(None, "seq", "heads"),
            P(None, None, "heads"),
            P(None, "heads"),
            P(),
            P(),
            P(None, "heads"),
            P(None, "heads"),
            P(None, "heads"),
            P(None, "heads"),
            P(None, "heads", "seq"),
        ),
        check_vma=False,
    )
```

profile of v0, /device:TPU:9, one launch (start us, length us, event | category | flops | bytes accessed | tf_op | source)
XLA Modules:
  0.0 2398.4 jit_solution(14839209425192188334)
XLA Ops:
  41.6 20.5 all-gather.49.cloned.1.call-done
  70.0 21.5 all-gather.63.cloned.1.call-done
  96.3 41.3 %all-gather.61.cloned.1.call-done = bf16[1,2048,512]{2,1,0:T(8,128)(2,1)} async-done(((bf16[1,512,512]{2,1,0:T(8,128)(2,1)}), bf16[1,2048,512]{2,1,0:T(8,128)(2,1)}) %all-gather.61.cloned.1.call-update) | async-done | bytes 2097168 | tf_op jit(solution)/shard_map/all_gather | solution.py:153
  178.3 25.4 %all-gather.65.cloned.1.call-done = bf16[16,8,64,128]{3,2,1,0:T(8,128)(2,1)} async-done(((bf16[4,8,64,128]{3,2,1,0:T(8,128)(2,1)}), bf16[16,8,64,128]{3,2,1,0:T(8,128)(2,1)}) %all-gather.65.cloned.1.call-update) | async-done | bytes 2097168 | tf_op jit(solution)/shard_map/all_gather | solution.py:19
  217.2 32.6 %all-gather.67.cloned.1.call-done = bf16[1,2048,512]{2,1,0:T(8,128)(2,1)} async-done(((bf16[1,512,512]{2,1,0:T(8,128)(2,1)}), bf16[1,2048,512]{2,1,0:T(8,128)(2,1)}) %all-gather.67.cloned.1.call-update) | async-done | bytes 2097168 | tf_op jit(solution)/shard_map/all_gather | solution.py:152
  257.2 12.5 psum.252
  270.3 26.0 %all-gather.69.cloned.1.call-done = bf16[1,512,2048]{2,1,0:T(8,128)(2,1)} async-done(((bf16[1,512,512]{2,1,0:T(8,128)(2,1)}), bf16[1,512,2048]{2,1,0:T(8,128)(2,1)}) %all-gather.69.cloned.1.call-update) | async-done | bytes 2097168 | tf_op jit(solution)/shard_map/all_gather | solution.py:156
  312.9 42.1 %reduce-scatter.19.cloned.1.call-done = bf16[32,4,2048]{2,0,1:T(8,128)(2,1)} async-done(((bf16[256,4,2048]{2,0,1:T(8,128)(2,1)}), bf16[32,4,2048]{2,0,1:T(8,128)(2,1)}) %reduce-scatter.19.cloned.1.call-update) | async-done | bytes 524304 | tf_op jit(solution)/shard_map/reduce_scatter | solution.py:208
  361.0 11.0 all-gather.10
  372.7 23.4 all-gather.51.cloned.1.call-done
  403.4 22.2 all-gather.73.cloned.1.call-done
  430.4 40.6 %all-gather.71.cloned.1.call-done = bf16[1,2048,512]{2,1,0:T(8,128)(2,1)} async-done(((bf16[1,512,512]{2,1,0:T(8,128)(2,1)}), bf16[1,2048,512]{2,1,0:T(8,128)(2,1)}) %all-gather.71.cloned.1.call-update) | async-done | bytes 2097168 | tf_op jit(solution)/shard_map/all_gather | solution.py:153
  506.0 31.9 %all-gather.75.cloned.1.call-done = bf16[16,8,64,128]{3,2,1,0:T(8,128)(2,1)} async-done(((bf16[4,8,64,128]{3,2,1,0:T(8,128)(2,1)}), bf16[16,8,64,128]{3,2,1,0:T(8,128)(2,1)}) %all-gather.75.cloned.1.call-update) | async-done | bytes 2097168 | tf_op jit(solution)/shard_map/all_gather | solution.py:19
  551.9 32.2 %all-gather.77.cloned.1.call-done = bf16[1,2048,512]{2,1,0:T(8,128)(2,1)} async-done(((bf16[1,512,512]{2,1,0:T(8,128)(2,1)}), bf16[1,2048,512]{2,1,0:T(8,128)(2,1)}) %all-gather.77.cloned.1.call-update) | async-done | bytes 2097168 | tf_op jit(solution)/shard_map/all_gather | solution.py:152
  591.6 12.5 psum.253
  604.7 25.7 %all-gather.79.cloned.1.call-done = bf16[1,512,2048]{2,1,0:T(8,128)(2,1)} async-done(((bf16[1,512,512]{2,1,0:T(8,128)(2,1)}), bf16[1,512,2048]{2,1,0:T(8,128)(2,1)}) %all-gather.79.cloned.1.call-update) | async-done | bytes 2097168 | tf_op jit(solution)/shard_map/all_gather | solution.py:156
  647.0 42.2 %reduce-scatter.21.cloned.1.call-done = bf16[32,4,2048]{2,0,1:T(8,128)(2,1)} async-done(((bf16[256,4,2048]{2,0,1:T(8,128)(2,1)}), bf16[32,4,2048]{2,0,1:T(8,128)(2,1)}) %reduce-scatter.21.cloned.1.call-update) | async-done | bytes 524304 | tf_op jit(solution)/shard_map/reduce_scatter | solution.py:208
  695.3 10.9 all-gather.17
  706.7 23.6 all-gather.53.cloned.1.call-done
  738.2 20.8 all-gather.83.cloned.1.call-done
  762.8 41.5 %all-gather.81.cloned.1.call-done = bf16[1,2048,512]{2,1,0:T(8,128)(2,1)} async-done(((bf16[1,512,512]{2,1,0:T(8,128)(2,1)}), bf16[1,2048,512]{2,1,0:T(8,128)(2,1)}) %all-gather.81.cloned.1.call-update) | async-done | bytes 2097168 | tf_op jit(solution)/shard_map/all_gather | solution.py:153
  851.3 23.8 all-gather.85.cloned.1.call-done
  894.8 26.5 %all-gather.87.cloned.1.call-done = bf16[1,2048,512]{2,1,0:T(8,128)(2,1)} async-done(((bf16[1,512,512]{2,1,0:T(8,128)(2,1)}), bf16[1,2048,512]{2,1,0:T(8,128)(2,1)}) %all-gather.87.cloned.1.call-update) | async-done | bytes 2097168 | tf_op jit(solution)/shard_map/all_gather | solution.py:152
  929.4 12.1 psum.254
  941.5 25.9 %all-gather.89.cloned.1.call-done = bf16[1,512,2048]{2,1,0:T(8,128)(2,1)} async-done(((bf16[1,512,512]{2,1,0:T(8,128)(2,1)}), bf16[1,512,2048]{2,1,0:T(8,128)(2,1)}) %all-gather.89.cloned.1.call-update) | async-done | bytes 2097168 | tf_op jit(solution)/shard_map/all_gather | solution.py:156
  967.4 39.7 %all-gather.55.cloned.1.call-done = bf16[256,4,2048]{2,0,1:T(8,128)(2,1)} async-done(((bf16[32,4,2048]{2,0,1:T(8,128)(2,1)}), bf16[256,4,2048]{2,0,1:T(8,128)(2,1)}) %all-gather.55.cloned.1.call-update) | async-done | bytes 4194320 | tf_op jit(solution)/shard_map/all_gather | solution.py:251
  1014.9 11.4 psum.255
  1070.0 14.6 all-gather.91.cloned.1.call-done
  1171.4 10.1 add_convert_fusion.2
  1181.6 50.9 %reduce-scatter.25.cloned.1.call-done = bf16[32,4,2048]{2,0,1:T(8,128)(2,1)} async-done(((bf16[256,4,2048]{2,0,1:T(8,128)(2,1)}), bf16[32,4,2048]{2,0,1:T(8,128)(2,1)}) %reduce-scatter.25.cloned.1.call-update) | async-done | bytes 524304 | tf_op jit(solution)/shard_map/reduce_scatter | solution.py:353
  1237.7 37.2 %all-gather.57.cloned.1.call-done = bf16[256,4,2048]{2,0,1:T(8,128)(2,1)} async-done(((bf16[32,4,2048]{2,0,1:T(8,128)(2,1)}), bf16[256,4,2048]{2,0,1:T(8,128)(2,1)}) %all-gather.57.cloned.1.call-update) | async-done | bytes 4194320 | tf_op jit(solution)/shard_map/all_gather | solution.py:251
  1282.7 11.4 psum.256
  1335.0 15.8 all-gather.93.cloned.1.call-done
  1443.3 43.2 %reduce-scatter.27.cloned.1.call-done = bf16[32,4,2048]{2,0,1:T(8,128)(2,1)} async-done(((bf16[256,4,2048]{2,0,1:T(8,128)(2,1)}), bf16[32,4,2048]{2,0,1:T(8,128)(2,1)}) %reduce-scatter.27.cloned.1.call-update) | async-done | bytes 524304 | tf_op jit(solution)/shard_map/reduce_scatter | solution.py:353
  1488.8 52.2 %reduce-scatter.23.cloned.1.call-done = bf16[32,4,2048]{2,0,1:T(8,128)(2,1)} async-done(((bf16[256,4,2048]{2,0,1:T(8,128)(2,1)}), bf16[32,4,2048]{2,0,1:T(8,128)(2,1)}) %reduce-scatter.23.cloned.1.call-update) | async-done | bytes 524304 | tf_op jit(solution)/shard_map/reduce_scatter | solution.py:208
  1544.9 37.2 %all-gather.59.cloned.1.call-done = bf16[256,4,2048]{2,0,1:T(8,128)(2,1)} async-done(((bf16[32,4,2048]{2,0,1:T(8,128)(2,1)}), bf16[256,4,2048]{2,0,1:T(8,128)(2,1)}) %all-gather.59.cloned.1.call-update) | async-done | bytes 4194320 | tf_op jit(solution)/shard_map/all_gather | solution.py:251
  1590.0 11.6 psum.257
  1636.2 21.5 all-gather.95.cloned.1.call-done
  1844.0 15.4 all-reduce.29
  1867.7 30.2 %reduce-scatter.35.cloned.1.call-done = bf16[512,512]{1,0:T(8,128)(2,1)} async-done(((bf16[2048,512]{1,0:T(8,128)(2,1)}), bf16[512,512]{1,0:T(8,128)(2,1)}) %reduce-scatter.35.cloned.1.call-update) | async-done | bytes 524304 | tf_op jit(solution)/shard_map/reduce_scatter | solution.py:374
  1897.9 45.5 %reduce-scatter.33.cloned.1.call-done = bf16[512,512]{1,0:T(8,128)(2,1)} async-done(((bf16[2048,512]{1,0:T(8,128)(2,1)}), bf16[512,512]{1,0:T(8,128)(2,1)}) %reduce-scatter.33.cloned.1.call-update) | async-done | bytes 524304 | tf_op jit(solution)/shard_map/reduce_scatter | solution.py:374
  1943.4 45.6 %reduce-scatter.31.cloned.1.call-done = bf16[512,512]{1,0:T(8,128)(2,1)} async-done(((bf16[2048,512]{1,0:T(8,128)(2,1)}), bf16[512,512]{1,0:T(8,128)(2,1)}) %reduce-scatter.31.cloned.1.call-update) | async-done | bytes 524304 | tf_op jit(solution)/shard_map/reduce_scatter | solution.py:374
  1992.3 160.8 %all-reduce.32.cloned.1.call-done = (f32[1,2048,256]{2,1,0:T(8,128)}, f32[1,2048,256]{2,1,0:T(8,128)}, f32[1,2048,256]{2,1,0:T(8,128)}) async-done(((f32[1,2048,256]{2,1,0:T(8,128)}, f32[1,2048,256]{2,1,0:T(8,128)}, f32[1,2048,256]{2,1,0:T(8,128)}), (f32[1,2048,256]{2,1,0:T(8,128)}, f32[1,2048,256]{2,1,0:T(8,128)}, f32[1,2048,256]{2,1,0:T(8,128)})) %all-reduce.32.cloned.1.call-update) | async-done | bytes 6291472 | tf_op jit(solution)/shard_map/psum | solution.py:403
  2155.7 41.5 %reduce-scatter.41.cloned.1.call-done = bf16[512,512]{1,0:T(8,128)(2,1)} async-done(((bf16[2048,512]{1,0:T(8,128)(2,1)}), bf16[512,512]{1,0:T(8,128)(2,1)}) %reduce-scatter.41.cloned.1.call-update) | async-done | bytes 524304 | tf_op jit(solution)/shard_map/reduce_scatter | solution.py:377
  2197.2 45.5 %reduce-scatter.39.cloned.1.call-done = bf16[512,512]{1,0:T(8,128)(2,1)} async-done(((bf16[2048,512]{1,0:T(8,128)(2,1)}), bf16[512,512]{1,0:T(8,128)(2,1)}) %reduce-scatter.39.cloned.1.call-update) | async-done | bytes 524304 | tf_op jit(solution)/shard_map/reduce_scatter | solution.py:377
  2242.7 46.2 %reduce-scatter.37.cloned.1.call-done = bf16[512,512]{1,0:T(8,128)(2,1)} async-done(((bf16[2048,512]{1,0:T(8,128)(2,1)}), bf16[512,512]{1,0:T(8,128)(2,1)}) %reduce-scatter.37.cloned.1.call-update) | async-done | bytes 524304 | tf_op jit(solution)/shard_map/reduce_scatter | solution.py:377
  2292.1 53.0 %reduce-scatter.29.cloned.1.call-done = bf16[32,4,2048]{2,0,1:T(8,128)(2,1)} async-done(((bf16[256,4,2048]{2,0,1:T(8,128)(2,1)}), bf16[32,4,2048]{2,0,1:T(8,128)(2,1)}) %reduce-scatter.29.cloned.1.call-update) | async-done | bytes 524304 | tf_op jit(solution)/shard_map/reduce_scatter | solution.py:353
  2350.0 39.2 %all-reduce.27 = (f32[1,2048]{1,0:T(1,128)S(1)}, f32[1,2048]{1,0:T(1,128)S(1)}, f32[1,2048]{1,0:T(1,128)S(1)}, f32[1,4,256]{2,1,0:T(4,128)S(1)}, f32[1,4,256]{2,...) all-reduce(f32[1,2048]{1,0:T(1,128)S(1)} %bitcast.907, ...), channel_id=1, replica_groups=mesh['seq'=4,'heads'=8] {'seq','heads'}, use_global_device_ids=true, to_apply=%region_70.72 | all-reduce | flops 9984 | bytes 79872 | tf_op jit(solution)/shard_map/psum | solution.py:403
  (1057 shorter events, 886.3 us)
Async XLA Ops:
  7.2 54.9 %all-gather.49.cloned.1.call-start = ((), (), s32[]{:S(2)}) async-start(), calls=%async_computation.18 | async-start | bytes 4718592 | tf_op jit(solution)/shard_map/all_gather | solution.py:167
  22.6 68.9 %all-gather.63.cloned.1.call-start = ((), (), s32[]{:S(2)}) async-start(), calls=%async_computation.43 | async-start | bytes 1310720 | tf_op jit(solution)/shard_map/all_gather | solution.py:154
  25.5 112.1 %all-gather.61.cloned.1.call-start = ((), (), s32[]{:S(2)}) async-start(), calls=%async_computation.42 | async-start | bytes 2621440 | tf_op jit(solution)/shard_map/all_gather | solution.py:153
  26.8 177.0 %all-gather.65.cloned.1.call-start = ((), (), s32[]{:S(2)}) async-start(), calls=%async_computation.44 | async-start | bytes 2621440 | tf_op jit(solution)/shard_map/all_gather | solution.py:19
  142.9 6.7 collective-permute-start
  159.5 90.2 %all-gather.67.cloned.1.call-start = ((), (), s32[]{:S(2)}) async-start(), calls=%async_computation.45 | async-start | bytes 2621440 | tf_op jit(solution)/shard_map/all_gather | solution.py:152
  160.9 135.4 %all-gather.69.cloned.1.call-start = ((), (), s32[]{:S(2)}) async-start(), calls=%async_computation.46 | async-start | bytes 2621440 | tf_op jit(solution)/shard_map/all_gather | solution.py:156
  163.6 191.4 %reduce-scatter.19.cloned.1.call-start = ((), (), s32[]{:S(2)}) async-start(), calls=%async_computation.19 | async-start | bytes 4718592 | tf_op jit(solution)/shard_map/reduce_scatter | solution.py:208
  303.1 93.0 %all-gather.51.cloned.1.call-start = ((), (), s32[]{:S(2)}) async-start(), calls=%async_computation.20 | async-start | bytes 4718592 | tf_op jit(solution)/shard_map/all_gather | solution.py:167
  358.8 66.8 %all-gather.73.cloned.1.call-start = ((), (), s32[]{:S(2)}) async-start(), calls=%async_computation.48 | async-start | bytes 1310720 | tf_op jit(solution)/shard_map/all_gather | solution.py:154
  359.7 111.2 %all-gather.71.cloned.1.call-start = ((), (), s32[]{:S(2)}) async-start(), calls=%async_computation.47 | async-start | bytes 2621440 | tf_op jit(solution)/shard_map/all_gather | solution.py:153
  360.3 177.6 %all-gather.75.cloned.1.call-start = ((), (), s32[]{:S(2)}) async-start(), calls=%async_computation.49 | async-start | bytes 2621440 | tf_op jit(solution)/shard_map/all_gather | solution.py:19
  476.9 6.7 collective-permute-start.1
  493.7 90.5 %all-gather.77.cloned.1.call-start = ((), (), s32[]{:S(2)}) async-start(), calls=%async_computation.50 | async-start | bytes 2621440 | tf_op jit(solution)/shard_map/all_gather | solution.py:152
  494.2 136.2 %all-gather.79.cloned.1.call-start = ((), (), s32[]{:S(2)}) async-start(), calls=%async_computation.51 | async-start | bytes 2621440 | tf_op jit(solution)/shard_map/all_gather | solution.py:156
  495.0 194.2 %reduce-scatter.21.cloned.1.call-start = ((), (), s32[]{:S(2)}) async-start(), calls=%async_computation.21 | async-start | bytes 4718592 | tf_op jit(solution)/shard_map/reduce_scatter | solution.py:208
  637.2 93.1 %all-gather.53.cloned.1.call-start = ((), (), s32[]{:S(2)}) async-start(), calls=%async_computation.22 | async-start | bytes 4718592 | tf_op jit(solution)/shard_map/all_gather | solution.py:167
  693.0 66.0 %all-gather.83.cloned.1.call-start = ((), (), s32[]{:S(2)}) async-start(), calls=%async_computation.53 | async-start | bytes 1310720 | tf_op jit(solution)/shard_map/all_gather | solution.py:154
  694.0 110.3 %all-gather.81.cloned.1.call-start = ((), (), s32[]{:S(2)}) async-start(), calls=%async_computation.52 | async-start | bytes 2621440 | tf_op jit(solution)/shard_map/all_gather | solution.py:153
  694.6 180.6 %all-gather.85.cloned.1.call-start = ((), (), s32[]{:S(2)}) async-start(), calls=%async_computation.54 | async-start | bytes 2621440 | tf_op jit(solution)/shard_map/all_gather | solution.py:19
  830.7 90.6 %all-gather.87.cloned.1.call-start = ((), (), s32[]{:S(2)}) async-start(), calls=%async_computation.55 | async-start | bytes 2621440 | tf_op jit(solution)/shard_map/all_gather | solution.py:152
  831.5 135.9 %all-gather.89.cloned.1.call-start = ((), (), s32[]{:S(2)}) async-start(), calls=%async_computation.56 | async-start | bytes 2621440 | tf_op jit(solution)/shard_map/all_gather | solution.py:156
  832.1 175.0 %all-gather.55.cloned.1.call-start = ((), (), s32[]{:S(2)}) async-start(), calls=%async_computation.24 | async-start | bytes 4718592 | tf_op jit(solution)/shard_map/all_gather | solution.py:251
  834.3 250.3 %all-gather.91.cloned.1.call-start = ((), (), s32[]{:S(2)}) async-start(), calls=%async_computation.57 | async-start | bytes 2621440 | tf_op jit(solution)/shard_map/all_gather | solution.py:40
  1039.1 193.4 %reduce-scatter.25.cloned.1.call-start = ((), (), s32[]{:S(2)}) async-start(), calls=%async_computation.25 | async-start | bytes 4718592 | tf_op jit(solution)/shard_map/reduce_scatter | solution.py:353
  1154.4 8.5 collective-permute-start.3
  1181.5 93.3 %all-gather.57.cloned.1.call-start = ((), (), s32[]{:S(2)}) async-start(), calls=%async_computation.26 | async-start | bytes 4718592 | tf_op jit(solution)/shard_map/all_gather | solution.py:251
  1237.6 113.2 %all-gather.93.cloned.1.call-start = ((), (), s32[]{:S(2)}) async-start(), calls=%async_computation.58 | async-start | bytes 2621440 | tf_op jit(solution)/shard_map/all_gather | solution.py:40
  1305.3 181.2 %reduce-scatter.27.cloned.1.call-start = ((), (), s32[]{:S(2)}) async-start(), calls=%async_computation.27 | async-start | bytes 4718592 | tf_op jit(solution)/shard_map/reduce_scatter | solution.py:353
  1409.7 7.5 collective-permute-start.4
  1435.6 105.4 %reduce-scatter.23.cloned.1.call-start = ((), (), s32[]{:S(2)}) async-start(), calls=%async_computation.23 | async-start | bytes 4718592 | tf_op jit(solution)/shard_map/reduce_scatter | solution.py:208
  1443.2 138.9 %all-gather.59.cloned.1.call-start = ((), (), s32[]{:S(2)}) async-start(), calls=%async_computation.28 | async-start | bytes 4718592 | tf_op jit(solution)/shard_map/all_gather | solution.py:251
  1544.9 112.9 %all-gather.95.cloned.1.call-start = ((), (), s32[]{:S(2)}) async-start(), calls=%async_computation.59 | async-start | bytes 2621440 | tf_op jit(solution)/shard_map/all_gather | solution.py:40
  1612.2 250.8 %reduce-scatter.47.cloned.1.call-start = ((), (), s32[]{:S(2)}) async-start(), calls=%async_computation.38 | async-start | bytes 40960 | tf_op jit(solution)/shard_map/reduce_scatter | solution.py:380
  1615.8 247.3 %reduce-scatter.45.cloned.1.call-start = ((), (), s32[]{:S(2)}) async-start(), calls=%async_computation.37 | async-start | bytes 40960 | tf_op jit(solution)/shard_map/reduce_scatter | solution.py:380
  1619.3 243.8 %reduce-scatter.43.cloned.1.call-start = ((), (), s32[]{:S(2)}) async-start(), calls=%async_computation.36 | async-start | bytes 40960 | tf_op jit(solution)/shard_map/reduce_scatter | solution.py:380
  1695.5 168.9 %reduce-scatter.53.cloned.1.call-start = ((), (), s32[]{:S(2)}) async-start(), calls=%async_computation.41 | async-start | bytes 2621440 | tf_op jit(solution)/shard_map/reduce_scatter | solution.py:383
  1702.3 162.2 %reduce-scatter.51.cloned.1.call-start = ((), (), s32[]{:S(2)}) async-start(), calls=%async_computation.40 | async-start | bytes 2621440 | tf_op jit(solution)/shard_map/reduce_scatter | solution.py:383
  1709.0 155.4 %reduce-scatter.49.cloned.1.call-start = ((), (), s32[]{:S(2)}) async-start(), calls=%async_computation.39 | async-start | bytes 2621440 | tf_op jit(solution)/shard_map/reduce_scatter | solution.py:383
  1716.0 181.9 %reduce-scatter.35.cloned.1.call-start = ((), (), s32[]{:S(2)}) async-start(), calls=%async_computation.32 | async-start | bytes 2621440 | tf_op jit(solution)/shard_map/reduce_scatter | solution.py:374
  1722.1 221.4 %reduce-scatter.33.cloned.1.call-start = ((), (), s32[]{:S(2)}) async-start(), calls=%async_computation.31 | async-start | bytes 2621440 | tf_op jit(solution)/shard_map/reduce_scatter | solution.py:374
  1728.4 260.7 %reduce-scatter.31.cloned.1.call-start = ((), (), s32[]{:S(2)}) async-start(), calls=%async_computation.30 | async-start | bytes 2621440 | tf_op jit(solution)/shard_map/reduce_scatter | solution.py:374
  1751.4 401.6 %all-reduce.32.cloned.1.call-start = ((), (), s32[]{:S(2)}) async-start(), calls=%async_computation.60 | async-start | bytes 12582912 | tf_op jit(solution)/shard_map/psum | solution.py:403
  1776.9 8.3 collective-permute-start.5
  1794.6 402.6 %reduce-scatter.41.cloned.1.call-start = ((), (), s32[]{:S(2)}) async-start(), calls=%async_computation.35 | async-start | bytes 2621440 | tf_op jit(solution)/shard_map/reduce_scatter | solution.py:377
  1802.4 440.3 %reduce-scatter.39.cloned.1.call-start = ((), (), s32[]{:S(2)}) async-start(), calls=%async_computation.34 | async-start | bytes 2621440 | tf_op jit(solution)/shard_map/reduce_scatter | solution.py:377
  1809.3 479.6 %reduce-scatter.37.cloned.1.call-start = ((), (), s32[]{:S(2)}) async-start(), calls=%async_computation.33 | async-start | bytes 2621440 | tf_op jit(solution)/shard_map/reduce_scatter | solution.py:377
  1815.5 529.7 %reduce-scatter.29.cloned.1.call-start = ((), (), s32[]{:S(2)}) async-start(), calls=%async_computation.29 | async-start | bytes 4718592 | tf_op jit(solution)/shard_map/reduce_scatter | solution.py:353
  (280 other events, 7203.1 us)
Sparse Core Ops, SparseCore 0:
  22.6 39.4 all-gather.48
  64.2 27.2 all-gather.62
  93.7 43.8 all-gather.60
  159.6 44.0 all-gather.64
  205.1 44.5 all-gather.66
  251.7 44.5 all-gather.68
  303.1 51.8 reduce-scatter.18
  358.9 37.1 all-gather.50
  398.3 27.2 all-gather.72
  427.1 43.8 all-gather.70
  493.8 44.1 all-gather.74
  539.5 44.6 all-gather.76
  585.8 44.6 all-gather.78
  637.3 51.8 reduce-scatter.20
  693.2 37.1 all-gather.52
  731.8 27.2 all-gather.82
  760.5 43.8 all-gather.80
  830.9 44.2 all-gather.84
  876.7 44.5 all-gather.86
  922.7 44.6 all-gather.88
  969.3 37.7 all-gather.54
  1039.2 45.3 all-gather.90
  1181.7 50.8 reduce-scatter.24
  1237.7 37.1 all-gather.56
  1305.4 45.3 all-gather.92
  1435.7 50.6 reduce-scatter.26
  1489.7 51.2 reduce-scatter.22
  1545.0 37.1 all-gather.58
  1612.3 45.3 all-gather.94
  1659.9 15.0 reduce-scatter.46
  1677.3 17.0 reduce-scatter.44
  1696.7 17.0 reduce-scatter.42
  1715.9 44.0 reduce-scatter.52
  1762.4 44.2 reduce-scatter.50
  1809.0 43.3 reduce-scatter.48
  1854.7 43.2 reduce-scatter.34
  1900.1 43.3 reduce-scatter.32
  1945.8 43.1 reduce-scatter.30
  1994.9 158.1 all-reduce.31
  2155.5 41.6 reduce-scatter.40
  2199.5 43.1 reduce-scatter.38
  2245.7 43.1 reduce-scatter.36
  2292.1 53.0 reduce-scatter.28
where the time goes:
time: 2410 us; the launch traced here: 2400 us
  waiting for transfers between devices  1380 us (57%)
  matrix products  416 us (17%)
  other arithmetic  231 us (10%)
  blocking collectives  205 us (9%)
  local copies, waits for them, and re-layouts  117 us (5%)
  starting transfers between devices  33.2 us (1%)
    psum x1, waiting for transfers between devices, shards(): lax.psum(shared_sets[layer_index], ('seq', 'heads'))  161 us
    reduce_scatter x3, waiting for transfers between devices, shards(): lax.psum_scatter(spread(jnp.int32(0), lax.axis_size('heads') * own_rows)....  147 us
    reduce_scatter x3, waiting for transfers between devices, shards(): lax.psum_scatter(project(jnp.int32(0), lax.axis_size('heads') * own_rows)...  137 us
    reduce_scatter x3, waiting for transfers between devices, shards(): lax.psum_scatter(d_mixed_w.astype(jnp.bfloat16), 'seq', scatter_dimension...  133 us
    all_gather x3, waiting for transfers between devices, gather_weights(): lax.all_gather(w_x[layer_index], 'seq', axis=0, tiled=True)  123 us
    reduce_scatter x3, waiting for transfers between devices, shards(): lax.psum_scatter(d_gate_w.astype(jnp.bfloat16), 'seq', scatter_dimension=...  121 us
    all_gather x3, waiting for transfers between devices, shards(): grad_block = lax.all_gather(grad_low, 'heads', axis=0, tiled=True)  114 us
    all_gather x3, waiting for transfers between devices, gather_weights(): lax.all_gather(w_z[layer_index], 'seq', axis=0, tiled=True)  91.2 us
  transfers between devices with their start and end apart: 49, of which 38 were waited for; matrix products, arithmetic and copies ran while one was open for 18% of the time, Pallas kernels for 0%

commit v1 on v0

v1 whole, which is shorter than its diff:
```python
import functools

import jax
import jax.numpy as jnp
from jax import lax
from jax.experimental import pallas as pl
from jax.experimental.pallas import tpu as pltpu
from jax.sharding import PartitionSpec as P

F32 = jnp.float32
BF = jnp.bfloat16
EPSILON = 1e-05
LANES = 128
HALO = 16
NN = ((1,), (0,))
NT = ((1,), (1,))
TN = ((0,), (0,))
GROUPS = 2
VMEM_BYTES = 56 * 1024 * 1024


def mm(a, b, dims=NN):
    return lax.dot_general(a, b, (dims, ((), ())), preferred_element_type=F32)


def smem():
    return pl.BlockSpec(memory_space=pltpu.SMEM)


def anywhere():
    return pl.BlockSpec(memory_space=pl.ANY)


def whole(a):
    rank = len(a.shape)
    return pl.BlockSpec(tuple(a.shape), lambda i: (0,) * rank)


def per_seq(a):
    rank = len(a.shape)
    return pl.BlockSpec((1,) + tuple(a.shape[1:]), lambda i: (i,) + (0,) * (rank - 1))


def sds(shape, dtype):
    return jax.ShapeDtypeStruct(shape, dtype)


class Line:
    def __init__(self):
        self.last = ()

    def call(self, body, grid, ins, in_specs, outs, out_specs, scratch=(), name=None, after=()):
        waits = tuple(self.last) + tuple(after)
        count, extra = len(ins), len(waits)
        made = len(outs)

        def kernel(*refs):
            body(*refs[:count], *refs[count + extra : count + extra + made], *refs[count + extra + made + 1 :])
            refs[count + extra + made][...] = jnp.zeros((8, LANES), F32)

        mark = sds((8, LANES), F32)
        *results, token = pl.pallas_call(
            kernel,
            grid=(grid,),
            in_specs=list(in_specs) + [anywhere()] * extra,
            out_specs=list(out_specs) + [whole(mark)],
            out_shape=list(outs) + [mark],
            scratch_shapes=list(scratch),
            compiler_params=pltpu.CompilerParams(vmem_limit_bytes=VMEM_BYTES),
            cost_estimate=pl.CostEstimate(flops=1, bytes_accessed=1, transcendentals=0),
            name=name,
        )(*ins, *waits)
        self.last = (token,)
        return results


def head_lanes(heads, width, parts):
    shape = (LANES, width)
    lane = lax.broadcasted_iota(jnp.int32, shape, 0)
    head = lax.broadcasted_iota(jnp.int32, shape, 1) // (width // heads)
    hit = lane == head
    for part in range(1, parts):
        hit = hit | (lane == head + part * heads)
    return hit.astype(F32).astype(BF)


def three_parts(per_head, heads):
    lane = lax.broadcasted_iota(jnp.int32, per_head.shape, 1)
    x = jnp.where(lane < heads, per_head, 0.0)
    high = x.astype(BF).astype(F32)
    rest = x - high
    middle = rest.astype(BF).astype(F32)
    packed = high + pltpu.roll(middle, heads, 1) + pltpu.roll(rest - middle, 2 * heads, 1)
    return packed.astype(BF)


def expand(per_head, width, size):
    heads = width // size
    return mm(three_parts(per_head, heads), head_lanes(heads, width, 3))


def collapse(wide, size):
    width = wide.shape[1]
    heads = width // size
    high = wide.astype(BF)
    low = (wide - high.astype(F32)).astype(BF)
    shape = (width, LANES)
    table = lax.broadcasted_iota(jnp.int32, shape, 0) // size == lax.broadcasted_iota(jnp.int32, shape, 1)
    table = table.astype(F32).astype(BF)
    return mm(high, table) + mm(low, table)


def running_sum(per_head, heads, back=False):
    made = mm(triangle(per_head.shape[0], back).astype(BF), three_parts(per_head, heads))
    made = made + pltpu.roll(made, LANES - heads, 1) + pltpu.roll(made, LANES - 2 * heads, 1)
    lane = lax.broadcasted_iota(jnp.int32, made.shape, 1)
    return jnp.where(lane < heads, made, 0.0)


def sigmoid(x):
    return 0.5 * jnp.tanh(0.5 * x) + 0.5


def softplus(x):
    return jnp.maximum(x, 0.0) + jnp.log1p(jnp.exp(-jnp.abs(x)))


def valid_column(info, lengths, seq, length):
    rows = lax.broadcasted_iota(jnp.int32, (length, 1), 0) + info[2]
    return (rows < lengths[seq]).astype(F32)


def triangle(length, flipped=False):
    a = lax.broadcasted_iota(jnp.int32, (length, length), 0)
    b = lax.broadcasted_iota(jnp.int32, (length, length), 1)
    return ((a <= b) if flipped else (a >= b)).astype(F32)


def split_two(x):
    high = x.astype(BF)
    return high, (x - high.astype(F32)).astype(BF)


def lane_pack(columns, rows):
    lane = lax.broadcasted_iota(jnp.int32, (rows, LANES), 1)
    out = jnp.zeros((rows, LANES), F32)
    for place, column in enumerate(columns):
        out = jnp.where(lane == place, column.astype(F32), out)
    return out.astype(BF)


def decay_blocks(rise, rise_rows, head, length):
    half = length // 2
    column = rise[:, head : head + 1]
    row = rise_rows[head : head + 1, :]
    low = lax.broadcasted_iota(jnp.int32, (half, half), 0) >= lax.broadcasted_iota(
        jnp.int32, (half, half), 1
    )
    top = jnp.where(low, jnp.exp(row[:, :half] - column[:half]), 0.0)
    left = jnp.exp(row[:, :half] - column[half:])
    right = jnp.where(low, jnp.exp(row[:, half:] - column[half:]), 0.0)
    return top, left, right


def norm_body(last, width, total, info, x, gain, *refs):
    pieces, (x_out, branch_out, normed_out, payload_out) = refs[:-4], refs[-4:]
    summed = pieces[0][0].astype(F32)
    for piece in pieces[1:]:
        summed = summed + piece[0].astype(F32)
    squares = summed[:, width : width + 1] + summed[:, width + 1 : width + 2]
    factor = lax.rsqrt(squares / total + EPSILON)
    branch = summed[:, :width] * factor
    x_new = x[0] + branch
    x_out[0] = x_new
    branch_out[0] = branch.astype(BF)
    q = lax.rsqrt(jnp.mean(x_new * x_new, axis=-1, keepdims=True) + EPSILON)
    normed_out[0] = (x_new * q * gain[...]).astype(BF)
    high, low = split_two(factor)
    payload_out[0] = lane_pack((high, low), summed.shape[0])


def first_norm_body(x, gain, normed_out):
    x_new = x[0]
    q = lax.rsqrt(jnp.mean(x_new * x_new, axis=-1, keepdims=True) + EPSILON)
    normed_out[0] = (x_new * q * gain[...]).astype(BF)


def back_payload(grad_low, branch, factor_lanes, out):
    width = grad_low.shape[1]
    dotted = jnp.sum(grad_low.astype(F32) * branch.astype(F32), axis=-1, keepdims=True)
    high, low = split_two(dotted)
    lane = lax.broadcasted_iota(jnp.int32, (grad_low.shape[0], LANES), 1)
    lanes = factor_lanes.astype(F32)
    lanes = jnp.where(lane == 2, high.astype(F32), lanes)
    lanes = jnp.where(lane == 3, low.astype(F32), lanes)
    out[0, :, :width] = grad_low
    out[0, :, width:] = lanes.astype(BF)


def first_back_body(grad, branch, factor_lanes, out):
    back_payload(grad[0], branch[0], factor_lanes[0], out)


def back_norm_body(width, x, gain, grad, branch, factor_lanes, *refs):
    pieces, (grad_out, payload_out, gain_out) = refs[:-3], refs[-3:]
    d_normed = pieces[0][0].astype(F32)
    for piece in pieces[1:]:
        d_normed = d_normed + piece[0].astype(F32)
    rows = x[0]
    q = lax.rsqrt(jnp.mean(rows * rows, axis=-1, keepdims=True) + EPSILON)
    scaled = d_normed * gain[...]
    cross = jnp.sum(scaled * rows, axis=-1, keepdims=True)
    grad_new = grad[0] + q * scaled - rows * (q * q * q * cross / width)
    grad_out[0] = grad_new
    gain_out[0] = jnp.broadcast_to(
        jnp.sum(d_normed * rows * q, axis=0, keepdims=True), gain_out.shape[1:]
    )
    back_payload(grad_new.astype(BF), branch[0], factor_lanes[0], payload_out)


def collect_body(n, nh, info, *refs):
    pieces, steps = refs[:nh], refs[nh : nh + n]
    shared_out, step_out = refs[nh + n :]
    here, place = info[0], info[1]
    for k in range(nh):
        owner = here ^ k
        for s in range(n):
            source = lax.rem(place - s + n, n)
            for layer in range(shared_out.shape[0]):
                shared_out[layer, source, owner] = pieces[k][s, layer]
    step_out[...] = jnp.zeros_like(step_out)
    rows = steps[0].shape[1]
    for s in range(n):
        source = lax.rem(place - s + n, n)
        wide = steps[s].shape[2]
        for layer in range(step_out.shape[0]):
            step_out[layer, 0:rows, pl.ds(pl.multiple_of(source * wide, wide), wide)] = steps[s][layer]


def project_body(nh, channels, info, *refs):
    pieces = refs[:nh]
    w_x, w_bc, w_dt = refs[nh : nh + 3]
    x_out, feed_out, raw_out = refs[nh + 3 :]
    own = pieces[0].shape[1]
    for k in range(nh):
        start = pl.multiple_of((info[0] ^ k) * own, own)
        x_out[0, pl.ds(start, own), :] = pieces[k][0]
    rows = x_out[0]
    feed_out[0, :, :channels] = mm(rows, flat_rows(w_x))
    feed_out[0, :, channels:] = mm(rows, w_bc[...])
    raw_out[0] = mm(rows, w_dt[...], NT)


def flat_rows(w):
    table = w[...]
    return table.reshape(table.shape[0] * table.shape[2], table.shape[3])


def gate_body(x, w_z, gate_out):
    gate_out[0] = mm(x[0], flat_rows(w_z)).astype(BF)


def rates_of(raw, head_params):
    lanes = head_params[2:3]
    return softplus(raw + head_params[0:1]) * lanes


def local_body(
    channels, size, taps, info, lengths, feed, raw, x_halo, w_x, w_bc, conv_w, head_params,
    chan, values_out, shared_out, rise_out, step_out, local_out, state_out, fade_out, halo_out,
    ext, halo_all,
):
    seq = pl.program_id(0)
    length = feed.shape[1]
    state = (feed.shape[2] - channels) // 2

    @pl.when(seq == 0)
    def _():
        halo_all[:, :channels] = mm(x_halo[...], flat_rows(w_x))
        halo_all[:, channels:] = mm(x_halo[...], w_bc[...])

    rim = halo_all[pl.ds(pl.multiple_of(seq * HALO, HALO), HALO), :]
    halo_out[0] = rim
    ext[:HALO] = rim
    ext[HALO:] = feed[0]
    valid = valid_column(info, lengths, seq, length)
    pre = conv_w[taps : taps + 1]
    for k in range(taps):
        pre = pre + conv_w[k : k + 1] * ext[HALO - taps + 1 + k : HALO - taps + 1 + k + length]
    act = pre * sigmoid(pre) * valid
    low = act.astype(BF)
    values_out[0] = low[:, :channels]
    shared_out[0] = low[:, channels:]
    values = low[:, :channels].astype(F32)
    keys = low[:, channels : channels + state]
    queries = low[:, channels + state :]
    params = head_params[...]
    step = rates_of(raw[0], params) * valid
    rise = running_sum(jnp.exp(params[1:2]) * step, channels // size)
    rise_out[0] = rise
    step_out[0] = step
    closing = rise[length - 1 :, :]
    weight = jnp.exp(rise - closing) * step
    weighted = (expand(weight, channels, size) * values).astype(BF)
    state_out[0] = mm(keys, weighted, TN).astype(BF)
    fade_out[0] = expand(jnp.broadcast_to(jnp.exp(-closing), (8, LANES)), channels, size)
    scores = mm(queries, keys, NT)
    stepped = (values * expand(step, channels, size)).astype(BF)
    rise_rows = jnp.transpose(rise)
    half = length // 2
    group = LANES // size
    lane = lax.broadcasted_iota(jnp.int32, (length, LANES), 1) // size
    for pair in range(channels // LANES):
        block = stepped[:, pair * LANES : (pair + 1) * LANES]
        upper = jnp.zeros((half, LANES), F32)
        lower = jnp.zeros((half, LANES), F32)
        for inner in range(group):
            top, left, right = decay_blocks(rise, rise_rows, pair * group + inner, length)
            part = jnp.where(lane == inner, block, jnp.zeros_like(block))
            upper = upper + mm((scores[:half, :half] * top).astype(BF), part[:half])
            lower = lower + mm((scores[half:, :half] * left).astype(BF), part[:half])
            lower = lower + mm((scores[half:, half:] * right).astype(BF), part[half:])
        at = slice(pair * LANES, (pair + 1) * LANES)
        skipped = chan[1:2, at] * values[:, at]
        local_out[0, :half, at] = upper + skipped[:half]
        local_out[0, half:, at] = lower + skipped[half:]


def hop_body(arrived, own, fade, out):
    out[0] = (fade[0, 0:1] * arrived[0].astype(F32) + own[0].astype(F32)).astype(BF)


def received(parts):
    summed = parts[0][0]
    for part in parts[1:]:
        summed = summed + part[0]
    return summed


def scatter_rows(info, outs, table, own):
    for k, out in enumerate(outs):
        start = pl.multiple_of((info[0] ^ k) * own, own)
        out[0] = table[pl.ds(start, own), :].astype(BF)


def output_body(
    n, nh, size, info, local, gate, shared, rise, w_out, chan, *refs
):
    parts, rest = refs[: n - 1], refs[n - 1 :]
    full_out, carried_out = rest[:2]
    outs, table = rest[2 : 2 + nh], rest[2 + nh]
    carried = received(parts)
    carried_out[0] = carried
    length, channels = local.shape[1:]
    state = shared.shape[2] // 2
    queries = shared[0, :, state:]
    far = mm(queries, carried) * expand(jnp.exp(-rise[0]), channels, size)
    full = local[0] + far
    full_out[0] = full
    wide = gate[0].astype(F32)
    gated = full * wide * sigmoid(wide)
    squares = jnp.sum(gated * gated, axis=-1, keepdims=True)
    low = (gated * chan[0:1]).astype(BF)
    cols = w_out.shape[3]
    for s in range(n):
        table[:, s * cols : (s + 1) * cols] = mm(low, w_out[s, 0])
    high, rest_part = split_two(squares)
    table[:, n * cols :] = lane_pack((high, rest_part), length).astype(F32)
    scatter_rows(info, outs, table, length // nh)


def gate_back_body(
    n, nh, size, total, info, gate, full, values, shared, rise, w_out, chan, *refs
):
    pieces = refs[:nh]
    grad_out, d_gate_out, normal_out, d_full_out, state_out, sums_out, table = refs[nh:]
    seq = pl.program_id(0)
    own = pieces[0].shape[1]
    width = grad_out.shape[2]
    length, channels = gate.shape[1:]
    for k in range(nh):
        start = pl.multiple_of((info[0] ^ k) * own, own)
        grad_out[0, pl.ds(start, own), :] = pieces[k][0, :, :width]
        table[pl.ds(start, own), :] = pieces[k][0, :, width:].astype(F32)
    factor = table[:, 0:1] + table[:, 1:2]
    dotted = table[:, 2:3] + table[:, 3:4]
    cols = w_out.shape[3]
    d_normal = mm(grad_out[0, :, :cols], w_out[0, 0], NT)
    for s in range(1, n):
        d_normal = d_normal + mm(grad_out[0, :, s * cols : (s + 1) * cols], w_out[s, 0], NT)
    wide = gate[0].astype(F32)
    sig = sigmoid(wide)
    silu = wide * sig
    full_wide = full[0]
    gated = full_wide * silu
    gain = chan[0:1]
    normal = gated * factor
    normal_out[0] = (normal * gain).astype(BF)
    d_gated = factor * (d_normal * gain) - gated * (factor * factor * dotted / total)
    d_full = d_gated * silu
    d_gate_out[0] = (d_gated * full_wide * (sig * (1.0 + wide * (1.0 - sig)))).astype(BF)
    d_full_out[0] = d_full.astype(BF)
    state = shared.shape[2] // 2
    queries = shared[0, :, state:]
    spread = (d_full * expand(jnp.exp(-rise[0]), channels, size)).astype(BF)
    state_out[0] = mm(queries, spread, TN).astype(BF)

    @pl.when(seq == 0)
    def _():
        sums_out[...] = jnp.zeros_like(sums_out)

    sums_out[0:1] += jnp.sum(d_normal * normal, axis=0, keepdims=True)
    sums_out[1:2] += jnp.sum(d_full * values[0].astype(F32), axis=0, keepdims=True)


def mix_back_body(
    size, d_full, full, values, shared, rise, step, carried, chan, d_values_out, d_shared_out, rates_out
):
    length, channels = d_full.shape[1:]
    state = shared.shape[2] // 2
    keys, queries = shared[0, :, :state], shared[0, :, state:]
    d_low = d_full[0]
    d_wide = d_low.astype(F32)
    wide = values[0].astype(F32)
    rise_all, step_all = rise[0], step[0]
    spread = (d_wide * expand(jnp.exp(-rise_all), channels, size)).astype(BF)
    d_queries = mm(spread, carried[0], NT)
    step_wide = expand(step_all, channels, size)
    stepped = (wide * step_wide).astype(BF)
    scores = mm(queries, keys, NT)
    rise_rows = jnp.transpose(rise_all)
    half = length // 2
    group = LANES // size
    lane = lax.broadcasted_iota(jnp.int32, (length, LANES), 1) // size
    d_top = jnp.zeros((half, half), F32)
    d_left = jnp.zeros((half, half), F32)
    d_right = jnp.zeros((half, half), F32)
    blocks = []
    for pair in range(channels // LANES):
        at = slice(pair * LANES, (pair + 1) * LANES)
        block, d_block = stepped[:, at], d_low[:, at]
        first = jnp.zeros((half, LANES), F32)
        second = jnp.zeros((half, LANES), F32)
        for inner in range(group):
            top, left, right = decay_blocks(rise_all, rise_rows, pair * group + inner, length)
            part = jnp.where(lane == inner, d_block, jnp.zeros_like(d_block))
            d_top = d_top + mm(part[:half], block[:half], NT) * top
            d_left = d_left + mm(part[half:], block[:half], NT) * left
            d_right = d_right + mm(part[half:], block[half:], NT) * right
            first = first + mm((scores[:half, :half] * top).astype(BF), part[:half], TN)
            first = first + mm((scores[half:, :half] * left).astype(BF), part[half:], TN)
            second = second + mm((scores[half:, half:] * right).astype(BF), part[half:], TN)
        blocks.append(jnp.concatenate([first, second], axis=0))
    d_stepped = jnp.concatenate(blocks, axis=1)
    d_top, d_left, d_right = d_top.astype(BF), d_left.astype(BF), d_right.astype(BF)
    d_shared_out[0, :half, :state] = mm(d_top, queries[:half], TN) + mm(d_left, queries[half:], TN)
    d_shared_out[0, half:, :state] = mm(d_right, queries[half:], TN)
    d_shared_out[0, :half, state:] = d_queries[:half] + mm(d_top, keys[:half])
    d_shared_out[0, half:, state:] = d_queries[half:] + mm(d_left, keys[:half]) + mm(d_right, keys[half:])
    skip = chan[1:2]
    d_values_out[0] = (skip * d_wide + step_wide * d_stepped).astype(BF)
    d_step = collapse(wide * d_stepped, size)
    d_rise = collapse(stepped.astype(F32) * d_stepped - d_wide * (full[0] - skip * wide), size)
    rates_out[0, :, :LANES] = d_rise
    rates_out[0, :, LANES:] = d_step


def state_back_body(
    n, channels, size, taps, info, lengths, feed, raw, rim, values, shared, rise, step, carried,
    d_values_in, d_shared_in, rates, conv_w, head_params, *refs
):
    parts, rest = refs[: n - 1], refs[n - 1 :]
    d_pre_out, first_out, d_raw_out, conv_out, head_out, ext = rest
    seq = pl.program_id(0)
    after = received(parts)
    length = feed.shape[1]
    state = shared.shape[2] // 2
    keys = shared[0, :, :state]
    wide = values[0].astype(F32)
    rise_all, step_all = rise[0], step[0]
    closing = rise_all[length - 1 :, :]
    ratio = jnp.exp(rise_all - closing)
    weight_wide = expand(ratio * step_all, channels, size)
    reached = mm(keys, after)
    d_values = d_values_in[0].astype(F32) + weight_wide * reached
    d_keys = d_shared_in[0, :, :state] + mm((weight_wide * wide).astype(BF), after, NT)
    d_queries = d_shared_in[0, :, state:]
    d_ratio = collapse(wide * reached, size) * ratio
    d_step = rates[0, :, LANES:] + d_ratio
    moved = d_ratio * step_all
    fade_terms = jnp.sum(after.astype(F32) * carried[0].astype(F32), axis=0, keepdims=True)
    d_fade = collapse(jnp.broadcast_to(fade_terms, (8, channels)), size)[0:1]
    d_close = jnp.sum(moved, axis=0, keepdims=True) + d_fade * jnp.exp(-closing)
    last = lax.broadcasted_iota(jnp.int32, (length, LANES), 0) == length - 1
    d_rise = rates[0, :, :LANES] + moved - jnp.where(last, d_close, 0.0)
    gathered = running_sum(d_rise, channels // size, True)
    params = head_params[...]
    rate = jnp.exp(params[1:2])
    valid = valid_column(info, lengths, seq, length)
    d_raw = (d_step + rate * gathered) * sigmoid(raw[0] + params[0:1]) * valid * params[2:3]
    d_raw_out[0] = d_raw.astype(BF)
    ext[:HALO] = rim[0]
    ext[HALO:] = feed[0]

    @pl.when(seq == 0)
    def _():
        conv_out[...] = jnp.zeros_like(conv_out)
        head_out[...] = jnp.zeros_like(head_out)

    head_out[0:1] += jnp.sum(d_raw, axis=0, keepdims=True)
    head_out[1:2] += rate * jnp.sum(step_all * gathered, axis=0, keepdims=True)
    for start, stop, d_act in (
        (0, channels, d_values),
        (channels, channels + state, d_keys),
        (channels + state, channels + 2 * state, d_queries),
    ):
        at = slice(start, stop)
        pre = conv_w[taps : taps + 1, at]
        for k in range(taps):
            begin = HALO - taps + 1 + k
            pre = pre + conv_w[k : k + 1, at] * ext[begin : begin + length, at]
        sig = sigmoid(pre)
        d_pre = d_act * valid * (sig * (1.0 + pre * (1.0 - sig)))
        d_pre_out[0, :, at] = d_pre
        first_out[0, :, at] = d_pre[:8]
        for k in range(taps):
            begin = HALO - taps + 1 + k
            conv_out[k : k + 1, at] += jnp.sum(d_pre * ext[begin : begin + length, at], axis=0, keepdims=True)
        conv_out[taps : taps + 1, at] += jnp.sum(d_pre, axis=0, keepdims=True)


def spread_body(n, nh, channels, taps, info, d_pre, d_next, d_gate, d_raw, w_z, w_x, w_bc, w_dt, conv_w, *refs):
    d_feed_out, outs, ext, table = refs[0], refs[1 : 1 + nh], refs[1 + nh], refs[2 + nh]
    length = d_pre.shape[1]
    ext[:length] = d_pre[0]
    ext[length:] = d_next[0]
    d_feed = conv_w[taps - 1 : taps] * ext[:length]
    for k in range(taps - 1):
        d_feed = d_feed + conv_w[k : k + 1] * ext[taps - 1 - k : taps - 1 - k + length]
    low = d_feed.astype(BF)
    d_feed_out[0] = low
    cols = w_z.shape[2]
    for s in range(n):
        at = slice(s * cols, (s + 1) * cols)
        running = mm(d_gate[0], w_z[s, 0], NT)
        running = running + mm(low[:, :channels], w_x[s, 0], NT)
        running = running + mm(low[:, channels:], w_bc[at, :], NT)
        table[:, at] = running + mm(d_raw[0], w_dt[:, at])
    scatter_rows(info, outs, table, length // nh)


def weight_body(groups, *refs):
    normal, grad, x, d_gate = (refs[i * groups : (i + 1) * groups] for i in range(4))
    out = refs[4 * groups]
    for place, (lefts, rights) in enumerate(((normal, grad), (x, d_gate))):
        summed = mm(lefts[0][...], rights[0][...], TN)
        for left, right in zip(lefts[1:], rights[1:]):
            summed = summed + mm(left[...], right[...], TN)
        out[0, place] = summed.astype(BF)


def feed_weight_body(nh, groups, channels, info, *refs):
    x, d_feed, d_raw = (refs[i * groups : (i + 1) * groups] for i in range(3))
    x_out, dt_out, *outs = refs[3 * groups : 3 * groups + 2 + nh]
    table = refs[3 * groups + 2 + nh]
    for g in range(groups):
        left = x[g][...]
        made = mm(left, d_feed[g][...], TN)
        steps = mm(d_raw[g][...], left, TN)[: dt_out.shape[1]]
        if g == 0:
            table[...] = made
            dt_out[0] = steps
        else:
            table[...] += made
            dt_out[0] += steps
    x_out[0] = table[:, :channels].astype(BF)
    own = table.shape[0] // nh
    for k, out in enumerate(outs):
        start = pl.multiple_of((info[0] ^ k) * own, own)
        out[0] = table[pl.ds(start, own), channels:].astype(BF)


def place_body(nh, info, *refs):
    pieces, out = refs[:nh], refs[nh]
    for k in range(nh):
        for layer in range(out.shape[0]):
            out[layer, info[0] ^ k] = pieces[k][layer]


def gather_plan(layers):
    order = [(kind, layer) for layer in range(layers) for kind in ("x", "z", "o")]
    return [order[:1]] + [order[at : at + 2] for at in range(1, len(order), 2)]


def shards(
    hidden_in, grad_out, lengths, norm_gain, w_z, w_x, w_bc, w_dt, conv_x, conv_x_bias, conv_bc,
    conv_bc_bias, dt_bias, a_log, d_skip, y_gain, w_out,
):
    n, nh = lax.axis_size("seq"), lax.axis_size("heads")
    layers, depth, channels = w_z.shape
    width = depth * n
    heads_here = w_dt.shape[2]
    size = channels // heads_here
    both = w_bc.shape[2]
    state = both // 2
    taps = conv_x.shape[1]
    own, batches, _ = hidden_in.shape
    length = own * nh
    total = channels * nh
    feed_width = channels + both
    groups = GROUPS
    while batches % groups:
        groups //= 2
    part = batches // groups
    tokens = part * length
    here, place = lax.axis_index("heads"), lax.axis_index("seq")
    every = range(groups)
    infos = [jnp.stack([here, place, place * length, g * part]).astype(jnp.int32) for g in every]
    spans = [lengths[g * part : (g + 1) * part] for g in every]
    line = Line()
    call = line.call

    def flip(x, k):
        return lax.ppermute(x, "heads", [(i, i ^ k) for i in range(nh)])

    def along(x, s, keep=lambda i, j: True):
        pairs = [(i, (i + s) % n) for i in range(n) if keep(i, (i + s) % n)]
        return lax.ppermute(x, "seq", pairs)

    def gather_heads(x):
        evens = [x] + [flip(x, k) for k in range(2, nh, 2)]
        odds = [flip(piece, 1) for piece in evens]
        return [piece for pair in zip(evens, odds) for piece in pair]

    def scatter_heads(pieces):
        sums = [
            (pieces[k].astype(F32) + flip(pieces[k + 1], 1).astype(F32)).astype(BF)
            for k in range(0, nh, 2)
        ]
        return [sums[0]] + [flip(sums[k // 2], k) for k in range(2, nh, 2)]

    def gather_seq(x):
        return [x] + [along(x, s) for s in range(1, n)]

    def scatter_seq(a):
        own_part = lax.dynamic_index_in_dim(a, place, 0, False).astype(F32)
        for s in range(1, n):
            piece = lax.dynamic_index_in_dim(a, lax.rem(place + s, n), 0, False)
            own_part = own_part + along(piece, s).astype(F32)
        return own_part

    def in_order(parts):
        return jnp.roll(jnp.stack(parts[::-1]), place + 1, axis=0)

    weights = {}
    for batch in gather_plan(layers):
        sources = [{"x": w_x, "z": w_z, "o": w_out}[kind][layer] for kind, layer in batch]
        table = lax.all_gather(jnp.stack(sources), "seq", axis=0)
        for at, key in enumerate(batch):
            weights[key] = (table, at)

    def weight_spec(table, at):
        rank = len(table.shape)
        return pl.BlockSpec((table.shape[0], 1) + tuple(table.shape[2:]), lambda i: (0, at) + (0,) * (rank - 2))

    gains = in_order(gather_seq(norm_gain)).transpose(1, 0, 2).reshape(layers, 1, width).astype(F32)
    x_res = [hidden_in[:, g * part : (g + 1) * part].transpose(1, 0, 2).astype(F32) for g in every]
    normed = []
    for g in every:
        outs = [sds((part, own, width), BF)]
        normed += call(
            first_norm_body, part, [x_res[g], gains[0]], [per_seq(x_res[g]), whole(gains[0])], outs,
            [per_seq(outs[0])], name="first_norm",
        )
    rows_here = depth // nh
    share = lax.dynamic_slice_in_dim(w_bc, here * rows_here, rows_here, 1)
    share = jnp.stack(gather_seq(share))
    step_rows = jnp.pad(w_dt.transpose(0, 2, 1), ((0, 0), (0, -heads_here % 16), (0, 0)))
    shared_pieces = gather_heads(share)
    step_pieces = gather_seq(step_rows)
    collected = [sds((layers, n, nh, rows_here, both), BF), sds((layers, LANES, width), BF)]
    ins = [infos[0]] + shared_pieces + step_pieces
    shared_w, step_w = call(
        functools.partial(collect_body, n, nh), 1, ins, [smem()] + [whole(a) for a in ins[1:]],
        collected, [whole(a) for a in collected], name="collect",
    )
    shared_w = shared_w.reshape(layers, width, both)

    conv_all = jnp.concatenate([conv_x, conv_bc], axis=-1)
    bias_all = jnp.concatenate([conv_x_bias, conv_bc_bias], axis=-1)
    conv_all = jnp.concatenate(
        [conv_all, bias_all[:, None], jnp.zeros((layers, 7 - taps, feed_width), F32)], axis=1
    )
    lanes_used = (jnp.arange(LANES) < heads_here).astype(F32)
    pad_heads = lambda a: jnp.pad(a, ((0, 0), (0, LANES - heads_here)))
    head_all = jnp.stack(
        [pad_heads(dt_bias), pad_heads(a_log), jnp.broadcast_to(lanes_used, (layers, LANES))]
        + [jnp.zeros((layers, LANES), F32)] * 5,
        axis=1,
    )
    chan_all = jnp.stack(
        [y_gain, jnp.repeat(d_skip, size, axis=1)] + [jnp.zeros((layers, channels), F32)] * 6, axis=1
    )

    state_shape = sds((part, state, channels), BF)

    def first_hop(states, back):
        pair = (n - 1, n - 2) if back else (0, 1)
        return [lax.ppermute(states, "seq", [pair])]

    def next_hop(arrived, states, fade, back):
        at = len(arrived)
        ins = [arrived[-1], states, fade]
        (out,) = call(
            hop_body, part, ins, [per_seq(a) for a in ins], [state_shape], [per_seq(state_shape)], name="hop"
        )
        pair = (n - 1 - at, n - 2 - at) if back else (at, at + 1)
        arrived.append(lax.ppermute(out, "seq", [pair]))

    def rim_of(pieces):
        rows = sum(
            jnp.where((here ^ k) == nh - 1, pieces[k][:, own - HALO :].astype(F32), 0.0) for k in range(nh)
        ).astype(BF)
        return along(rows, 1, lambda i, j: j == i + 1).reshape(part * HALO, width)

    stored = []
    for layer in range(layers):
        conv_w, head_params, chan = conv_all[layer], head_all[layer], chan_all[layer]
        wbc_full, wdt_full = shared_w[layer], step_w[layer]
        w_x_full, w_z_full, w_o_full = weights["x", layer], weights["z", layer], weights["o", layer]
        saved = [dict(x_res=x_res[g]) for g in every]
        arrived, states, local = [None] * groups, [None] * groups, [None] * groups
        for g in every:
            it = saved[g]
            pieces = gather_heads(normed[g])
            x_halo = rim_of(pieces)
            ins = [infos[g]] + pieces + [w_x_full[0], wbc_full, wdt_full]
            outs = [
                sds((part, length, width), BF),
                sds((part, length, feed_width), F32),
                sds((part, length, LANES), F32),
            ]
            it["x_all"], it["feed"], it["raw"] = call(
                functools.partial(project_body, nh, channels), part, ins,
                [smem()] + [per_seq(a) for a in pieces] + [weight_spec(*w_x_full), whole(wbc_full), whole(wdt_full)],
                outs, [per_seq(a) for a in outs],
                name="project",
            )
            ins = [infos[g], spans[g], it["feed"], it["raw"], x_halo, w_x_full[0], wbc_full, conv_w, head_params, chan]
            outs = [
                sds((part, length, channels), BF),
                sds((part, length, both), BF),
                sds((part, length, LANES), F32),
                sds((part, length, LANES), F32),
                sds((part, length, channels), F32),
                state_shape,
                sds((part, 8, channels), F32),
                sds((part, HALO, feed_width), F32),
            ]
            specs = [per_seq(a) for a in outs]
            it["values"], it["shared"], it["rise"], it["step"], local[g], states[g], it["fade"], it["rim"] = call(
                functools.partial(local_body, channels, size, taps), part, ins,
                [smem(), smem(), per_seq(ins[2]), per_seq(ins[3]), whole(x_halo), weight_spec(*w_x_full)]
                + [whole(a) for a in ins[6:]],
                outs, specs,
                scratch=[
                    pltpu.VMEM((HALO + length, feed_width), F32),
                    pltpu.VMEM((part * HALO, feed_width), F32),
                ],
                name="local",
            )
            arrived[g] = first_hop(states[g], False)

        def gate(g):
            it = saved[g]
            outs = [sds((part, length, channels), BF)]
            (it["gate"],) = call(
                gate_body, part, [it["x_all"], w_z_full[0]], [per_seq(it["x_all"]), weight_spec(*w_z_full)],
                outs, [per_seq(outs[0])], name="gate",
            )

        def all_hops(fillers):
            for at in range(1, n - 1):
                for g in every:
                    next_hop(arrived[g], states[g], saved[g]["fade"], False)
                if fillers:
                    fillers.pop(0)()
            for filler in fillers:
                filler()

        all_hops([functools.partial(gate, g) for g in every])
        summed = [None] * groups
        for g in every:
            it = saved[g]
            ins = [infos[g], local[g], it["gate"], it["shared"], it["rise"], w_o_full[0], chan] + arrived[g]
            outs = [sds((part, length, channels), F32), sds((part, state, channels), BF)] + [
                sds((part, own, width + LANES), BF)
            ] * nh
            it["full"], it["carried"], *projected = call(
                functools.partial(output_body, n, nh, size), part, ins,
                [smem()] + [per_seq(a) for a in ins[1:5]] + [weight_spec(*w_o_full), whole(chan)]
                + [per_seq(a) for a in ins[7:]],
                outs, [per_seq(a) for a in outs],
                scratch=[pltpu.VMEM((length, width + LANES), F32)],
                name="output",
            )
            summed[g] = scatter_heads(projected)
        gain_next = gains[min(layer + 1, layers - 1)]
        for g in every:
            it = saved[g]
            ins = [infos[g], x_res[g], gain_next] + summed[g]
            outs = [
                sds((part, own, width), F32),
                sds((part, own, width), BF),
                sds((part, own, width), BF),
                sds((part, own, LANES), BF),
            ]
            x_res[g], it["branch"], normed[g], it["factor"] = call(
                functools.partial(norm_body, False, width, total), part, ins,
                [smem(), per_seq(ins[1]), whole(gain_next)] + [per_seq(a) for a in summed[g]],
                outs, [per_seq(a) for a in outs], name="norm",
            )
        stored.append(saved)

    grad_res, payload = [None] * groups, [None] * groups
    for g in every:
        top = stored[-1][g]
        grad_low = grad_out[:, g * part : (g + 1) * part].transpose(1, 0, 2)
        ins = [grad_low, top["branch"], top["factor"]]
        outs = [sds((part, own, width + LANES), BF)]
        (payload[g],) = call(
            first_back_body, part, ins, [per_seq(a) for a in ins], outs, [per_seq(a) for a in outs],
            name="first_back",
        )
        grad_res[g] = grad_low.astype(F32)
    flat = lambda a: a.reshape(tokens, a.shape[2])
    cut = pl.BlockSpec((tokens, depth), lambda i: (0, i))
    early_grads, late_grads = [None] * layers, [None] * layers
    shared_grads, small_grads = [None] * layers, [None] * layers
    for layer in reversed(range(layers)):
        conv_w, head_params, chan = conv_all[layer], head_all[layer], chan_all[layer]
        wbc_full, wdt_full = shared_w[layer], step_w[layer]
        w_x_full, w_z_full, w_o_full = weights["x", layer], weights["z", layer], weights["o", layer]
        saved = stored[layer]
        work = [dict() for g in every]
        for g in every:
            it, to = saved[g], work[g]
            pieces = gather_heads(payload[g])
            ins = [infos[g]] + [it[k] for k in ("gate", "full", "values", "shared", "rise")]
            ins += [w_o_full[0], chan] + pieces
            outs = [
                sds((part, length, width), BF),
                sds((part, length, channels), BF),
                sds((part, length, channels), BF),
                sds((part, length, channels), BF),
                state_shape,
                sds((8, channels), F32),
            ]
            specs = [per_seq(a) for a in outs[:5]] + [whole(outs[5])]
            to["grad"], to["d_gate"], to["normal"], to["d_full"], states[g], to["chan"] = call(
                functools.partial(gate_back_body, n, nh, size, total), part, ins,
                [smem()] + [per_seq(a) for a in ins[1:6]] + [weight_spec(*w_o_full), whole(chan)]
                + [per_seq(a) for a in pieces],
                outs, specs, scratch=[pltpu.VMEM((length, LANES), F32)],
                name="gate_back",
            )
            arrived[g] = first_hop(states[g], True)
        ins = [flat(to["normal"]) for to in work] + [flat(to["grad"]) for to in work]
        ins += [flat(it["x_all"]) for it in saved] + [flat(to["d_gate"]) for to in work]
        outs = [sds((n, 2, depth, channels), BF)]
        (early,) = call(
            functools.partial(weight_body, groups), n, ins,
            [whole(a) for a in ins[:groups]] + [cut] * (2 * groups) + [whole(a) for a in ins[3 * groups :]],
            outs, [per_seq(outs[0])], name="early_weights",
        )
        early_grads[layer] = lax.psum_scatter(early, "seq", scatter_dimension=0, tiled=False)

        def mix_back(g):
            it, to = saved[g], work[g]
            ins = [to["d_full"]] + [it[k] for k in ("full", "values", "shared", "rise", "step", "carried")] + [chan]
            outs = [
                sds((part, length, channels), BF),
                sds((part, length, both), F32),
                sds((part, length, 2 * LANES), F32),
            ]
            to["d_values"], to["d_shared"], to["d_rates"] = call(
                functools.partial(mix_back_body, size), part, ins,
                [per_seq(a) for a in ins[:-1]] + [whole(chan)], outs, [per_seq(a) for a in outs],
                name="mix_back",
                after=[late_grads[layer + 1]] if layer + 1 < layers and g == groups - 1 else [],
            )

        def state_back(g):
            it, to = saved[g], work[g]
            ins = [infos[g], spans[g]]
            ins += [it[k] for k in ("feed", "raw", "rim", "values", "shared", "rise", "step", "carried")]
            ins += [to["d_values"], to["d_shared"], to["d_rates"], conv_w, head_params] + arrived[g]
            outs = [
                sds((part, length, feed_width), F32),
                sds((part, 8, feed_width), F32),
                sds((part, length, LANES), BF),
                sds((8, feed_width), F32),
                sds((8, LANES), F32),
            ]
            to["d_pre"], first_rows, to["d_raw"], to["conv"], to["head"] = call(
                functools.partial(state_back_body, n, channels, size, taps), part, ins,
                [smem(), smem()] + [per_seq(a) for a in ins[2:13]] + [whole(conv_w), whole(head_params)]
                + [per_seq(a) for a in ins[15:]],
                outs, [per_seq(a) for a in outs[:3]] + [whole(a) for a in outs[3:]],
                scratch=[pltpu.VMEM((HALO + length, feed_width), F32)],
                name="state_back",
            )
            to["next"] = along(first_rows, -1, lambda i, j: j == i - 1)

        def spread(g):
            to = work[g]
            ins = [infos[g], to["d_pre"], to["next"], to["d_gate"], to["d_raw"]]
            ins += [w_z_full[0], w_x_full[0], wbc_full, wdt_full, conv_w]
            outs = [sds((part, length, feed_width), BF)] + [sds((part, own, width), BF)] * nh
            to["d_feed"], *pieces = call(
                functools.partial(spread_body, n, nh, channels, taps), part, ins,
                [smem()] + [per_seq(a) for a in ins[1:5]] + [weight_spec(*w_z_full), weight_spec(*w_x_full)]
                + [whole(a) for a in ins[7:]],
                outs, [per_seq(a) for a in outs],
                scratch=[pltpu.VMEM((length + 8, feed_width), F32), pltpu.VMEM((length, width), F32)],
                name="spread",
            )
            to["summed"] = scatter_heads(pieces)

        def all_hops_back(fillers):
            for at in range(1, n - 1):
                for g in every:
                    next_hop(arrived[g], states[g], saved[g]["fade"], True)
                if fillers:
                    fillers.pop(0)()
            for filler in fillers:
                filler()

        all_hops_back([functools.partial(mix_back, g) for g in every])
        for g in every:
            state_back(g)
        for g in every:
            spread(g)
        ins = [infos[0]] + [flat(it["x_all"]) for it in saved]
        ins += [flat(to["d_feed"]) for to in work] + [flat(to["d_raw"]) for to in work]
        outs = [sds((n, depth, channels), BF), sds((n, 16, depth), F32)] + [sds((n, rows_here, both), BF)] * nh
        d_wx, d_wdt, *shared_parts = call(
            functools.partial(feed_weight_body, nh, groups, channels), n, ins,
            [smem()] + [cut] * groups + [whole(a) for a in ins[1 + groups :]], outs, [per_seq(a) for a in outs],
            scratch=[pltpu.VMEM((depth, feed_width), F32)],
                name="late_weights",
        )
        late_grads[layer] = lax.psum_scatter(d_wx, "seq", scatter_dimension=0, tiled=False)
        below = stored[max(layer - 1, 0)]
        for g in every:
            it, to = saved[g], work[g]
            ins = [it["x_res"], gains[layer], grad_res[g], below[g]["branch"], below[g]["factor"]] + to["summed"]
            outs = [
                sds((part, own, width), F32),
                sds((part, own, width + LANES), BF),
                sds((part, 8, width), F32),
            ]
            grad_res[g], payload[g], to["gain"] = call(
                functools.partial(back_norm_body, width), part, ins,
                [per_seq(ins[0]), whole(ins[1])] + [per_seq(a) for a in ins[2:]],
                outs, [per_seq(a) for a in outs], name="back_norm",
                after=[early_grads[layer]] if g == groups - 1 and layer > 0 else [],
            )
        shared_grads[layer] = (shared_parts, d_wdt)
        small_grads[layer] = tuple(sum(to[k] for to in work) for k in ("chan", "conv", "head")) + (
            sum(jnp.sum(to["gain"][:, 0], axis=0) for to in work),
        )

    def sum_seq(a):
        return sum(gather_seq(a)[1:], a)

    def sum_heads(a):
        for bit in range(nh.bit_length() - 1):
            a = a + flip(a, 1 << bit)
        return a

    per_head = jnp.stack(
        [
            jnp.concatenate(
                [
                    s[0][:2].reshape(-1),
                    s[1][: taps + 1, :channels].reshape(-1),
                    s[2][:2].reshape(-1),
                    s[1][: taps + 1, channels:].reshape(-1),
                    s[3],
                ]
            )
            for s in small_grads
        ]
    )
    per_head = sum_seq(per_head)
    cut_at = 2 * channels + (taps + 1) * channels + 2 * LANES
    everywhere = sum_heads(per_head[:, cut_at:])
    chan_total = per_head[:, : 2 * channels].reshape(layers, 2, channels)
    conv_total = per_head[:, 2 * channels : (taps + 3) * channels].reshape(layers, taps + 1, channels)
    head_total = per_head[:, (taps + 3) * channels : cut_at].reshape(layers, 2, LANES)
    conv_shared = everywhere[:, : (taps + 1) * both].reshape(layers, taps + 1, both)
    gain_grad = lax.dynamic_slice_in_dim(everywhere[:, (taps + 1) * both :], place * depth, depth, 1)
    stacked = [jnp.stack([s[0][k] for s in shared_grads], axis=1) for k in range(nh)]
    in_plane = sum(a.astype(F32) for a in scatter_heads(stacked)).reshape(n, -1, both)
    steps = jnp.stack([s[1] for s in shared_grads], axis=1).reshape(n, -1, both)
    summed = scatter_seq(jnp.concatenate([in_plane, steps], axis=1))
    split_at = layers * rows_here
    pieces = gather_heads(summed[:split_at].reshape(layers, rows_here, both))
    step_sums = summed[split_at:].reshape(layers, 16, depth)
    ins = [infos[0]] + pieces
    outs = [sds((layers, nh, rows_here, both), F32)]
    (table,) = call(
        functools.partial(place_body, nh), 1, ins, [smem()] + [whole(a) for a in pieces],
        outs, [whole(outs[0])], name="place",
    )
    shared_grad = table.reshape(layers, depth, both)
    dt_grad = step_sums[:, :heads_here].transpose(0, 2, 1)
    back = lambda parts: jnp.concatenate(parts, axis=0).transpose(1, 0, 2)
    return (
        back(x_res),
        back(grad_res),
        gain_grad,
        jnp.stack([e[1] for e in early_grads]).astype(F32),
        jnp.stack(late_grads).astype(F32),
        shared_grad,
        dt_grad,
        conv_total[:, :taps],
        conv_total[:, taps],
        conv_shared[:, :taps],
        conv_shared[:, taps],
        head_total[:, 0, :heads_here],
        head_total[:, 1, :heads_here],
        jnp.sum(chan_total[:, 1].reshape(layers, heads_here, size), axis=-1),
        chan_total[:, 0],
        jnp.stack([e[0] for e in early_grads]).astype(F32),
    )


def solution(mesh):
    rows = P(("seq", "heads"), None, None)
    placed = (
        rows, rows, P(), P(None, "seq"), P(None, "seq", "heads"), P(None, "seq", "heads"),
        P(None, "seq", None), P(None, "seq", "heads"), P(None, None, "heads"), P(None, "heads"), P(), P(),
        P(None, "heads"), P(None, "heads"), P(None, "heads"), P(None, "heads"), P(None, "heads", "seq"),
    )
    made = (
        rows, rows, P(None, "seq"), P(None, "seq", "heads"), P(None, "seq", "heads"),
        P(None, "seq", None), P(None, "seq", "heads"), P(None, None, "heads"), P(None, "heads"), P(), P(),
        P(None, "heads"), P(None, "heads"), P(None, "heads"), P(None, "heads"), P(None, "heads", "seq"),
    )
    return jax.shard_map(shards, mesh=mesh, in_specs=placed, out_specs=made, check_vma=False)
```

time: 2410 us -> 1300 us (0.54)
  waiting for transfers between devices: 1380 us -> 358 us
  Pallas kernels: 0 us -> 456 us
  matrix products: 416 us -> 0 us
  starting transfers between devices: 33.2 us -> 321 us
  blocking collectives: 205 us -> 0 us
  other arithmetic: 231 us -> 50.6 us
  local copies, waits for them, and re-layouts: 117 us -> 89.7 us
    all_gather x24 -> x5, waiting for transfers between devices: 671 us -> 0.06 us  [shards(): table = lax.all_gather(jnp.stack(sources), 'seq', axis=0)]
    reduce_scatter x18 -> x6, waiting for transfers between devices: 538 us -> 0.05 us  [the longest x3 0.04 us: shards(): lax.psum_scatter(d_wx, 'seq', scatter_dimension=0, tiled=False)]
    pallas_call x0 -> x96, Pallas kernels: none -> 456 us  [call(): pl.pallas_call(kernel, grid=(grid,), in_specs=list(in_specs) + [anywhere(...]
    dot_general x81 -> x0, matrix products: 416 us -> none  [the longest x9 36.4 us: block_state(): jnp.einsum('smh,smhp,smn->mhpn', weighting, value_heads, key_rows, precis...]
    ppermute x6 -> x255, waiting for transfers between devices: 0.84 us -> 358 us  [the longest x192 149 us: flip(): return lax.ppermute(x, 'heads', [(i, i ^ k) for i in range(nh)])]
    ppermute x6 -> x255, starting transfers between devices: 30.4 us -> 320 us  [the longest x192 193 us: flip(): return lax.ppermute(x, 'heads', [(i, i ^ k) for i in range(nh)])]
    psum x1 -> x0, waiting for transfers between devices: 161 us -> none  [shards(): lax.psum(shared_sets[layer_index], ('seq', 'heads'))]
    psum x8 -> x0, blocking collectives: 126 us -> none  [the longest x1 39.2 us: shards(): lax.psum(shared_sets[layer_index], ('seq', 'heads'))]
  transfers between devices with their start and end apart: 49 -> 266, of which waited for: 38 -> 65; matrix products, arithmetic and copies ran while one was open for 18% -> 6% of each run, Pallas kernels for 0% -> 32%
where the time goes in v1:
time: 1300 us; the launch traced here: 1290 us
  Pallas kernels  456 us (35%)
  waiting for transfers between devices  358 us (28%)
  starting transfers between devices  321 us (25%)
  local copies, waits for them, and re-layouts  89.7 us (7%)
  other arithmetic  50.6 us (4%)
  between operations  18.2 us (1%)
    pallas_call x96, Pallas kernels, call(): pl.pallas_call(kernel, grid=(grid,), in_specs=list(in_specs) + [anywhere(...  456 us
    ppermute x192, starting transfers between devices, flip(): return lax.ppermute(x, 'heads', [(i, i ^ k) for i in range(nh)])  193 us
    ppermute x192, waiting for transfers between devices, flip(): return lax.ppermute(x, 'heads', [(i, i ^ k) for i in range(nh)])  149 us
    ppermute x27, waiting for transfers between devices, along(): return lax.ppermute(x, 'seq', pairs)  103 us
    ppermute x24, waiting for transfers between devices, next_hop(): arrived.append(lax.ppermute(out, 'seq', [pair]))  94.9 us
    ppermute x27, starting transfers between devices, along(): return lax.ppermute(x, 'seq', pairs)  85.3 us
    unnamed x628, local copies, waits for them, and re-layouts  62.8 us
    ppermute x24, starting transfers between devices, next_hop(): arrived.append(lax.ppermute(out, 'seq', [pair]))  29.6 us
  transfers between devices with their start and end apart: 266, of which 65 were waited for; matrix products, arithmetic and copies ran while one was open for 6% of the time, Pallas kernels for 32%

profile of v1, /device:TPU:9, one launch (start us, length us, event | category | flops | bytes accessed | tf_op | source)
XLA Modules:
  0.0 1292.4 jit_solution(5140480749499184231)
XLA Ops:
  48.1 8.6 collective-permute-done.11
  118.4 8.2 local.6
  139.8 8.0 collective-permute-done.31
  148.5 8.2 local.7
  176.5 14.1 %collective-permute-done.36.refs_0_.refs_8_ = bf16[2,128,512]{2,1,0:T(8,128)(2,1)S(1)} collective-permute-done((bf16[2,128,512]{2,1,0:T(8,128)(2,1)}, bf16[2,128,512]{2,1,0:T(8,128)(2,1)S(1)}, u32[]{:S(2)}, u32[]{:S(2)}) %collective-permute-start.36) | collective-permute-done | bytes 262176 | tf_op jit(solution)/shard_map/ppermute | solution.py:718
  235.7 6.5 collective-permute-done.56.refs_5_
  261.1 11.8 collective-permute-start.49
  275.4 28.9 %collective-permute-start.59 = (bf16[2,16,2048]{2,1,0:T(8,128)(2,1)}, bf16[2,16,2048]{2,1,0:T(8,128)(2,1)S(1)}, u32[]{:S(2)}, u32[]{:S(2)}) collective-permute-start(bf16[2,16,2048]{2,1,0:T(8,128)(2,1)} %add_convert_fusion.55), channel_id=1, source_target_pairs={{0,8},{8,16},{16,24},{1,9},{9,17},{17,25},{2,10},{10,18},{18,26},{... | collective-permute-start | bytes 393224 | tf_op jit(solution)/shard_map/ppermute | solution.py:628
  314.2 8.3 local.8
  340.3 8.3 local.9
  414.9 6.6 collective-permute-done.92.refs_5_
  430.3 7.9 collective-permute-done.99.refs_5_
  442.2 7.2 collective-permute-done.84.refs_5_
  453.0 6.7 collective-permute-start.95
  466.5 8.4 local.10
  487.6 8.3 local.11
  562.0 6.7 collective-permute-done.121.refs_5_
  617.5 9.3 early_weights.3
  637.0 6.7 mix_back.6
  643.7 15.8 %collective-permute-done.140.refs_0_.refs_16_ = bf16[2,128,512]{2,1,0:T(8,128)(2,1)S(1)} collective-permute-done((bf16[2,128,512]{2,1,0:T(8,128)(2,1)}, bf16[2,128,512]{2,1,0:T(8,128)(2,1)S(1)}, u32[]{:S(2)}, u32[]{:S(2)}) %collective-permute-start.140) | collective-permute-done | bytes 262176 | tf_op jit(solution)/shard_map/ppermute | solution.py:718
  663.3 18.7 %collective-permute-done.142.refs_0_.refs_16_ = bf16[2,128,512]{2,1,0:T(8,128)(2,1)S(1)} collective-permute-done((bf16[2,128,512]{2,1,0:T(8,128)(2,1)}, bf16[2,128,512]{2,1,0:T(8,128)(2,1)S(1)}, u32[]{:S(2)}, u32[]{:S(2)}) %collective-permute-start.142) | collective-permute-done | bytes 262176 | tf_op jit(solution)/shard_map/ppermute | solution.py:718
  685.8 6.7 mix_back.7
  693.2 7.4 state_back.6
  709.5 7.5 state_back.7
  717.7 8.1 spread.6
  733.8 8.1 spread.7
  742.7 7.8 late_weights.3
  820.5 9.3 early_weights.4
  839.9 6.7 mix_back.8
  846.6 15.1 %collective-permute-done.176.refs_0_.refs_16_ = bf16[2,128,512]{2,1,0:T(8,128)(2,1)S(1)} collective-permute-done((bf16[2,128,512]{2,1,0:T(8,128)(2,1)}, bf16[2,128,512]{2,1,0:T(8,128)(2,1)S(1)}, u32[]{:S(2)}, u32[]{:S(2)}) %collective-permute-start.176) | collective-permute-done | bytes 262176 | tf_op jit(solution)/shard_map/ppermute | solution.py:718
  865.4 18.7 %collective-permute-done.178.refs_0_.refs_16_ = bf16[2,128,512]{2,1,0:T(8,128)(2,1)S(1)} collective-permute-done((bf16[2,128,512]{2,1,0:T(8,128)(2,1)}, bf16[2,128,512]{2,1,0:T(8,128)(2,1)S(1)}, u32[]{:S(2)}, u32[]{:S(2)}) %collective-permute-start.178) | collective-permute-done | bytes 262176 | tf_op jit(solution)/shard_map/ppermute | solution.py:718
  888.0 6.7 mix_back.9
  895.4 7.4 state_back.8
  911.6 7.4 state_back.9
  919.6 8.1 spread.8
  937.5 8.1 spread.9
  946.5 7.8 late_weights.4
  1024.8 9.2 early_weights.5
  1042.1 6.7 mix_back.10
  1058.0 6.7 mix_back.11
  1065.4 7.4 state_back.10
  1075.5 7.4 state_back.11
  1085.6 8.1 spread.10
  1094.3 8.1 spread.11
  1102.4 7.8 late_weights.5
  1170.6 12.9 collective-permute-done.233
  1204.7 9.2 collective-permute-done.245
  1213.9 39.4 %collective-permute-done.246 = f32[288,256]{1,0:T(8,128)S(1)} collective-permute-done((f32[288,256]{1,0:T(8,128)}, f32[288,256]{1,0:T(8,128)S(1)}, u32[]{:S(2)}, u32[]{:S(2)}) %collective-permute-start.246) | collective-permute-done | bytes 294944 | tf_op jit(solution)/shard_map/ppermute | solution.py:628
  (1397 shorter events, 797.3 us)
Async XLA Ops:
  7.2 104.3 %all-gather.11.cloned.1.call-start = ((), (), s32[]{:S(2)}) async-start(), calls=%async_computation.12 | async-start | bytes 2621440 | tf_op jit(solution)/shard_map/all_gather | solution.py:658
  9.8 159.2 %all-gather.13.cloned.1.call-start = ((), (), s32[]{:S(2)}) async-start(), calls=%async_computation.13 | async-start | bytes 5242880 | tf_op jit(solution)/shard_map/all_gather | solution.py:658
  13.0 291.3 %all-gather.15.cloned.1.call-start = ((), (), s32[]{:S(2)}) async-start(), calls=%async_computation.14 | async-start | bytes 5242880 | tf_op jit(solution)/shard_map/all_gather | solution.py:658
  17.8 24.8 %collective-permute-start.20 = (bf16[3,16,512]{2,1,0:T(8,128)(2,1)S(1)}, bf16[3,16,512]{2,1,0:T(8,128)(2,1)}, u32[]{:S(2)}, u32[]{:S(2)}) collective-permute-start(bf16[3,16,512]{2,1,0:T(8,128)(2,1)S(1)} %pad.11.refs_9_), channel_id=1, source_target_pairs={{0,8},{8,16},{16,24},{24,0},{1,9},{9,17},{17,25},{25,1},{2,10},{10... | collective-permute-start | bytes 147464 | tf_op jit(solution)/shard_map/ppermute | solution.py:628
  17.8 26.6 %collective-permute-start.21 = (bf16[3,16,512]{2,1,0:T(8,128)(2,1)S(1)}, bf16[3,16,512]{2,1,0:T(8,128)(2,1)}, u32[]{:S(2)}, u32[]{:S(2)}) collective-permute-start(bf16[3,16,512]{2,1,0:T(8,128)(2,1)S(1)} %pad.11.refs_9_), channel_id=1, source_target_pairs={{0,16},{8,24},{16,0},{24,8},{1,17},{9,25},{17,1},{25,9},{2,18},{10... | collective-permute-start | bytes 147464 | tf_op jit(solution)/shard_map/ppermute | solution.py:628
  21.4 354.1 %all-gather.17.cloned.1.call-start = ((), (), s32[]{:S(2)}) async-start(), calls=%async_computation.15 | async-start | bytes 5242880 | tf_op jit(solution)/shard_map/all_gather | solution.py:658
  36.3 29.2 %collective-permute-start.4 = (bf16[2,32,2048]{2,1,0:T(8,128)(2,1)}, bf16[2,32,2048]{2,1,0:T(8,128)(2,1)S(1)}, u32[]{:S(2)}, u32[]{:S(2)}) collective-permute-start(bf16[2,32,2048]{2,1,0:T(8,128)(2,1)} %get-tuple-element.483.refs_1_), channel_id=1, source_target_pairs={{0,2},{1,3},{2,0},{3,1},{4,6},{5,7},{6,4},{7,5},{8,10},{9,11},{10,... | collective-permute-start | bytes 786440 | tf_op jit(solution)/shard_map/ppermute | solution.py:624
  37.5 28.1 %collective-permute-start.6 = (bf16[2,32,2048]{2,1,0:T(8,128)(2,1)}, bf16[2,32,2048]{2,1,0:T(8,128)(2,1)}, u32[]{:S(2)}, u32[]{:S(2)}) collective-permute-start(bf16[2,32,2048]{2,1,0:T(8,128)(2,1)} %get-tuple-element.483.refs_1_), channel_id=1, source_target_pairs={{0,4},{1,5},{2,6},{3,7},{4,0},{5,1},{6,2},{7,3},{8,12},{9,13},{10,... | collective-permute-start | bytes 786440 | tf_op jit(solution)/shard_map/ppermute | solution.py:624
  94.9 33.0 %collective-permute-start.24 = (bf16[2,32,2048]{2,1,0:T(8,128)(2,1)S(1)}, bf16[2,32,2048]{2,1,0:T(8,128)(2,1)S(1)}, u32[]{:S(2)}, u32[]{:S(2)}) collective-permute-start(bf16[2,32,2048]{2,1,0:T(8,128)(2,1)S(1)} %copy-done.69), channel_id=1, source_target_pairs={{0,1},{1,0},{2,3},{3,2},{4,5},{5,4},{6,7},{7,6},{8,9},{9,8},{10,11... | collective-permute-start | bytes 786440 | tf_op jit(solution)/shard_map/ppermute | solution.py:624
  99.0 28.9 %collective-permute-start.26 = (bf16[2,32,2048]{2,1,0:T(8,128)(2,1)}, bf16[2,32,2048]{2,1,0:T(8,128)(2,1)}, u32[]{:S(2)}, u32[]{:S(2)}) collective-permute-start(bf16[2,32,2048]{2,1,0:T(8,128)(2,1)} %collective-permute-done.25.refs_3_), channel_id=1, source_target_pairs={{0,1},{1,0},{2,3},{3,2},{4,5},{5,4},{6,7},{7,6},{8,9},{9,8},{10,11... | collective-permute-start | bytes 786440 | tf_op jit(solution)/shard_map/ppermute | solution.py:624
  99.1 28.8 %collective-permute-start.28 = (bf16[2,32,2048]{2,1,0:T(8,128)(2,1)}, bf16[2,32,2048]{2,1,0:T(8,128)(2,1)}, u32[]{:S(2)}, u32[]{:S(2)}) collective-permute-start(bf16[2,32,2048]{2,1,0:T(8,128)(2,1)} %collective-permute-done.27.refs_5_), channel_id=1, source_target_pairs={{0,1},{1,0},{2,3},{3,2},{4,5},{5,4},{6,7},{7,6},{8,9},{9,8},{10,11... | collective-permute-start | bytes 786440 | tf_op jit(solution)/shard_map/ppermute | solution.py:624
  99.6 28.4 %collective-permute-start.30 = (bf16[2,32,2048]{2,1,0:T(8,128)(2,1)}, bf16[2,32,2048]{2,1,0:T(8,128)(2,1)}, u32[]{:S(2)}, u32[]{:S(2)}) collective-permute-start(bf16[2,32,2048]{2,1,0:T(8,128)(2,1)} %collective-permute-done.29.refs_7_), channel_id=1, source_target_pairs={{0,1},{1,0},{2,3},{3,2},{4,5},{5,4},{6,7},{7,6},{8,9},{9,8},{10,11... | collective-permute-start | bytes 786440 | tf_op jit(solution)/shard_map/ppermute | solution.py:624
  126.6 31.4 %collective-permute-start.33 = (bf16[2,128,512]{2,1,0:T(8,128)(2,1)}, bf16[2,128,512]{2,1,0:T(8,128)(2,1)S(1)}, u32[]{:S(2)}, u32[]{:S(2)}) collective-permute-start(bf16[2,128,512]{2,1,0:T(8,128)(2,1)} %get-tuple-element.501.refs_1_), channel_id=1, source_target_pairs={{0,8},{1,9},{2,10},{3,11},{4,12},{5,13},{6,14},{7,15}} | collective-permute-start | bytes 786440 | tf_op jit(solution)/shard_map/ppermute | solution.py:709
  167.7 23.0 %collective-permute-start.36 = (bf16[2,128,512]{2,1,0:T(8,128)(2,1)}, bf16[2,128,512]{2,1,0:T(8,128)(2,1)S(1)}, u32[]{:S(2)}, u32[]{:S(2)}) collective-permute-start(bf16[2,128,512]{2,1,0:T(8,128)(2,1)} %get-tuple-element.513), channel_id=1, source_target_pairs={{8,16},{9,17},{10,18},{11,19},{12,20},{13,21},{14,22},{15,23}} | collective-permute-start | bytes 786440 | tf_op jit(solution)/shard_map/ppermute | solution.py:718
  206.4 301.7 %all-gather.19.cloned.1.call-start = ((), (), s32[]{:S(2)}) async-start(), calls=%async_computation.16 | async-start | bytes 5242880 | tf_op jit(solution)/shard_map/all_gather | solution.py:658
  248.7 24.2 %collective-permute-start.50 = (bf16[2,32,2048]{2,1,0:T(8,128)(2,1)S(1)}, bf16[2,32,2048]{2,1,0:T(8,128)(2,1)S(1)}, u32[]{:S(2)}, u32[]{:S(2)}) collective-permute-start(bf16[2,32,2048]{2,1,0:T(8,128)(2,1)S(1)} %copy-done.46), channel_id=1, source_target_pairs={{0,6},{1,7},{2,4},{3,5},{4,2},{5,3},{6,0},{7,1},{8,14},{9,15},{10,... | collective-permute-start | bytes 786440 | tf_op jit(solution)/shard_map/ppermute | solution.py:624
  273.0 50.8 %collective-permute-start.60 = (bf16[2,32,2048]{2,1,0:T(8,128)(2,1)}, bf16[2,32,2048]{2,1,0:T(8,128)(2,1)S(1)}, u32[]{:S(2)}, u32[]{:S(2)}) collective-permute-start(bf16[2,32,2048]{2,1,0:T(8,128)(2,1)} %get-tuple-element.549.refs_1_), channel_id=1, source_target_pairs={{0,1},{1,0},{2,3},{3,2},{4,5},{5,4},{6,7},{7,6},{8,9},{9,8},{10,11... | collective-permute-start | bytes 786440 | tf_op jit(solution)/shard_map/ppermute | solution.py:624
  273.5 50.4 %collective-permute-start.62 = (bf16[2,32,2048]{2,1,0:T(8,128)(2,1)S(1)}, bf16[2,32,2048]{2,1,0:T(8,128)(2,1)S(1)}, u32[]{:S(2)}, u32[]{:S(2)}) collective-permute-start(bf16[2,32,2048]{2,1,0:T(8,128)(2,1)S(1)} %collective-permute-done.61.refs_3_), channel_id=1, source_target_pairs={{0,1},{1,0},{2,3},{3,2},{4,5},{5,4},{6,7},{7,6},{8,9},{9,8},{10,11... | collective-permute-start | bytes 786440 | tf_op jit(solution)/shard_map/ppermute | solution.py:624
  273.6 50.3 %collective-permute-start.64 = (bf16[2,32,2048]{2,1,0:T(8,128)(2,1)S(1)}, bf16[2,32,2048]{2,1,0:T(8,128)(2,1)}, u32[]{:S(2)}, u32[]{:S(2)}) collective-permute-start(bf16[2,32,2048]{2,1,0:T(8,128)(2,1)S(1)} %collective-permute-done.63.refs_5_), channel_id=1, source_target_pairs={{0,1},{1,0},{2,3},{3,2},{4,5},{5,4},{6,7},{7,6},{8,9},{9,8},{10,11... | collective-permute-start | bytes 786440 | tf_op jit(solution)/shard_map/ppermute | solution.py:624
  274.1 49.8 %collective-permute-start.66 = (bf16[2,32,2048]{2,1,0:T(8,128)(2,1)S(1)}, bf16[2,32,2048]{2,1,0:T(8,128)(2,1)}, u32[]{:S(2)}, u32[]{:S(2)}) collective-permute-start(bf16[2,32,2048]{2,1,0:T(8,128)(2,1)S(1)} %collective-permute-done.65.refs_7_), channel_id=1, source_target_pairs={{0,1},{1,0},{2,3},{3,2},{4,5},{5,4},{6,7},{7,6},{8,9},{9,8},{10,11... | collective-permute-start | bytes 786440 | tf_op jit(solution)/shard_map/ppermute | solution.py:624
  275.4 38.2 %collective-permute-start.59 = (bf16[2,16,2048]{2,1,0:T(8,128)(2,1)}, bf16[2,16,2048]{2,1,0:T(8,128)(2,1)S(1)}, u32[]{:S(2)}, u32[]{:S(2)}) collective-permute-start(bf16[2,16,2048]{2,1,0:T(8,128)(2,1)} %add_convert_fusion.55), channel_id=1, source_target_pairs={{0,8},{8,16},{16,24},{1,9},{9,17},{17,25},{2,10},{10,18},{18,26},{... | collective-permute-start | bytes 393224 | tf_op jit(solution)/shard_map/ppermute | solution.py:628
  322.6 27.4 %collective-permute-start.69 = (bf16[2,128,512]{2,1,0:T(8,128)(2,1)}, bf16[2,128,512]{2,1,0:T(8,128)(2,1)S(1)}, u32[]{:S(2)}, u32[]{:S(2)}) collective-permute-start(bf16[2,128,512]{2,1,0:T(8,128)(2,1)} %get-tuple-element.556.refs_1_), channel_id=1, source_target_pairs={{0,8},{1,9},{2,10},{3,11},{4,12},{5,13},{6,14},{7,15}} | collective-permute-start | bytes 786440 | tf_op jit(solution)/shard_map/ppermute | solution.py:709
  385.1 400.9 %reduce-scatter.7.cloned.1.call-start = ((), (), s32[]{:S(2)}) async-start(), calls=%async_computation.6 | async-start | bytes 5242880 | tf_op jit(solution)/shard_map/reduce_scatter | solution.py:876
  450.9 25.2 %collective-permute-start.96 = (bf16[2,32,2048]{2,1,0:T(8,128)(2,1)}, bf16[2,32,2048]{2,1,0:T(8,128)(2,1)S(1)}, u32[]{:S(2)}, u32[]{:S(2)}) collective-permute-start(bf16[2,32,2048]{2,1,0:T(8,128)(2,1)} %get-tuple-element.605.refs_1_), channel_id=1, source_target_pairs={{0,1},{1,0},{2,3},{3,2},{4,5},{5,4},{6,7},{7,6},{8,9},{9,8},{10,11... | collective-permute-start | bytes 786440 | tf_op jit(solution)/shard_map/ppermute | solution.py:624
  452.2 24.0 %collective-permute-start.100 = (bf16[2,32,2048]{2,1,0:T(8,128)(2,1)S(1)}, bf16[2,32,2048]{2,1,0:T(8,128)(2,1)S(1)}, u32[]{:S(2)}, u32[]{:S(2)}) collective-permute-start(bf16[2,32,2048]{2,1,0:T(8,128)(2,1)S(1)} %collective-permute-done.99.refs_5_), channel_id=1, source_target_pairs={{0,1},{1,0},{2,3},{3,2},{4,5},{5,4},{6,7},{7,6},{8,9},{9,8},{10,11... | collective-permute-start | bytes 786440 | tf_op jit(solution)/shard_map/ppermute | solution.py:624
  452.3 23.9 %collective-permute-start.102 = (bf16[2,32,2048]{2,1,0:T(8,128)(2,1)S(1)}, bf16[2,32,2048]{2,1,0:T(8,128)(2,1)S(1)}, u32[]{:S(2)}, u32[]{:S(2)}) collective-permute-start(bf16[2,32,2048]{2,1,0:T(8,128)(2,1)S(1)} %collective-permute-done.101.refs_7_), channel_id=1, source_target_pairs={{0,1},{1,0},{2,3},{3,2},{4,5},{5,4},{6,7},{7,6},{8,9},{9,8},{10,11... | collective-permute-start | bytes 786440 | tf_op jit(solution)/shard_map/ppermute | solution.py:624
  452.7 23.5 %collective-permute-start.98 = (bf16[2,32,2048]{2,1,0:T(8,128)(2,1)S(1)}, bf16[2,32,2048]{2,1,0:T(8,128)(2,1)S(1)}, u32[]{:S(2)}, u32[]{:S(2)}) collective-permute-start(bf16[2,32,2048]{2,1,0:T(8,128)(2,1)S(1)} %collective-permute-done.97.refs_3_), channel_id=1, source_target_pairs={{0,1},{1,0},{2,3},{3,2},{4,5},{5,4},{6,7},{7,6},{8,9},{9,8},{10,11... | collective-permute-start | bytes 786440 | tf_op jit(solution)/shard_map/ppermute | solution.py:624
  626.8 261.1 %reduce-scatter.9.cloned.1.call-start = ((), (), s32[]{:S(2)}) async-start(), calls=%async_computation.7 | async-start | bytes 2621440 | tf_op jit(solution)/shard_map/reduce_scatter | solution.py:953
  631.7 27.9 %collective-permute-start.140 = (bf16[2,128,512]{2,1,0:T(8,128)(2,1)}, bf16[2,128,512]{2,1,0:T(8,128)(2,1)S(1)}, u32[]{:S(2)}, u32[]{:S(2)}) collective-permute-start(bf16[2,128,512]{2,1,0:T(8,128)(2,1)} %get-tuple-element.690), channel_id=1, source_target_pairs={{16,8},{17,9},{18,10},{19,11},{20,12},{21,13},{22,14},{23,15}} | collective-permute-start | bytes 786440 | tf_op jit(solution)/shard_map/ppermute | solution.py:718
  635.5 46.5 %collective-permute-start.142 = (bf16[2,128,512]{2,1,0:T(8,128)(2,1)}, bf16[2,128,512]{2,1,0:T(8,128)(2,1)S(1)}, u32[]{:S(2)}, u32[]{:S(2)}) collective-permute-start(bf16[2,128,512]{2,1,0:T(8,128)(2,1)} %get-tuple-element.696), channel_id=1, source_target_pairs={{16,8},{17,9},{18,10},{19,11},{20,12},{21,13},{22,14},{23,15}} | collective-permute-start | bytes 786440 | tf_op jit(solution)/shard_map/ppermute | solution.py:718
  662.0 30.5 %collective-permute-start.141 = (bf16[2,128,512]{2,1,0:T(8,128)(2,1)}, bf16[2,128,512]{2,1,0:T(8,128)(2,1)S(1)}, u32[]{:S(2)}, u32[]{:S(2)}) collective-permute-start(bf16[2,128,512]{2,1,0:T(8,128)(2,1)} %get-tuple-element.692), channel_id=1, source_target_pairs={{8,0},{9,1},{10,2},{11,3},{12,4},{13,5},{14,6},{15,7}} | collective-permute-start | bytes 786440 | tf_op jit(solution)/shard_map/ppermute | solution.py:718
  684.5 24.3 %collective-permute-start.144 = (bf16[2,128,512]{2,1,0:T(8,128)(2,1)}, bf16[2,128,512]{2,1,0:T(8,128)(2,1)S(1)}, u32[]{:S(2)}, u32[]{:S(2)}) collective-permute-start(bf16[2,128,512]{2,1,0:T(8,128)(2,1)} %get-tuple-element.707), channel_id=1, source_target_pairs={{8,0},{9,1},{10,2},{11,3},{12,4},{13,5},{14,6},{15,7}} | collective-permute-start | bytes 786440 | tf_op jit(solution)/shard_map/ppermute | solution.py:718
  725.8 24.8 %collective-permute-start.150 = (bf16[2,32,2048]{2,1,0:T(8,128)(2,1)}, bf16[2,32,2048]{2,1,0:T(8,128)(2,1)S(1)}, u32[]{:S(2)}, u32[]{:S(2)}) collective-permute-start(bf16[2,32,2048]{2,1,0:T(8,128)(2,1)} %get-tuple-element.717), channel_id=1, source_target_pairs={{0,1},{1,0},{2,3},{3,2},{4,5},{5,4},{6,7},{7,6},{8,9},{9,8},{10,11... | collective-permute-start | bytes 786440 | tf_op jit(solution)/shard_map/ppermute | solution.py:624
  750.6 239.2 %reduce-scatter.11.cloned.1.call-start = ((), (), s32[]{:S(2)}) async-start(), calls=%async_computation.8 | async-start | bytes 5242880 | tf_op jit(solution)/shard_map/reduce_scatter | solution.py:876
  829.8 228.2 %reduce-scatter.13.cloned.1.call-start = ((), (), s32[]{:S(2)}) async-start(), calls=%async_computation.9 | async-start | bytes 2621440 | tf_op jit(solution)/shard_map/reduce_scatter | solution.py:953
  834.6 27.0 %collective-permute-start.176 = (bf16[2,128,512]{2,1,0:T(8,128)(2,1)}, bf16[2,128,512]{2,1,0:T(8,128)(2,1)S(1)}, u32[]{:S(2)}, u32[]{:S(2)}) collective-permute-start(bf16[2,128,512]{2,1,0:T(8,128)(2,1)} %get-tuple-element.768), channel_id=1, source_target_pairs={{16,8},{17,9},{18,10},{19,11},{20,12},{21,13},{22,14},{23,15}} | collective-permute-start | bytes 786440 | tf_op jit(solution)/shard_map/ppermute | solution.py:718
  838.4 45.7 %collective-permute-start.178 = (bf16[2,128,512]{2,1,0:T(8,128)(2,1)}, bf16[2,128,512]{2,1,0:T(8,128)(2,1)S(1)}, u32[]{:S(2)}, u32[]{:S(2)}) collective-permute-start(bf16[2,128,512]{2,1,0:T(8,128)(2,1)} %get-tuple-element.774), channel_id=1, source_target_pairs={{16,8},{17,9},{18,10},{19,11},{20,12},{21,13},{22,14},{23,15}} | collective-permute-start | bytes 786440 | tf_op jit(solution)/shard_map/ppermute | solution.py:718
  864.1 30.5 %collective-permute-start.177 = (bf16[2,128,512]{2,1,0:T(8,128)(2,1)}, bf16[2,128,512]{2,1,0:T(8,128)(2,1)S(1)}, u32[]{:S(2)}, u32[]{:S(2)}) collective-permute-start(bf16[2,128,512]{2,1,0:T(8,128)(2,1)} %get-tuple-element.770), channel_id=1, source_target_pairs={{8,0},{9,1},{10,2},{11,3},{12,4},{13,5},{14,6},{15,7}} | collective-permute-start | bytes 786440 | tf_op jit(solution)/shard_map/ppermute | solution.py:718
  886.6 24.2 %collective-permute-start.180 = (bf16[2,128,512]{2,1,0:T(8,128)(2,1)}, bf16[2,128,512]{2,1,0:T(8,128)(2,1)S(1)}, u32[]{:S(2)}, u32[]{:S(2)}) collective-permute-start(bf16[2,128,512]{2,1,0:T(8,128)(2,1)} %get-tuple-element.786), channel_id=1, source_target_pairs={{8,0},{9,1},{10,2},{11,3},{12,4},{13,5},{14,6},{15,7}} | collective-permute-start | bytes 786440 | tf_op jit(solution)/shard_map/ppermute | solution.py:718
  927.7 26.7 %collective-permute-start.186 = (bf16[2,32,2048]{2,1,0:T(8,128)(2,1)}, bf16[2,32,2048]{2,1,0:T(8,128)(2,1)S(1)}, u32[]{:S(2)}, u32[]{:S(2)}) collective-permute-start(bf16[2,32,2048]{2,1,0:T(8,128)(2,1)} %get-tuple-element.796), channel_id=1, source_target_pairs={{0,1},{1,0},{2,3},{3,2},{4,5},{5,4},{6,7},{7,6},{8,9},{9,8},{10,11... | collective-permute-start | bytes 786440 | tf_op jit(solution)/shard_map/ppermute | solution.py:624
  954.4 323.1 %reduce-scatter.17.cloned.1.call-start = ((), (), s32[]{:S(2)}) async-start(), calls=%async_computation.11 | async-start | bytes 2621440 | tf_op jit(solution)/shard_map/reduce_scatter | solution.py:953
  1110.3 170.2 %reduce-scatter.15.cloned.1.call-start = ((), (), s32[]{:S(2)}) async-start(), calls=%async_computation.10 | async-start | bytes 5242880 | tf_op jit(solution)/shard_map/reduce_scatter | solution.py:876
  1146.3 50.0 %collective-permute-start.238 = (bf16[4,3,64,256]{3,2,0,1:T(8,128)(2,1)S(1)}, bf16[4,3,64,256]{3,2,0,1:T(8,128)(2,1)S(1)}, u32[]{:S(2)}, u32[]{:S(2)}) collective-permute-start(bf16[4,3,64,256]{3,2,0,1:T(8,128)(2,1)S(1)} %pad_maximum_fusion.5), channel_id=1, source_target_pairs={{0,1},{1,0},{2,3},{3,2},{4,5},{5,4},{6,7},{7,6},{8,9},{9,8},{10,11... | collective-permute-start | bytes 1179656 | tf_op jit(solution)/shard_map/ppermute | solution.py:624
  1147.0 49.4 %collective-permute-start.240 = (bf16[4,3,64,256]{3,2,0,1:T(8,128)(2,1)S(1)}, bf16[4,3,64,256]{3,2,0,1:T(8,128)(2,1)S(1)}, u32[]{:S(2)}, u32[]{:S(2)}) collective-permute-start(bf16[4,3,64,256]{3,2,0,1:T(8,128)(2,1)S(1)} %add_convert_fusion.2), channel_id=1, source_target_pairs={{0,2},{1,3},{2,0},{3,1},{4,6},{5,7},{6,4},{7,5},{8,10},{9,11},{10,... | collective-permute-start | bytes 1179656 | tf_op jit(solution)/shard_map/ppermute | solution.py:624
  1164.8 24.4 %collective-permute-start.234 = (f32[3,7168]{1,0:T(4,128)S(1)}, f32[3,7168]{1,0:T(4,128)S(1)}, u32[]{:S(2)}, u32[]{:S(2)}) collective-permute-start(f32[3,7168]{1,0:T(4,128)S(1)} %pad_maximum_fusion.10), channel_id=1, source_target_pairs={{0,24},{8,0},{16,8},{24,16},{1,25},{9,1},{17,9},{25,17},{2,26},{10... | collective-permute-start | bytes 258056 | tf_op jit(solution)/shard_map/ppermute | solution.py:628
  1169.2 27.2 %collective-permute-start.242 = (bf16[4,3,64,256]{3,2,0,1:T(8,128)(2,1)S(1)}, bf16[4,3,64,256]{3,2,0,1:T(8,128)(2,1)S(1)}, u32[]{:S(2)}, u32[]{:S(2)}) collective-permute-start(bf16[4,3,64,256]{3,2,0,1:T(8,128)(2,1)S(1)} %add_convert_fusion.1), channel_id=1, source_target_pairs={{0,4},{1,5},{2,6},{3,7},{4,0},{5,1},{6,2},{7,3},{8,12},{9,13},{10,... | collective-permute-start | bytes 1179656 | tf_op jit(solution)/shard_map/ppermute | solution.py:624
  1197.7 55.6 %collective-permute-start.246 = (f32[288,256]{1,0:T(8,128)}, f32[288,256]{1,0:T(8,128)S(1)}, u32[]{:S(2)}, u32[]{:S(2)}) collective-permute-start(f32[288,256]{1,0:T(8,128)} %get-tuple-element.1016), channel_id=1, source_target_pairs={{0,16},{8,24},{16,0},{24,8},{1,17},{9,25},{17,1},{25,9},{2,18},{10... | collective-permute-start | bytes 884744 | tf_op jit(solution)/shard_map/ppermute | solution.py:628
  1200.1 59.5 %collective-permute-start.247 = (f32[288,256]{1,0:T(8,128)}, f32[288,256]{1,0:T(8,128)S(1)}, u32[]{:S(2)}, u32[]{:S(2)}) collective-permute-start(f32[288,256]{1,0:T(8,128)} %get-tuple-element.1017), channel_id=1, source_target_pairs={{0,24},{8,0},{16,8},{24,16},{1,25},{9,1},{17,9},{25,17},{2,26},{10... | collective-permute-start | bytes 884744 | tf_op jit(solution)/shard_map/ppermute | solution.py:628
  (519 other events, 4447.4 us)
Sparse Core Ops, SparseCore 0:
  10.2 55.5 all-gather.10
  67.3 91.2 all-gather.12
  160.2 81.5 all-gather.14
  243.2 92.3 all-gather.16
  385.3 80.1 all-gather.18
  627.0 86.5 reduce-scatter.6
  750.7 40.9 reduce-scatter.8
  829.9 87.7 reduce-scatter.10
  954.5 40.0 reduce-scatter.12
  1110.4 42.9 reduce-scatter.16
  1155.7 113.7 reduce-scatter.14

commit v2 on v1

--- a/solution.py
+++ b/solution.py
@@ -11,11 +11,15 @@
 BF = jnp.bfloat16
 EPSILON = 1e-05
 LANES = 128
-HALO = 16
+HALO = 8
+RIM = 4
+FADES = 16
 NN = ((1,), (0,))
 NT = ((1,), (1,))
 TN = ((0,), (0,))
-GROUPS = 2
+GROUPS = 1
+EARLY_AT = ("state_back", 1)
+LATE_AT = ("spread", 1)
 VMEM_BYTES = 56 * 1024 * 1024
 
 
@@ -49,7 +53,14 @@
     def __init__(self):
         self.last = ()
 
-    def call(self, body, grid, ins, in_specs, outs, out_specs, scratch=(), name=None, after=()):
+    def hand_on(self, arrays, after=()):
+        shapes = [sds(a.shape, a.dtype) for a in arrays]
+        return self.call(
+            lambda *refs: None, 1, arrays, [anywhere()] * len(arrays), shapes, [anywhere()] * len(arrays),
+            name="hand_on", after=after, aliases={i: i for i in range(len(arrays))},
+        )
+
+    def call(self, body, grid, ins, in_specs, outs, out_specs, scratch=(), name=None, after=(), aliases={}):
         waits = tuple(self.last) + tuple(after)
         count, extra = len(ins), len(waits)
         made = len(outs)
@@ -68,6 +79,7 @@
             scratch_shapes=list(scratch),
             compiler_params=pltpu.CompilerParams(vmem_limit_bytes=VMEM_BYTES),
             cost_estimate=pl.CostEstimate(flops=1, bytes_accessed=1, transcendentals=0),
+            input_output_aliases=aliases,
             name=name,
         )(*ins, *waits)
         self.last = (token,)
@@ -219,22 +231,17 @@
 
 
 def collect_body(n, nh, info, *refs):
-    pieces, steps = refs[:nh], refs[nh : nh + n]
-    shared_out, step_out = refs[nh + n :]
-    here, place = info[0], info[1]
+    pieces, steps = refs[:nh], refs[nh]
+    shared_out, step_out = refs[nh + 1 :]
+    step_out[...] = jnp.zeros_like(step_out)
+    rows, wide = steps.shape[2:]
     for k in range(nh):
-        owner = here ^ k
         for s in range(n):
-            source = lax.rem(place - s + n, n)
             for layer in range(shared_out.shape[0]):
-                shared_out[layer, source, owner] = pieces[k][s, layer]
-    step_out[...] = jnp.zeros_like(step_out)
-    rows = steps[0].shape[1]
+                shared_out[layer, s, info[0] ^ k] = pieces[k][s, layer]
     for s in range(n):
-        source = lax.rem(place - s + n, n)
-        wide = steps[s].shape[2]
         for layer in range(step_out.shape[0]):
-            step_out[layer, 0:rows, pl.ds(pl.multiple_of(source * wide, wide), wide)] = steps[s][layer]
+            step_out[layer, 0:rows, s * wide : (s + 1) * wide] = steps[s, layer]
 
 
 def project_body(nh, channels, info, *refs):
@@ -267,8 +274,7 @@
 
 def local_body(
     channels, size, taps, info, lengths, feed, raw, x_halo, w_x, w_bc, conv_w, head_params,
-    chan, values_out, shared_out, rise_out, step_out, local_out, state_out, fade_out, halo_out,
-    ext, halo_all,
+    values_out, shared_out, rise_out, step_out, state_out, halo_out, ext, halo_all,
 ):
     seq = pl.program_id(0)
     length = feed.shape[1]
@@ -276,10 +282,14 @@
 
     @pl.when(seq == 0)
     def _():
-        halo_all[:, :channels] = mm(x_halo[...], flat_rows(w_x))
-        halo_all[:, channels:] = mm(x_halo[...], w_bc[...])
-
-    rim = halo_all[pl.ds(pl.multiple_of(seq * HALO, HALO), HALO), :]
+        wide = mm(x_halo[...], flat_rows(w_x))
+        narrow = mm(x_halo[...], w_bc[...])
+        for m in range(halo_all.shape[0]):
+            rows = slice(m * RIM, (m + 1) * RIM)
+            halo_all[m, HALO - RIM :, :channels] = wide[rows]
+            halo_all[m, HALO - RIM :, channels:] = narrow[rows]
+
+    rim = halo_all[seq]
     halo_out[0] = rim
     ext[:HALO] = rim
     ext[HALO:] = feed[0]
@@ -293,7 +303,6 @@
     shared_out[0] = low[:, channels:]
     values = low[:, :channels].astype(F32)
     keys = low[:, channels : channels + state]
-    queries = low[:, channels + state :]
     params = head_params[...]
     step = rates_of(raw[0], params) * valid
     rise = running_sum(jnp.exp(params[1:2]) * step, channels // size)
@@ -302,10 +311,18 @@
     closing = rise[length - 1 :, :]
     weight = jnp.exp(rise - closing) * step
     weighted = (expand(weight, channels, size) * values).astype(BF)
-    state_out[0] = mm(keys, weighted, TN).astype(BF)
-    fade_out[0] = expand(jnp.broadcast_to(jnp.exp(-closing), (8, LANES)), channels, size)
+    fade = expand(jnp.broadcast_to(jnp.exp(-closing), (FADES, LANES)), channels, size)
+    put_state(state_out, mm(keys, weighted, TN), fade)
+
+
+def mix_body(size, values, shared, rise_in, step, chan, local_out):
+    length, channels = values.shape[1:]
+    state = shared.shape[2] // 2
+    keys, queries = shared[0, :, :state], shared[0, :, state:]
+    wide = values[0].astype(F32)
+    rise = rise_in[0]
     scores = mm(queries, keys, NT)
-    stepped = (values * expand(step, channels, size)).astype(BF)
+    stepped = (wide * expand(step[0], channels, size)).astype(BF)
     rise_rows = jnp.transpose(rise)
     half = length // 2
     group = LANES // size
@@ -321,20 +338,47 @@
             lower = lower + mm((scores[half:, :half] * left).astype(BF), part[:half])
             lower = lower + mm((scores[half:, half:] * right).astype(BF), part[half:])
         at = slice(pair * LANES, (pair + 1) * LANES)
-        skipped = chan[1:2, at] * values[:, at]
+        skipped = chan[1:2, at] * wide[:, at]
         local_out[0, :half, at] = upper + skipped[:half]
         local_out[0, half:, at] = lower + skipped[half:]
 
 
-def hop_body(arrived, own, fade, out):
-    out[0] = (fade[0, 0:1] * arrived[0].astype(F32) + own[0].astype(F32)).astype(BF)
-
-
-def received(parts):
-    summed = parts[0][0]
-    for part in parts[1:]:
-        summed = summed + part[0]
-    return summed
+def put_state(out, made, fade=None):
+    state, narrow = made.shape[0], out.shape[3]
+    if fade is not None:
+        high, low = split_two(fade)
+        odd = lax.broadcasted_iota(jnp.int32, fade.shape, 0) % 2
+        fade = jnp.where(odd == 0, high.astype(F32), low.astype(F32)).astype(BF)
+    for j in range(out.shape[0]):
+        at = slice(j * narrow, (j + 1) * narrow)
+        out[j, 0, :state] = made[:, at].astype(BF)
+        if fade is not None:
+            out[j, 0, state:] = fade[:, at]
+
+
+def get_state(part):
+    pieces = [part[j, 0] for j in range(part.shape[0])]
+    return pieces[0] if len(pieces) == 1 else jnp.concatenate(pieces, axis=1)
+
+
+def chain_body(parts, carried, fades):
+    state = carried.shape[2]
+    for item in range(parts.shape[1]):
+        running = jnp.zeros(carried.shape[2:], F32)
+        for block in range(parts.shape[0]):
+            carried[block, item] = running.astype(BF)
+            rows = parts[block, item, state:].astype(F32)
+            fade = rows[0:1] + rows[1:2]
+            fades[block, item] = jnp.broadcast_to(fade, fades.shape[2:])
+            running = fade * running + parts[block, item, :state].astype(F32)
+
+
+def chain_back_body(parts, fades, carried):
+    for item in range(parts.shape[1]):
+        running = jnp.zeros(carried.shape[2:], F32)
+        for block in range(parts.shape[0] - 1, -1, -1):
+            carried[block, item] = running.astype(BF)
+            running = fades[block, item, 0:1] * running + parts[block, item].astype(F32)
 
 
 def scatter_rows(info, outs, table, own):
@@ -344,12 +388,11 @@
 
 
 def output_body(
-    n, nh, size, info, local, gate, shared, rise, w_out, chan, *refs
+    n, nh, size, info, local, gate, shared, rise, w_out, chan, arrived, *rest
 ):
-    parts, rest = refs[: n - 1], refs[n - 1 :]
     full_out, carried_out = rest[:2]
     outs, table = rest[2 : 2 + nh], rest[2 + nh]
-    carried = received(parts)
+    carried = get_state(arrived)
     carried_out[0] = carried
     length, channels = local.shape[1:]
     state = shared.shape[2] // 2
@@ -403,7 +446,7 @@
     state = shared.shape[2] // 2
     queries = shared[0, :, state:]
     spread = (d_full * expand(jnp.exp(-rise[0]), channels, size)).astype(BF)
-    state_out[0] = mm(queries, spread, TN).astype(BF)
+    put_state(state_out, mm(queries, spread, TN))
 
     @pl.when(seq == 0)
     def _():
@@ -466,13 +509,12 @@
 
 
 def state_back_body(
-    n, channels, size, taps, info, lengths, feed, raw, rim, values, shared, rise, step, carried,
-    d_values_in, d_shared_in, rates, conv_w, head_params, *refs
+    channels, size, taps, info, lengths, feed, raw, rim, values, shared, rise, step, carried,
+    d_values_in, d_shared_in, rates, conv_w, head_params, arrived, *rest
 ):
-    parts, rest = refs[: n - 1], refs[n - 1 :]
     d_pre_out, first_out, d_raw_out, conv_out, head_out, ext = rest
     seq = pl.program_id(0)
-    after = received(parts)
+    after = get_state(arrived)
     length = feed.shape[1]
     state = shared.shape[2] // 2
     keys = shared[0, :, :state]
@@ -584,12 +626,7 @@
     pieces, out = refs[:nh], refs[nh]
     for k in range(nh):
         for layer in range(out.shape[0]):
-            out[layer, info[0] ^ k] = pieces[k][layer]
-
-
-def gather_plan(layers):
-    order = [(kind, layer) for layer in range(layers) for kind in ("x", "z", "o")]
-    return [order[:1]] + [order[at : at + 2] for at in range(1, len(order), 2)]
+            out[layer, info[0] ^ k] = pieces[k][layer].astype(F32)
 
 
 def shards(
@@ -612,6 +649,8 @@
     while batches % groups:
         groups //= 2
     part = batches // groups
+    factor, per = max(1, n // part), max(1, part // n)
+    narrow = channels // factor
     tokens = part * length
     here, place = lax.axis_index("heads"), lax.axis_index("seq")
     every = range(groups)
@@ -652,16 +691,29 @@
     def in_order(parts):
         return jnp.roll(jnp.stack(parts[::-1]), place + 1, axis=0)
 
+    rows_here = depth // nh
+    share = lax.dynamic_slice_in_dim(w_bc, here * rows_here, rows_here, 1)
+    step_rows = jnp.pad(w_dt.transpose(0, 2, 1), ((0, 0), (0, -heads_here % 16), (0, 0)))
+    small = jnp.concatenate([share.reshape(-1, channels), step_rows.reshape(-1, channels)], axis=0)
+    share_rows = share.size // channels
     weights = {}
-    for batch in gather_plan(layers):
-        sources = [{"x": w_x, "z": w_z, "o": w_out}[kind][layer] for kind, layer in batch]
-        table = lax.all_gather(jnp.stack(sources), "seq", axis=0)
-        for at, key in enumerate(batch):
+
+    def fetch(*keys, after=None):
+        sources = [{"x": w_x, "z": w_z, "o": w_out}[kind][layer] for kind, layer in keys]
+        table = sources[0][None] if len(sources) == 1 else jnp.stack(sources)
+        if not weights:
+            table = jnp.concatenate([table, small.reshape(1, -1, channels)], axis=1)
+        if after is not None:
+            (table,) = line.hand_on([table], after)
+        table = lax.all_gather(table, "seq", axis=0)
+        for at, key in enumerate(keys):
             weights[key] = (table, at)
 
+    fetch(("x", 0))
+    fetch(("z", 0), ("o", 0))
+
     def weight_spec(table, at):
-        rank = len(table.shape)
-        return pl.BlockSpec((table.shape[0], 1) + tuple(table.shape[2:]), lambda i: (0, at) + (0,) * (rank - 2))
+        return pl.BlockSpec((n, 1, depth, channels), lambda i: (0, at, 0, 0))
 
     gains = in_order(gather_seq(norm_gain)).transpose(1, 0, 2).reshape(layers, 1, width).astype(F32)
     x_res = [hidden_in[:, g * part : (g + 1) * part].transpose(1, 0, 2).astype(F32) for g in every]
@@ -672,14 +724,11 @@
             first_norm_body, part, [x_res[g], gains[0]], [per_seq(x_res[g]), whole(gains[0])], outs,
             [per_seq(outs[0])], name="first_norm",
         )
-    rows_here = depth // nh
-    share = lax.dynamic_slice_in_dim(w_bc, here * rows_here, rows_here, 1)
-    share = jnp.stack(gather_seq(share))
-    step_rows = jnp.pad(w_dt.transpose(0, 2, 1), ((0, 0), (0, -heads_here % 16), (0, 0)))
-    shared_pieces = gather_heads(share)
-    step_pieces = gather_seq(step_rows)
+    small = weights["x", 0][0][:, 0, depth:]
+    shared_pieces = gather_heads(small[:, :share_rows].reshape(n, layers, rows_here, both))
+    step_pieces = small[:, share_rows:].reshape(n, layers, -1, depth)
     collected = [sds((layers, n, nh, rows_here, both), BF), sds((layers, LANES, width), BF)]
-    ins = [infos[0]] + shared_pieces + step_pieces
+    ins = [infos[0]] + shared_pieces + [step_pieces]
     shared_w, step_w = call(
         functools.partial(collect_body, n, nh), 1, ins, [smem()] + [whole(a) for a in ins[1:]],
         collected, [whole(a) for a in collected], name="collect",
@@ -702,26 +751,17 @@
         [y_gain, jnp.repeat(d_skip, size, axis=1)] + [jnp.zeros((layers, channels), F32)] * 6, axis=1
     )
 
-    state_shape = sds((part, state, channels), BF)
-
-    def first_hop(states, back):
-        pair = (n - 1, n - 2) if back else (0, 1)
-        return [lax.ppermute(states, "seq", [pair])]
-
-    def next_hop(arrived, states, fade, back):
-        at = len(arrived)
-        ins = [arrived[-1], states, fade]
-        (out,) = call(
-            hop_body, part, ins, [per_seq(a) for a in ins], [state_shape], [per_seq(state_shape)], name="hop"
-        )
-        pair = (n - 1 - at, n - 2 - at) if back else (at, at + 1)
-        arrived.append(lax.ppermute(out, "seq", [pair]))
+    state_shape = sds((n, per, state, narrow), BF)
+    state_spec = lambda rows: pl.BlockSpec((factor, 1, rows, narrow), lambda i: (i // per, i % per, 0, 0))
+
+    def turn(states):
+        return lax.all_to_all(states, "seq", 0, 0)
 
     def rim_of(pieces):
         rows = sum(
-            jnp.where((here ^ k) == nh - 1, pieces[k][:, own - HALO :].astype(F32), 0.0) for k in range(nh)
+            jnp.where((here ^ k) == nh - 1, pieces[k][:, own - RIM :].astype(F32), 0.0) for k in range(nh)
         ).astype(BF)
-        return along(rows, 1, lambda i, j: j == i + 1).reshape(part * HALO, width)
+        return along(rows.reshape(part * RIM, width), 1, lambda i, j: j == i + 1)
 
     stored = []
     for layer in range(layers):
@@ -746,30 +786,37 @@
                 outs, [per_seq(a) for a in outs],
                 name="project",
             )
-            ins = [infos[g], spans[g], it["feed"], it["raw"], x_halo, w_x_full[0], wbc_full, conv_w, head_params, chan]
+            ins = [infos[g], spans[g], it["feed"], it["raw"], x_halo, w_x_full[0], wbc_full, conv_w, head_params]
             outs = [
                 sds((part, length, channels), BF),
                 sds((part, length, both), BF),
                 sds((part, length, LANES), F32),
                 sds((part, length, LANES), F32),
-                sds((part, length, channels), F32),
-                state_shape,
-                sds((part, 8, channels), F32),
+                sds((n, per, state + FADES, narrow), BF),
                 sds((part, HALO, feed_width), F32),
             ]
             specs = [per_seq(a) for a in outs]
-            it["values"], it["shared"], it["rise"], it["step"], local[g], states[g], it["fade"], it["rim"] = call(
+            specs[4] = state_spec(state + FADES)
+            it["values"], it["shared"], it["rise"], it["step"], states[g], it["rim"] = call(
                 functools.partial(local_body, channels, size, taps), part, ins,
                 [smem(), smem(), per_seq(ins[2]), per_seq(ins[3]), whole(x_halo), weight_spec(*w_x_full)]
                 + [whole(a) for a in ins[6:]],
                 outs, specs,
                 scratch=[
                     pltpu.VMEM((HALO + length, feed_width), F32),
-                    pltpu.VMEM((part * HALO, feed_width), F32),
+                    pltpu.VMEM((part, HALO, feed_width), F32),
                 ],
                 name="local",
             )
-            arrived[g] = first_hop(states[g], False)
+            arrived[g] = turn(states[g])
+        for g in every:
+            it = saved[g]
+            ins = [it[k] for k in ("values", "shared", "rise", "step")] + [chan]
+            outs = [sds((part, length, channels), F32)]
+            (local[g],) = call(
+                functools.partial(mix_body, size), part, ins, [per_seq(a) for a in ins[:-1]] + [whole(chan)],
+                outs, [per_seq(outs[0])], name="mix",
+            )
 
         def gate(g):
             it = saved[g]
@@ -779,27 +826,27 @@
                 outs, [per_seq(outs[0])], name="gate",
             )
 
-        def all_hops(fillers):
-            for at in range(1, n - 1):
-                for g in every:
-                    next_hop(arrived[g], states[g], saved[g]["fade"], False)
-                if fillers:
-                    fillers.pop(0)()
-            for filler in fillers:
-                filler()
-
-        all_hops([functools.partial(gate, g) for g in every])
+        for g in every:
+            outs = [state_shape, sds((n, per, 8, narrow), F32)]
+            made, saved[g]["fades"] = call(
+                chain_body, 1, [arrived[g]], [whole(arrived[g])], outs, [whole(a) for a in outs], name="chain"
+            )
+            arrived[g] = turn(made)
+        for g in every:
+            gate(g)
+        if layer + 1 < layers:
+            fetch(("x", layer + 1), ("z", layer + 1), after=arrived)
+            fetch(("o", layer + 1), after=arrived)
         summed = [None] * groups
         for g in every:
             it = saved[g]
-            ins = [infos[g], local[g], it["gate"], it["shared"], it["rise"], w_o_full[0], chan] + arrived[g]
+            ins = [infos[g], local[g], it["gate"], it["shared"], it["rise"], w_o_full[0], chan, arrived[g]]
             outs = [sds((part, length, channels), F32), sds((part, state, channels), BF)] + [
                 sds((part, own, width + LANES), BF)
             ] * nh
             it["full"], it["carried"], *projected = call(
                 functools.partial(output_body, n, nh, size), part, ins,
-                [smem()] + [per_seq(a) for a in ins[1:5]] + [weight_spec(*w_o_full), whole(chan)]
-                + [per_seq(a) for a in ins[7:]],
+                [smem()] + [per_seq(a) for a in ins[1:5]] + [weight_spec(*w_o_full), whole(chan), state_spec(state)],
                 outs, [per_seq(a) for a in outs],
                 scratch=[pltpu.VMEM((length, width + LANES), F32)],
                 name="output",
@@ -836,6 +883,14 @@
     flat = lambda a: a.reshape(tokens, a.shape[2])
     cut = pl.BlockSpec((tokens, depth), lambda i: (0, i))
     early_grads, late_grads = [None] * layers, [None] * layers
+
+    def tied(layer, kernel):
+        found = []
+        for grads, (where, later) in ((early_grads, EARLY_AT), (late_grads, LATE_AT)):
+            if where == kernel and 0 <= layer + later < layers and grads[layer + later] is not None:
+                found.append(grads[layer + later])
+        return found
+
     shared_grads, small_grads = [None] * layers, [None] * layers
     for layer in reversed(range(layers)):
         conv_w, head_params, chan = conv_all[layer], head_all[layer], chan_all[layer]
@@ -856,24 +911,29 @@
                 state_shape,
                 sds((8, channels), F32),
             ]
-            specs = [per_seq(a) for a in outs[:5]] + [whole(outs[5])]
+            specs = [per_seq(a) for a in outs[:4]] + [state_spec(state), whole(outs[5])]
             to["grad"], to["d_gate"], to["normal"], to["d_full"], states[g], to["chan"] = call(
                 functools.partial(gate_back_body, n, nh, size, total), part, ins,
                 [smem()] + [per_seq(a) for a in ins[1:6]] + [weight_spec(*w_o_full), whole(chan)]
                 + [per_seq(a) for a in pieces],
                 outs, specs, scratch=[pltpu.VMEM((length, LANES), F32)],
-                name="gate_back",
-            )
-            arrived[g] = first_hop(states[g], True)
-        ins = [flat(to["normal"]) for to in work] + [flat(to["grad"]) for to in work]
-        ins += [flat(it["x_all"]) for it in saved] + [flat(to["d_gate"]) for to in work]
-        outs = [sds((n, 2, depth, channels), BF)]
-        (early,) = call(
-            functools.partial(weight_body, groups), n, ins,
-            [whole(a) for a in ins[:groups]] + [cut] * (2 * groups) + [whole(a) for a in ins[3 * groups :]],
-            outs, [per_seq(outs[0])], name="early_weights",
-        )
-        early_grads[layer] = lax.psum_scatter(early, "seq", scatter_dimension=0, tiled=False)
+                name="gate_back", after=tied(layer, "gate_back"),
+            )
+            arrived[g] = turn(states[g])
+        def early_weights():
+            ins = [flat(to["normal"]) for to in work] + [flat(to["grad"]) for to in work]
+            ins += [flat(it["x_all"]) for it in saved] + [flat(to["d_gate"]) for to in work]
+            outs = [sds((n, 2, depth, channels), BF)]
+            (early,) = call(
+                functools.partial(weight_body, groups), n, ins,
+                [whole(a) for a in ins[:groups]] + [cut] * (2 * groups) + [whole(a) for a in ins[3 * groups :]],
+                outs, [per_seq(outs[0])], name="early_weights",
+            )
+            return early
+
+        def send_early(early, after=()):
+            (held,) = line.hand_on([early], after)
+            early_grads[layer] = lax.psum_scatter(held, "seq", scatter_dimension=0, tiled=False)
 
         def mix_back(g):
             it, to = saved[g], work[g]
@@ -886,15 +946,14 @@
             to["d_values"], to["d_shared"], to["d_rates"] = call(
                 functools.partial(mix_back_body, size), part, ins,
                 [per_seq(a) for a in ins[:-1]] + [whole(chan)], outs, [per_seq(a) for a in outs],
-                name="mix_back",
-                after=[late_grads[layer + 1]] if layer + 1 < layers and g == groups - 1 else [],
+                name="mix_back", after=tied(layer, "mix_back"),
             )
 
         def state_back(g):
             it, to = saved[g], work[g]
             ins = [infos[g], spans[g]]
             ins += [it[k] for k in ("feed", "raw", "rim", "values", "shared", "rise", "step", "carried")]
-            ins += [to["d_values"], to["d_shared"], to["d_rates"], conv_w, head_params] + arrived[g]
+            ins += [to["d_values"], to["d_shared"], to["d_rates"], conv_w, head_params, arrived[g]]
             outs = [
                 sds((part, length, feed_width), F32),
                 sds((part, 8, feed_width), F32),
@@ -903,12 +962,11 @@
                 sds((8, LANES), F32),
             ]
             to["d_pre"], first_rows, to["d_raw"], to["conv"], to["head"] = call(
-                functools.partial(state_back_body, n, channels, size, taps), part, ins,
-                [smem(), smem()] + [per_seq(a) for a in ins[2:13]] + [whole(conv_w), whole(head_params)]
-                + [per_seq(a) for a in ins[15:]],
+                functools.partial(state_back_body, channels, size, taps), part, ins,
+                [smem(), smem()] + [per_seq(a) for a in ins[2:13]] + [whole(conv_w), whole(head_params), state_spec(state)],
                 outs, [per_seq(a) for a in outs[:3]] + [whole(a) for a in outs[3:]],
                 scratch=[pltpu.VMEM((HALO + length, feed_width), F32)],
-                name="state_back",
+                name="state_back", after=tied(layer, "state_back"),
             )
             to["next"] = along(first_rows, -1, lambda i, j: j == i - 1)
 
@@ -923,34 +981,51 @@
                 + [whole(a) for a in ins[7:]],
                 outs, [per_seq(a) for a in outs],
                 scratch=[pltpu.VMEM((length + 8, feed_width), F32), pltpu.VMEM((length, width), F32)],
-                name="spread",
+                name="spread", after=tied(layer, "spread"),
             )
             to["summed"] = scatter_heads(pieces)
 
-        def all_hops_back(fillers):
-            for at in range(1, n - 1):
-                for g in every:
-                    next_hop(arrived[g], states[g], saved[g]["fade"], True)
-                if fillers:
-                    fillers.pop(0)()
-            for filler in fillers:
-                filler()
-
-        all_hops_back([functools.partial(mix_back, g) for g in every])
+        early = early_weights()
+        for g in every:
+            fades = saved[g]["fades"]
+            (made,) = call(
+                chain_back_body, 1, [arrived[g], fades], [whole(arrived[g]), whole(fades)], [state_shape],
+                [whole(state_shape)], name="chain_back",
+            )
+            arrived[g] = turn(made)
+        for g in every:
+            mix_back(g)
+        send_early(early, arrived)
         for g in every:
             state_back(g)
         for g in every:
             spread(g)
-        ins = [infos[0]] + [flat(it["x_all"]) for it in saved]
-        ins += [flat(to["d_feed"]) for to in work] + [flat(to["d_raw"]) for to in work]
-        outs = [sds((n, depth, channels), BF), sds((n, 16, depth), F32)] + [sds((n, rows_here, both), BF)] * nh
-        d_wx, d_wdt, *shared_parts = call(
-            functools.partial(feed_weight_body, nh, groups, channels), n, ins,
-            [smem()] + [cut] * groups + [whole(a) for a in ins[1 + groups :]], outs, [per_seq(a) for a in outs],
-            scratch=[pltpu.VMEM((depth, feed_width), F32)],
-                name="late_weights",
-        )
-        late_grads[layer] = lax.psum_scatter(d_wx, "seq", scatter_dimension=0, tiled=False)
+        def late_weights(after):
+            ins = [infos[0]] + [flat(it["x_all"]) for it in saved]
+            ins += [flat(to["d_feed"]) for to in work] + [flat(to["d_raw"]) for to in work]
+            outs = [sds((n, depth, channels), BF), sds((n, 16, depth), F32)] + [sds((n, rows_here, both), BF)] * nh
+            d_wx, d_wdt, *shared_parts = call(
+                functools.partial(feed_weight_body, nh, groups, channels), n, ins,
+                [smem()] + [cut] * groups + [whole(a) for a in ins[1 + groups :]], outs, [per_seq(a) for a in outs],
+                scratch=[pltpu.VMEM((depth, feed_width), F32)],
+                    name="late_weights", after=after,
+            )
+            shared_grads[layer] = (shared_parts, d_wdt)
+            return d_wx
+
+        def send_late(d_wx, after=()):
+            (held,) = line.hand_on([d_wx], after)
+            late_grads[layer] = lax.psum_scatter(held, "seq", scatter_dimension=0, tiled=False)
+
+        d_wx = late_weights([])
+        if layer == 0:
+            stacked = [jnp.stack([parts[k] for parts, steps in shared_grads], axis=1) for k in range(nh)]
+            in_plane = sum(a.astype(F32) for a in scatter_heads(stacked)).astype(BF)
+            steps = jnp.stack([steps for parts, steps in shared_grads], axis=1).astype(BF)
+            send_late(
+                jnp.concatenate([d_wx] + [a.reshape(n, -1, channels) for a in (in_plane, steps)], axis=1),
+                early_grads[:1],
+            )
         below = stored[max(layer - 1, 0)]
         for g in every:
             it, to = saved[g], work[g]
@@ -963,10 +1038,10 @@
             grad_res[g], payload[g], to["gain"] = call(
                 functools.partial(back_norm_body, width), part, ins,
                 [per_seq(ins[0]), whole(ins[1])] + [per_seq(a) for a in ins[2:]],
-                outs, [per_seq(a) for a in outs], name="back_norm",
-                after=[early_grads[layer]] if g == groups - 1 and layer > 0 else [],
-            )
-        shared_grads[layer] = (shared_parts, d_wdt)
+                outs, [per_seq(a) for a in outs], name="back_norm", after=tied(layer, "back_norm"),
+            )
+        if layer > 0:
+            send_late(d_wx)
         small_grads[layer] = tuple(sum(to[k] for to in work) for k in ("chan", "conv", "head")) + (
             sum(jnp.sum(to["gain"][:, 0], axis=0) for to in work),
         )
@@ -1001,13 +1076,11 @@
     head_total = per_head[:, (taps + 3) * channels : cut_at].reshape(layers, 2, LANES)
     conv_shared = everywhere[:, : (taps + 1) * both].reshape(layers, taps + 1, both)
     gain_grad = lax.dynamic_slice_in_dim(everywhere[:, (taps + 1) * both :], place * depth, depth, 1)
-    stacked = [jnp.stack([s[0][k] for s in shared_grads], axis=1) for k in range(nh)]
-    in_plane = sum(a.astype(F32) for a in scatter_heads(stacked)).reshape(n, -1, both)
-    steps = jnp.stack([s[1] for s in shared_grads], axis=1).reshape(n, -1, both)
-    summed = scatter_seq(jnp.concatenate([in_plane, steps], axis=1))
-    split_at = layers * rows_here
+    summed = late_grads[0][depth:]
+    late_grads[0] = late_grads[0][:depth]
+    split_at = layers * rows_here * both // channels
     pieces = gather_heads(summed[:split_at].reshape(layers, rows_here, both))
-    step_sums = summed[split_at:].reshape(layers, 16, depth)
+    step_sums = summed[split_at:].reshape(layers, -1, depth).astype(F32)
     ins = [infos[0]] + pieces
     outs = [sds((layers, nh, rows_here, both), F32)]
     (table,) = call(

time: 1300 us -> 1120 us (0.86)
  starting transfers between devices: 321 us -> 227 us
  Pallas kernels: 456 us -> 366 us
  waiting for transfers between devices: 358 us -> 401 us
  local copies, waits for them, and re-layouts: 89.7 us -> 58.1 us
    ppermute x192 -> x108, waiting for transfers between devices: 149 us -> 255 us  [flip(): return lax.ppermute(x, 'heads', [(i, i ^ k) for i in range(nh)])]
    ppermute x36 -> x0, waiting for transfers between devices: 105 us -> none  [the longest x24 94.9 us: next_hop(): arrived.append(lax.ppermute(out, 'seq', [pair]))]
    pallas_call x96 -> x59, Pallas kernels: 456 us -> 366 us  [call(): pl.pallas_call(kernel, grid=(grid,), in_specs=list(in_specs) + [anywhere(...]
    all_to_all x0 -> x12, waiting for transfers between devices: none -> 89.8 us  [turn(): return lax.all_to_all(states, 'seq', 0, 0)]
    all_to_all x0 -> x12, starting transfers between devices: none -> 77.7 us  [turn(): return lax.all_to_all(states, 'seq', 0, 0)]
    ppermute x192 -> x108, starting transfers between devices: 193 us -> 117 us  [flip(): return lax.ppermute(x, 'heads', [(i, i ^ k) for i in range(nh)])]
    ppermute x27 -> x12, waiting for transfers between devices: 103 us -> 38.5 us  [along(): return lax.ppermute(x, 'seq', pairs)]
    ppermute x27 -> x12, starting transfers between devices: 85.3 us -> 31.4 us  [along(): return lax.ppermute(x, 'seq', pairs)]
  transfers between devices with their start and end apart: 266 -> 144, of which waited for: 65 -> 71; matrix products, arithmetic and copies ran while one was open for 6% -> 6% of each run, Pallas kernels for 32% -> 30%
where the time goes in v2:
time: 1120 us; the launch traced here: 1110 us
  waiting for transfers between devices  401 us (36%)
  Pallas kernels  366 us (33%)
  starting transfers between devices  227 us (20%)
  local copies, waits for them, and re-layouts  58.1 us (5%)
  other arithmetic  43.9 us (4%)
  between operations  16.5 us (1%)
    pallas_call x59, Pallas kernels, call(): pl.pallas_call(kernel, grid=(grid,), in_specs=list(in_specs) + [anywhere(...  366 us
    ppermute x108, waiting for transfers between devices, flip(): return lax.ppermute(x, 'heads', [(i, i ^ k) for i in range(nh)])  255 us
    ppermute x108, starting transfers between devices, flip(): return lax.ppermute(x, 'heads', [(i, i ^ k) for i in range(nh)])  117 us
    all_to_all x12, waiting for transfers between devices, turn(): return lax.all_to_all(states, 'seq', 0, 0)  89.8 us
    all_to_all x12, starting transfers between devices, turn(): return lax.all_to_all(states, 'seq', 0, 0)  77.7 us
    ppermute x12, waiting for transfers between devices, along(): return lax.ppermute(x, 'seq', pairs)  38.5 us
    unnamed x337, local copies, waits for them, and re-layouts  35.9 us
    ppermute x12, starting transfers between devices, along(): return lax.ppermute(x, 'seq', pairs)  31.4 us
  transfers between devices with their start and end apart: 144, of which 71 were waited for; matrix products, arithmetic and copies ran while one was open for 6% of the time, Pallas kernels for 30%

profile of v2, /device:TPU:9, one launch (start us, length us, event | category | flops | bytes accessed | tf_op | source)
XLA Modules:
  0.0 1112.1 jit_solution(7409455471119083621)
XLA Ops:
  43.3 8.3 collective-permute-done.6.refs_5_
  52.1 15.1 %all-gather.13.cloned.1.call-done = bf16[4,656,512]{2,1,0:T(8,128)(2,1)} async-done(((bf16[1,656,512]{2,1,0:T(8,128)(2,1)}), bf16[4,656,512]{2,1,0:T(8,128)(2,1)}) %all-gather.13.cloned.1.call-update) | async-done | bytes 2686992 | tf_op jit(solution)/shard_map/all_gather | solution.py:708
  105.8 9.1 project.3
  115.5 10.2 local.3
  135.8 21.2 %all-to-all-done.refs_0_ = bf16[4,1,144,512]{3,2,1,0:T(8,128)(2,1)S(1)} async-done(((bf16[4,1,144,512]{3,2,1,0:T(8,128)(2,1)}), bf16[4,1,144,512]{3,2,1,0:T(8,128)(2,1)S(1)}, u32[]{:S(2)}, u32[]{:S(2)}) %all-to-all-start) | async-done | bytes 589856 | tf_op jit(solution)/shard_map/all_to_all | solution.py:758
  178.7 8.2 output.3
  196.1 9.9 collective-permute-done.20.refs_4_
  207.3 11.5 %collective-permute-done.24.refs_6_ = bf16[4,32,2176]{2,1,0:T(8,128)(2,1)S(1)} collective-permute-done((bf16[4,32,2176]{2,1,0:T(8,128)(2,1)S(1)}, bf16[4,32,2176]{2,1,0:T(8,128)(2,1)S(1)}, u32[]{:S(2)}, u32[]{:S(2)}) %collective-permute-start.24) | collective-permute-done | bytes 557088 | tf_op jit(solution)/shard_map/ppermute | solution.py:663
  241.8 8.5 collective-permute-done.28.refs_5_
  258.7 9.1 project.4
  268.4 10.3 local.4
  290.4 20.4 %all-to-all-done.2.refs_0_ = bf16[4,1,144,512]{3,2,1,0:T(8,128)(2,1)S(1)} async-done(((bf16[4,1,144,512]{3,2,1,0:T(8,128)(2,1)}), bf16[4,1,144,512]{3,2,1,0:T(8,128)(2,1)S(1)}, u32[]{:S(2)}, u32[]{:S(2)}) %all-to-all-start.2) | async-done | bytes 589856 | tf_op jit(solution)/shard_map/all_to_all | solution.py:758
  313.5 9.5 all-to-all-start.3
  336.2 8.3 output.4
  353.4 9.7 collective-permute-done.35.refs_4_
  364.3 11.7 %collective-permute-done.39.refs_6_ = bf16[4,32,2176]{2,1,0:T(8,128)(2,1)S(1)} collective-permute-done((bf16[4,32,2176]{2,1,0:T(8,128)(2,1)S(1)}, bf16[4,32,2176]{2,1,0:T(8,128)(2,1)S(1)}, u32[]{:S(2)}, u32[]{:S(2)}) %collective-permute-start.39) | collective-permute-done | bytes 557088 | tf_op jit(solution)/shard_map/ppermute | solution.py:663
  398.9 8.6 collective-permute-done.43.refs_5_
  416.4 9.1 project.5
  426.2 10.3 local.5
  448.1 20.6 %all-to-all-done.4.refs_0_ = bf16[4,1,144,512]{3,2,1,0:T(8,128)(2,1)S(1)} async-done(((bf16[4,1,144,512]{3,2,1,0:T(8,128)(2,1)}), bf16[4,1,144,512]{3,2,1,0:T(8,128)(2,1)S(1)}, u32[]{:S(2)}, u32[]{:S(2)}) %all-to-all-start.4) | async-done | bytes 589856 | tf_op jit(solution)/shard_map/all_to_all | solution.py:758
  471.5 9.6 all-to-all-start.5
  493.1 8.3 output.5
  518.8 14.9 %collective-permute-done.52.refs_5_ = bf16[4,32,2176]{2,1,0:T(8,128)(2,1)S(1)} collective-permute-done((bf16[4,32,2176]{2,1,0:T(8,128)(2,1)S(1)}, bf16[4,32,2176]{2,1,0:T(8,128)(2,1)S(1)}, u32[]{:S(2)}, u32[]{:S(2)}) %collective-permute-start.52) | collective-permute-done | bytes 557088 | tf_op jit(solution)/shard_map/ppermute | solution.py:663
  547.3 9.4 collective-permute-done.60.refs_14_
  560.6 9.7 collective-permute-done.58.refs_12_
  573.9 10.0 gate_back.3
  590.3 9.1 early_weights.3
  611.1 11.1 %mix_back.3 = (bf16[4,256,512]{2,1,0:T(8,128)(2,1)}, f32[4,256,256]{2,1,0:T(8,128)}, f32[4,256,256]{2,1,0:T(8,128)}, f32[8,128]{1,0:T(8,128)}) custom-call(bf16[4,256,512]{2,1,0:T(8,128)(2,1)} %get-tuple-element.387.refs_0_, f32[4,256,512]{2,1,0:T(8,128)} %get-tuple-element.381.refs_2_.refs_1_, ...), custom_call_target="tpu_custom_call" | custom-call | flops 1 | bytes 1 | tf_op jit(solution)/shard_map/mix_back/pallas_call | solution.py:73
  623.8 12.4 %state_back.3 = (f32[4,256,768]{2,1,0:T(8,128)}, f32[4,8,768]{2,1,0:T(8,128)}, bf16[4,256,128]{2,1,0:T(8,128)(2,1)}, f32[8,768]{1,0:T(8,128)}, f32[8,128]{1,0:T(8,128)}, /*index=5*/f32[8,128]{1,0:T(8,128)}) custom-call(s32[4]{0:T(128)} %pad_add_fusion.refs_0_, s32[4]{0:T(128)} %refs_1_.11, f32[4,256,768]{2,1,0:T(8,128)} %get-tuple-element.350.refs_2_, ...), custom_call_target="tpu_custom_call" | custom-call | flops 1 | bytes 1 | tf_op jit(solution)/shard_map/state_back/pallas_call | solution.py:73
  647.8 12.3 %spread.3 = (bf16[4,256,768]{2,1,0:T(8,128)(2,1)}, bf16[4,32,2048]{2,1,0:T(8,128)(2,1)}, bf16[4,32,2048]{2,1,0:T(8,128)(2,1)}, bf16[4,32,2048]{2,1,0:T(8,128)(2,...) custom-call(s32[4]{0:T(128)} %pad_add_fusion.refs_0_, ...), custom_call_target="tpu_custom_call" | custom-call | flops 1 | bytes 1 | tf_op jit(solution)/shard_map/spread/pallas_call | solution.py:73
  678.3 10.8 collective-permute-done.69.refs_8_
  701.6 8.0 collective-permute-done.75.refs_14_
  714.5 9.2 collective-permute-done.73.refs_12_
  727.4 10.0 gate_back.4
  743.0 9.1 early_weights.4
  767.7 11.1 %mix_back.4 = (bf16[4,256,512]{2,1,0:T(8,128)(2,1)}, f32[4,256,256]{2,1,0:T(8,128)}, f32[4,256,256]{2,1,0:T(8,128)}, f32[8,128]{1,0:T(8,128)}) custom-call(bf16[4,256,512]{2,1,0:T(8,128)(2,1)} %get-tuple-element.428.refs_0_, f32[4,256,512]{2,1,0:T(8,128)} %get-tuple-element.423.refs_2_.refs_1_, ...), custom_call_target="tpu_custom_call" | custom-call | flops 1 | bytes 1 | tf_op jit(solution)/shard_map/mix_back/pallas_call | solution.py:73
  780.3 12.3 %state_back.4 = (f32[4,256,768]{2,1,0:T(8,128)}, f32[4,8,768]{2,1,0:T(8,128)}, bf16[4,256,128]{2,1,0:T(8,128)(2,1)}, f32[8,768]{1,0:T(8,128)}, f32[8,128]{1,0:T(8,128)}, /*index=5*/f32[8,128]{1,0:T(8,128)}) custom-call(s32[4]{0:T(128)} %pad_add_fusion.refs_0_, s32[4]{0:T(128)} %refs_1_.11, f32[4,256,768]{2,1,0:T(8,128)} %get-tuple-element.318.refs_2_, ...), custom_call_target="tpu_custom_call" | custom-call | flops 1 | bytes 1 | tf_op jit(solution)/shard_map/state_back/pallas_call | solution.py:73
  804.9 12.3 %spread.4 = (bf16[4,256,768]{2,1,0:T(8,128)(2,1)}, bf16[4,32,2048]{2,1,0:T(8,128)(2,1)}, bf16[4,32,2048]{2,1,0:T(8,128)(2,1)}, bf16[4,32,2048]{2,1,0:T(8,128)(2,...) custom-call(s32[4]{0:T(128)} %pad_add_fusion.refs_0_, ...), custom_call_target="tpu_custom_call" | custom-call | flops 1 | bytes 1 | tf_op jit(solution)/shard_map/spread/pallas_call | solution.py:73
  835.7 10.8 collective-permute-done.84.refs_8_
  859.0 8.0 collective-permute-done.90.refs_14_
  872.0 9.2 collective-permute-done.88.refs_12_
  884.8 10.1 gate_back.5
  900.7 9.2 early_weights.5
  925.5 11.2 %mix_back.5 = (bf16[4,256,512]{2,1,0:T(8,128)(2,1)}, f32[4,256,256]{2,1,0:T(8,128)}, f32[4,256,256]{2,1,0:T(8,128)}, f32[8,128]{1,0:T(8,128)}) custom-call(bf16[4,256,512]{2,1,0:T(8,128)(2,1)} %get-tuple-element.469.refs_0_, f32[4,256,512]{2,1,0:T(8,128)} %get-tuple-element.464.refs_2_.refs_1_, ...), custom_call_target="tpu_custom_call" | custom-call | flops 1 | bytes 1 | tf_op jit(solution)/shard_map/mix_back/pallas_call | solution.py:73
  946.9 12.8 %state_back.5 = (f32[4,256,768]{2,1,0:T(8,128)}, f32[4,8,768]{2,1,0:T(8,128)}, bf16[4,256,128]{2,1,0:T(8,128)(2,1)}, f32[8,768]{1,0:T(8,128)}, f32[8,128]{1,0:T(8,128)}, /*index=5*/f32[8,128]{1,0:T(8,128)}) custom-call(s32[4]{0:T(128)} %pad_add_fusion.refs_0_, s32[4]{0:T(128)} %refs_1_.11, f32[4,256,768]{2,1,0:T(8,128)} %get-tuple-element.287.refs_2_, ...), custom_call_target="tpu_custom_call" | custom-call | flops 1 | bytes 1 | tf_op jit(solution)/shard_map/state_back/pallas_call | solution.py:73
  973.4 12.3 %spread.5 = (bf16[4,256,768]{2,1,0:T(8,128)(2,1)}, bf16[4,32,2048]{2,1,0:T(8,128)(2,1)}, bf16[4,32,2048]{2,1,0:T(8,128)(2,1)}, bf16[4,32,2048]{2,1,0:T(8,128)(2,...) custom-call(s32[4]{0:T(128)} %pad_add_fusion.refs_0_, ...), custom_call_target="tpu_custom_call" | custom-call | flops 1 | bytes 1 | tf_op jit(solution)/shard_map/spread/pallas_call | solution.py:73
  1034.6 10.4 collective-permute-done.99.refs_8_
  1064.5 14.2 %collective-permute-done.109 = f32[3,7168]{1,0:T(4,128)S(1)} collective-permute-done((f32[3,7168]{1,0:T(4,128)S(1)}, f32[3,7168]{1,0:T(4,128)S(1)}, u32[]{:S(2)}, u32[]{:S(2)}) %collective-permute-start.109) | collective-permute-done | bytes 86048 | tf_op jit(solution)/shard_map/ppermute | solution.py:667
  (791 shorter events, 568.4 us)
Async XLA Ops:
  7.2 60.0 %all-gather.13.cloned.1.call-start = ((), (), s32[]{:S(2)}) async-start(), calls=%async_computation.24 | async-start | bytes 3358720 | tf_op jit(solution)/shard_map/all_gather | solution.py:708
  12.1 154.8 %all-gather.15.cloned.1.call-start = ((), (), s32[]{:S(2)}) async-start(), calls=%async_computation.25 | async-start | bytes 5242880 | tf_op jit(solution)/shard_map/all_gather | solution.py:708
  27.4 24.1 %collective-permute-start.6 = (bf16[4,32,2048]{2,1,0:T(8,128)(2,1)}, bf16[4,32,2048]{2,1,0:T(8,128)(2,1)}, u32[]{:S(2)}, u32[]{:S(2)}) collective-permute-start(bf16[4,32,2048]{2,1,0:T(8,128)(2,1)} %get-tuple-element.282.refs_1_), channel_id=1, source_target_pairs={{0,4},{1,5},{2,6},{3,7},{4,0},{5,1},{6,2},{7,3},{8,12},{9,13},{10,... | collective-permute-start | bytes 1572872 | tf_op jit(solution)/shard_map/ppermute | solution.py:663
  27.6 24.4 %collective-permute-start.4 = (bf16[4,32,2048]{2,1,0:T(8,128)(2,1)}, bf16[4,32,2048]{2,1,0:T(8,128)(2,1)}, u32[]{:S(2)}, u32[]{:S(2)}) collective-permute-start(bf16[4,32,2048]{2,1,0:T(8,128)(2,1)} %get-tuple-element.282.refs_1_), channel_id=1, source_target_pairs={{0,2},{1,3},{2,0},{3,1},{4,6},{5,7},{6,4},{7,5},{8,10},{9,11},{10,... | collective-permute-start | bytes 1572872 | tf_op jit(solution)/shard_map/ppermute | solution.py:663
  27.9 43.5 %collective-permute-start.3 = (bf16[4,32,2048]{2,1,0:T(8,128)(2,1)}, bf16[4,32,2048]{2,1,0:T(8,128)(2,1)}, u32[]{:S(2)}, u32[]{:S(2)}) collective-permute-start(bf16[4,32,2048]{2,1,0:T(8,128)(2,1)} %get-tuple-element.282.refs_1_), channel_id=1, source_target_pairs={{0,1},{1,0},{2,3},{3,2},{4,5},{5,4},{6,7},{7,6},{8,9},{9,8},{10,11... | collective-permute-start | bytes 1572872 | tf_op jit(solution)/shard_map/ppermute | solution.py:663
  38.3 33.4 %collective-permute-start.9 = (bf16[4,32,2048]{2,1,0:T(8,128)(2,1)}, bf16[4,32,2048]{2,1,0:T(8,128)(2,1)}, u32[]{:S(2)}, u32[]{:S(2)}) collective-permute-start(bf16[4,32,2048]{2,1,0:T(8,128)(2,1)} %collective-permute-done.8.refs_7_), channel_id=1, source_target_pairs={{0,1},{1,0},{2,3},{3,2},{4,5},{5,4},{6,7},{7,6},{8,9},{9,8},{10,11... | collective-permute-start | bytes 1572872 | tf_op jit(solution)/shard_map/ppermute | solution.py:663
  52.0 38.5 %collective-permute-start.5 = (bf16[4,32,2048]{2,1,0:T(8,128)(2,1)}, bf16[4,32,2048]{2,1,0:T(8,128)(2,1)}, u32[]{:S(2)}, u32[]{:S(2)}) collective-permute-start(bf16[4,32,2048]{2,1,0:T(8,128)(2,1)} %collective-permute-done.4.refs_3_), channel_id=1, source_target_pairs={{0,1},{1,0},{2,3},{3,2},{4,5},{5,4},{6,7},{7,6},{8,9},{9,8},{10,11... | collective-permute-start | bytes 1572872 | tf_op jit(solution)/shard_map/ppermute | solution.py:663
  73.7 23.1 %collective-permute-start.10 = (bf16[4,3,64,256]{3,2,1,0:T(8,128)(2,1)}, bf16[4,3,64,256]{3,2,1,0:T(8,128)(2,1)}, u32[]{:S(2)}, u32[]{:S(2)}) collective-permute-start(bf16[4,3,64,256]{3,2,1,0:T(8,128)(2,1)} %reshape.219.refs_1_), channel_id=1, source_target_pairs={{0,1},{1,0},{2,3},{3,2},{4,5},{5,4},{6,7},{7,6},{8,9},{9,8},{10,11... | collective-permute-start | bytes 1179656 | tf_op jit(solution)/shard_map/ppermute | solution.py:663
  92.2 22.7 %collective-permute-start.17 = (bf16[16,2048]{1,0:T(8,128)(2,1)S(1)}, bf16[16,2048]{1,0:T(8,128)(2,1)S(1)}, u32[]{:S(2)}, u32[]{:S(2)}) collective-permute-start(bf16[16,2048]{1,0:T(8,128)(2,1)S(1)} %reshape.221), channel_id=1, source_target_pairs={{0,8},{8,16},{16,24},{1,9},{9,17},{17,25},{2,10},{10,18},{18,26},{... | collective-permute-start | bytes 196616 | tf_op jit(solution)/shard_map/ppermute | solution.py:667
  125.7 31.4 %all-to-all-start = ((bf16[4,1,144,512]{3,2,1,0:T(8,128)(2,1)}), bf16[4,1,144,512]{3,2,1,0:T(8,128)(2,1)S(1)}, u32[]{:S(2)}, u32[]{:S(2)}) async-start(bf16[4,1,144,512]{3,2,1,0:T(8,128)(2,1)} %get-tuple-element.297), calls=%async_computation | async-start | bytes 1179648 | tf_op jit(solution)/shard_map/all_to_all | solution.py:758
  165.9 92.8 %all-gather.17.cloned.1.call-start = ((), (), s32[]{:S(2)}) async-start(), calls=%async_computation.26 | async-start | bytes 5242880 | tf_op jit(solution)/shard_map/all_gather | solution.py:708
  177.9 158.3 %all-gather.19.cloned.1.call-start = ((), (), s32[]{:S(2)}) async-start(), calls=%async_computation.27 | async-start | bytes 2621440 | tf_op jit(solution)/shard_map/all_gather | solution.py:708
  194.2 24.5 %collective-permute-start.24 = (bf16[4,32,2176]{2,1,0:T(8,128)(2,1)S(1)}, bf16[4,32,2176]{2,1,0:T(8,128)(2,1)S(1)}, u32[]{:S(2)}, u32[]{:S(2)}) collective-permute-start(bf16[4,32,2176]{2,1,0:T(8,128)(2,1)S(1)} %add_convert_fusion.8), channel_id=1, source_target_pairs={{0,6},{1,7},{2,4},{3,5},{4,2},{5,3},{6,0},{7,1},{8,14},{9,15},{10,... | collective-permute-start | bytes 1671176 | tf_op jit(solution)/shard_map/ppermute | solution.py:663
  225.3 25.0 %collective-permute-start.28 = (bf16[4,32,2048]{2,1,0:T(8,128)(2,1)}, bf16[4,32,2048]{2,1,0:T(8,128)(2,1)S(1)}, u32[]{:S(2)}, u32[]{:S(2)}) collective-permute-start(bf16[4,32,2048]{2,1,0:T(8,128)(2,1)} %get-tuple-element.315.refs_1_), channel_id=1, source_target_pairs={{0,4},{1,5},{2,6},{3,7},{4,0},{5,1},{6,2},{7,3},{8,12},{9,13},{10,... | collective-permute-start | bytes 1572872 | tf_op jit(solution)/shard_map/ppermute | solution.py:663
  225.9 24.7 %collective-permute-start.26 = (bf16[4,32,2048]{2,1,0:T(8,128)(2,1)}, bf16[4,32,2048]{2,1,0:T(8,128)(2,1)S(1)}, u32[]{:S(2)}, u32[]{:S(2)}) collective-permute-start(bf16[4,32,2048]{2,1,0:T(8,128)(2,1)} %get-tuple-element.315.refs_1_), channel_id=1, source_target_pairs={{0,2},{1,3},{2,0},{3,1},{4,6},{5,7},{6,4},{7,5},{8,10},{9,11},{10,... | collective-permute-start | bytes 1572872 | tf_op jit(solution)/shard_map/ppermute | solution.py:663
  226.6 24.1 %collective-permute-start.25 = (bf16[4,32,2048]{2,1,0:T(8,128)(2,1)}, bf16[4,32,2048]{2,1,0:T(8,128)(2,1)S(1)}, u32[]{:S(2)}, u32[]{:S(2)}) collective-permute-start(bf16[4,32,2048]{2,1,0:T(8,128)(2,1)} %get-tuple-element.315.refs_1_), channel_id=1, source_target_pairs={{0,1},{1,0},{2,3},{3,2},{4,5},{5,4},{6,7},{7,6},{8,9},{9,8},{10,11... | collective-permute-start | bytes 1572872 | tf_op jit(solution)/shard_map/ppermute | solution.py:663
  278.8 32.0 %all-to-all-start.2 = ((bf16[4,1,144,512]{3,2,1,0:T(8,128)(2,1)}), bf16[4,1,144,512]{3,2,1,0:T(8,128)(2,1)S(1)}, u32[]{:S(2)}, u32[]{:S(2)}) async-start(bf16[4,1,144,512]{3,2,1,0:T(8,128)(2,1)} %get-tuple-element.328), calls=%async_computation.2 | async-start | bytes 1179648 | tf_op jit(solution)/shard_map/all_to_all | solution.py:758
  323.0 93.4 %all-gather.21.cloned.1.call-start = ((), (), s32[]{:S(2)}) async-start(), calls=%async_computation.28 | async-start | bytes 5242880 | tf_op jit(solution)/shard_map/all_gather | solution.py:708
  335.6 151.7 %all-gather.23.cloned.1.call-start = ((), (), s32[]{:S(2)}) async-start(), calls=%async_computation.29 | async-start | bytes 2621440 | tf_op jit(solution)/shard_map/all_gather | solution.py:708
  351.9 24.1 %collective-permute-start.39 = (bf16[4,32,2176]{2,1,0:T(8,128)(2,1)S(1)}, bf16[4,32,2176]{2,1,0:T(8,128)(2,1)S(1)}, u32[]{:S(2)}, u32[]{:S(2)}) collective-permute-start(bf16[4,32,2176]{2,1,0:T(8,128)(2,1)S(1)} %add_convert_fusion.4), channel_id=1, source_target_pairs={{0,6},{1,7},{2,4},{3,5},{4,2},{5,3},{6,0},{7,1},{8,14},{9,15},{10,... | collective-permute-start | bytes 1671176 | tf_op jit(solution)/shard_map/ppermute | solution.py:663
  382.4 25.1 %collective-permute-start.43 = (bf16[4,32,2048]{2,1,0:T(8,128)(2,1)}, bf16[4,32,2048]{2,1,0:T(8,128)(2,1)S(1)}, u32[]{:S(2)}, u32[]{:S(2)}) collective-permute-start(bf16[4,32,2048]{2,1,0:T(8,128)(2,1)} %get-tuple-element.347.refs_1_), channel_id=1, source_target_pairs={{0,4},{1,5},{2,6},{3,7},{4,0},{5,1},{6,2},{7,3},{8,12},{9,13},{10,... | collective-permute-start | bytes 1572872 | tf_op jit(solution)/shard_map/ppermute | solution.py:663
  383.5 24.4 %collective-permute-start.41 = (bf16[4,32,2048]{2,1,0:T(8,128)(2,1)}, bf16[4,32,2048]{2,1,0:T(8,128)(2,1)S(1)}, u32[]{:S(2)}, u32[]{:S(2)}) collective-permute-start(bf16[4,32,2048]{2,1,0:T(8,128)(2,1)} %get-tuple-element.347.refs_1_), channel_id=1, source_target_pairs={{0,2},{1,3},{2,0},{3,1},{4,6},{5,7},{6,4},{7,5},{8,10},{9,11},{10,... | collective-permute-start | bytes 1572872 | tf_op jit(solution)/shard_map/ppermute | solution.py:663
  383.9 24.3 %collective-permute-start.40 = (bf16[4,32,2048]{2,1,0:T(8,128)(2,1)}, bf16[4,32,2048]{2,1,0:T(8,128)(2,1)S(1)}, u32[]{:S(2)}, u32[]{:S(2)}) collective-permute-start(bf16[4,32,2048]{2,1,0:T(8,128)(2,1)} %get-tuple-element.347.refs_1_), channel_id=1, source_target_pairs={{0,1},{1,0},{2,3},{3,2},{4,5},{5,4},{6,7},{7,6},{8,9},{9,8},{10,11... | collective-permute-start | bytes 1572872 | tf_op jit(solution)/shard_map/ppermute | solution.py:663
  436.5 32.2 %all-to-all-start.4 = ((bf16[4,1,144,512]{3,2,1,0:T(8,128)(2,1)}), bf16[4,1,144,512]{3,2,1,0:T(8,128)(2,1)S(1)}, u32[]{:S(2)}, u32[]{:S(2)}) async-start(bf16[4,1,144,512]{3,2,1,0:T(8,128)(2,1)} %get-tuple-element.360), calls=%async_computation.4 | async-start | bytes 1179648 | tf_op jit(solution)/shard_map/all_to_all | solution.py:758
  507.9 25.8 %collective-permute-start.52 = (bf16[4,32,2176]{2,1,0:T(8,128)(2,1)S(1)}, bf16[4,32,2176]{2,1,0:T(8,128)(2,1)S(1)}, u32[]{:S(2)}, u32[]{:S(2)}) collective-permute-start(bf16[4,32,2176]{2,1,0:T(8,128)(2,1)S(1)} %add_convert_fusion.1), channel_id=1, source_target_pairs={{0,4},{1,5},{2,6},{3,7},{4,0},{5,1},{6,2},{7,3},{8,12},{9,13},{10,... | collective-permute-start | bytes 1671176 | tf_op jit(solution)/shard_map/ppermute | solution.py:663
  509.2 24.5 %collective-permute-start.54 = (bf16[4,32,2176]{2,1,0:T(8,128)(2,1)S(1)}, bf16[4,32,2176]{2,1,0:T(8,128)(2,1)S(1)}, u32[]{:S(2)}, u32[]{:S(2)}) collective-permute-start(bf16[4,32,2176]{2,1,0:T(8,128)(2,1)S(1)} %add_convert_fusion), channel_id=1, source_target_pairs={{0,6},{1,7},{2,4},{3,5},{4,2},{5,3},{6,0},{7,1},{8,14},{9,15},{10,... | collective-permute-start | bytes 1671176 | tf_op jit(solution)/shard_map/ppermute | solution.py:663
  544.7 25.5 %collective-permute-start.58 = (bf16[4,32,2176]{2,1,0:T(8,128)(2,1)}, bf16[4,32,2176]{2,1,0:T(8,128)(2,1)S(1)}, u32[]{:S(2)}, u32[]{:S(2)}) collective-permute-start(bf16[4,32,2176]{2,1,0:T(8,128)(2,1)} %get-tuple-element.385.refs_8_), channel_id=1, source_target_pairs={{0,4},{1,5},{2,6},{3,7},{4,0},{5,1},{6,2},{7,3},{8,12},{9,13},{10,... | collective-permute-start | bytes 1671176 | tf_op jit(solution)/shard_map/ppermute | solution.py:663
  545.0 25.7 %collective-permute-start.56 = (bf16[4,32,2176]{2,1,0:T(8,128)(2,1)}, bf16[4,32,2176]{2,1,0:T(8,128)(2,1)S(1)}, u32[]{:S(2)}, u32[]{:S(2)}) collective-permute-start(bf16[4,32,2176]{2,1,0:T(8,128)(2,1)} %get-tuple-element.385.refs_8_), channel_id=1, source_target_pairs={{0,2},{1,3},{2,0},{3,1},{4,6},{5,7},{6,4},{7,5},{8,10},{9,11},{10,... | collective-permute-start | bytes 1671176 | tf_op jit(solution)/shard_map/ppermute | solution.py:663
  545.3 25.5 %collective-permute-start.55 = (bf16[4,32,2176]{2,1,0:T(8,128)(2,1)}, bf16[4,32,2176]{2,1,0:T(8,128)(2,1)S(1)}, u32[]{:S(2)}, u32[]{:S(2)}) collective-permute-start(bf16[4,32,2176]{2,1,0:T(8,128)(2,1)} %get-tuple-element.385.refs_8_), channel_id=1, source_target_pairs={{0,1},{1,0},{2,3},{3,2},{4,5},{5,4},{6,7},{7,6},{8,9},{9,8},{10,11... | collective-permute-start | bytes 1671176 | tf_op jit(solution)/shard_map/ppermute | solution.py:663
  610.7 169.6 %reduce-scatter.7.cloned.1.call-start = ((), (), s32[]{:S(2)}) async-start(), calls=%async_computation.18 | async-start | bytes 5242880 | tf_op jit(solution)/shard_map/reduce_scatter | solution.py:936
  623.7 173.8 %reduce-scatter.9.cloned.1.call-start = ((), (), s32[]{:S(2)}) async-start(), calls=%async_computation.19 | async-start | bytes 2621440 | tf_op jit(solution)/shard_map/reduce_scatter | solution.py:1018
  666.5 22.6 %collective-permute-start.69 = (bf16[4,32,2048]{2,1,0:T(8,128)(2,1)S(1)}, bf16[4,32,2048]{2,1,0:T(8,128)(2,1)S(1)}, u32[]{:S(2)}, u32[]{:S(2)}) collective-permute-start(bf16[4,32,2048]{2,1,0:T(8,128)(2,1)S(1)} %add_convert_fusion.20), channel_id=1, source_target_pairs={{0,6},{1,7},{2,4},{3,5},{4,2},{5,3},{6,0},{7,1},{8,14},{9,15},{10,... | collective-permute-start | bytes 1572872 | tf_op jit(solution)/shard_map/ppermute | solution.py:663
  697.4 26.3 %collective-permute-start.73 = (bf16[4,32,2176]{2,1,0:T(8,128)(2,1)S(1)}, bf16[4,32,2176]{2,1,0:T(8,128)(2,1)S(1)}, u32[]{:S(2)}, u32[]{:S(2)}) collective-permute-start(bf16[4,32,2176]{2,1,0:T(8,128)(2,1)S(1)} %copy-done.36), channel_id=1, source_target_pairs={{0,4},{1,5},{2,6},{3,7},{4,0},{5,1},{6,2},{7,3},{8,12},{9,13},{10,... | collective-permute-start | bytes 1671176 | tf_op jit(solution)/shard_map/ppermute | solution.py:663
  698.6 25.5 %collective-permute-start.71 = (bf16[4,32,2176]{2,1,0:T(8,128)(2,1)S(1)}, bf16[4,32,2176]{2,1,0:T(8,128)(2,1)S(1)}, u32[]{:S(2)}, u32[]{:S(2)}) collective-permute-start(bf16[4,32,2176]{2,1,0:T(8,128)(2,1)S(1)} %copy-done.36), channel_id=1, source_target_pairs={{0,2},{1,3},{2,0},{3,1},{4,6},{5,7},{6,4},{7,5},{8,10},{9,11},{10,... | collective-permute-start | bytes 1671176 | tf_op jit(solution)/shard_map/ppermute | solution.py:663
  699.0 25.6 %collective-permute-start.70 = (bf16[4,32,2176]{2,1,0:T(8,128)(2,1)S(1)}, bf16[4,32,2176]{2,1,0:T(8,128)(2,1)S(1)}, u32[]{:S(2)}, u32[]{:S(2)}) collective-permute-start(bf16[4,32,2176]{2,1,0:T(8,128)(2,1)S(1)} %copy-done.36), channel_id=1, source_target_pairs={{0,1},{1,0},{2,3},{3,2},{4,5},{5,4},{6,7},{7,6},{8,9},{9,8},{10,11... | collective-permute-start | bytes 1671176 | tf_op jit(solution)/shard_map/ppermute | solution.py:663
  767.7 179.2 %reduce-scatter.11.cloned.1.call-start = ((), (), s32[]{:S(2)}) async-start(), calls=%async_computation.20 | async-start | bytes 5242880 | tf_op jit(solution)/shard_map/reduce_scatter | solution.py:936
  780.2 192.5 %reduce-scatter.13.cloned.1.call-start = ((), (), s32[]{:S(2)}) async-start(), calls=%async_computation.21 | async-start | bytes 2621440 | tf_op jit(solution)/shard_map/reduce_scatter | solution.py:1018
  824.0 22.6 %collective-permute-start.84 = (bf16[4,32,2048]{2,1,0:T(8,128)(2,1)S(1)}, bf16[4,32,2048]{2,1,0:T(8,128)(2,1)S(1)}, u32[]{:S(2)}, u32[]{:S(2)}) collective-permute-start(bf16[4,32,2048]{2,1,0:T(8,128)(2,1)S(1)} %add_convert_fusion.16), channel_id=1, source_target_pairs={{0,6},{1,7},{2,4},{3,5},{4,2},{5,3},{6,0},{7,1},{8,14},{9,15},{10,... | collective-permute-start | bytes 1572872 | tf_op jit(solution)/shard_map/ppermute | solution.py:663
  854.9 26.3 %collective-permute-start.88 = (bf16[4,32,2176]{2,1,0:T(8,128)(2,1)S(1)}, bf16[4,32,2176]{2,1,0:T(8,128)(2,1)S(1)}, u32[]{:S(2)}, u32[]{:S(2)}) collective-permute-start(bf16[4,32,2176]{2,1,0:T(8,128)(2,1)S(1)} %copy-done.37), channel_id=1, source_target_pairs={{0,4},{1,5},{2,6},{3,7},{4,0},{5,1},{6,2},{7,3},{8,12},{9,13},{10,... | collective-permute-start | bytes 1671176 | tf_op jit(solution)/shard_map/ppermute | solution.py:663
  856.1 25.6 %collective-permute-start.86 = (bf16[4,32,2176]{2,1,0:T(8,128)(2,1)S(1)}, bf16[4,32,2176]{2,1,0:T(8,128)(2,1)S(1)}, u32[]{:S(2)}, u32[]{:S(2)}) collective-permute-start(bf16[4,32,2176]{2,1,0:T(8,128)(2,1)S(1)} %copy-done.37), channel_id=1, source_target_pairs={{0,2},{1,3},{2,0},{3,1},{4,6},{5,7},{6,4},{7,5},{8,10},{9,11},{10,... | collective-permute-start | bytes 1671176 | tf_op jit(solution)/shard_map/ppermute | solution.py:663
  856.5 25.6 %collective-permute-start.85 = (bf16[4,32,2176]{2,1,0:T(8,128)(2,1)S(1)}, bf16[4,32,2176]{2,1,0:T(8,128)(2,1)S(1)}, u32[]{:S(2)}, u32[]{:S(2)}) collective-permute-start(bf16[4,32,2176]{2,1,0:T(8,128)(2,1)S(1)} %copy-done.37), channel_id=1, source_target_pairs={{0,1},{1,0},{2,3},{3,2},{4,5},{5,4},{6,7},{7,6},{8,9},{9,8},{10,11... | collective-permute-start | bytes 1671176 | tf_op jit(solution)/shard_map/ppermute | solution.py:663
  925.5 101.2 %reduce-scatter.15.cloned.1.call-start = ((), (), s32[]{:S(2)}) async-start(), calls=%async_computation.22 | async-start | bytes 5242880 | tf_op jit(solution)/shard_map/reduce_scatter | solution.py:936
  938.2 151.4 %reduce-scatter.17.cloned.1.call-start = ((), (), s32[]{:S(2)}) async-start(), calls=%async_computation.23 | async-start | bytes 3358720 | tf_op jit(solution)/shard_map/reduce_scatter | solution.py:1018
  1007.9 25.8 %collective-permute-start.95 = (bf16[4,32,2048]{2,1,0:T(8,128)(2,1)}, bf16[4,32,2048]{2,1,0:T(8,128)(2,1)}, u32[]{:S(2)}, u32[]{:S(2)}) collective-permute-start(bf16[4,32,2048]{2,1,0:T(8,128)(2,1)} %add_convert_fusion.14), channel_id=1, source_target_pairs={{0,2},{1,3},{2,0},{3,1},{4,6},{5,7},{6,4},{7,5},{8,10},{9,11},{10,... | collective-permute-start | bytes 1572872 | tf_op jit(solution)/shard_map/ppermute | solution.py:663
  1009.1 25.5 %collective-permute-start.97 = (bf16[4,32,2048]{2,1,0:T(8,128)(2,1)}, bf16[4,32,2048]{2,1,0:T(8,128)(2,1)}, u32[]{:S(2)}, u32[]{:S(2)}) collective-permute-start(bf16[4,32,2048]{2,1,0:T(8,128)(2,1)} %add_convert_fusion.13), channel_id=1, source_target_pairs={{0,4},{1,5},{2,6},{3,7},{4,0},{5,1},{6,2},{7,3},{8,12},{9,13},{10,... | collective-permute-start | bytes 1572872 | tf_op jit(solution)/shard_map/ppermute | solution.py:663
  1013.9 31.0 %collective-permute-start.99 = (bf16[4,32,2048]{2,1,0:T(8,128)(2,1)}, bf16[4,32,2048]{2,1,0:T(8,128)(2,1)}, u32[]{:S(2)}, u32[]{:S(2)}) collective-permute-start(bf16[4,32,2048]{2,1,0:T(8,128)(2,1)} %add_convert_fusion.12), channel_id=1, source_target_pairs={{0,6},{1,7},{2,4},{3,5},{4,2},{5,3},{6,0},{7,1},{8,14},{9,15},{10,... | collective-permute-start | bytes 1572872 | tf_op jit(solution)/shard_map/ppermute | solution.py:663
  1050.9 27.9 %collective-permute-start.109 = (f32[3,7168]{1,0:T(4,128)S(1)}, f32[3,7168]{1,0:T(4,128)S(1)}, u32[]{:S(2)}, u32[]{:S(2)}) collective-permute-start(f32[3,7168]{1,0:T(4,128)S(1)} %pad_maximum_fusion.10), channel_id=1, source_target_pairs={{0,24},{8,0},{16,8},{24,16},{1,25},{9,1},{17,9},{25,17},{2,26},{10... | collective-permute-start | bytes 258056 | tf_op jit(solution)/shard_map/ppermute | solution.py:667
  1053.1 25.7 %collective-permute-start.107 = (f32[3,7168]{1,0:T(4,128)S(1)}, f32[3,7168]{1,0:T(4,128)S(1)}, u32[]{:S(2)}, u32[]{:S(2)}) collective-permute-start(f32[3,7168]{1,0:T(4,128)S(1)} %pad_maximum_fusion.10), channel_id=1, source_target_pairs={{0,8},{8,16},{16,24},{24,0},{1,9},{9,17},{17,25},{25,1},{2,10},{10... | collective-permute-start | bytes 258056 | tf_op jit(solution)/shard_map/ppermute | solution.py:667
  (251 other events, 1828.6 us)
Sparse Core Ops, SparseCore 0:
  12.2 54.9 all-gather.12
  69.4 91.7 all-gather.14
  178.0 80.5 all-gather.16
  260.1 56.1 all-gather.18
  335.7 80.6 all-gather.20
  417.8 56.4 all-gather.22
  623.8 80.2 reduce-scatter.6
  706.5 46.8 reduce-scatter.8
  780.3 81.3 reduce-scatter.10
  864.5 46.9 reduce-scatter.12
  938.3 81.1 reduce-scatter.14
  1027.4 62.1 reduce-scatter.16

commit v3 on v2

--- a/solution.py
+++ b/solution.py
@@ -701,8 +701,6 @@
     def fetch(*keys, after=None):
         sources = [{"x": w_x, "z": w_z, "o": w_out}[kind][layer] for kind, layer in keys]
         table = sources[0][None] if len(sources) == 1 else jnp.stack(sources)
-        if not weights:
-            table = jnp.concatenate([table, small.reshape(1, -1, channels)], axis=1)
         if after is not None:
             (table,) = line.hand_on([table], after)
         table = lax.all_gather(table, "seq", axis=0)
@@ -724,7 +722,7 @@
             first_norm_body, part, [x_res[g], gains[0]], [per_seq(x_res[g]), whole(gains[0])], outs,
             [per_seq(outs[0])], name="first_norm",
         )
-    small = weights["x", 0][0][:, 0, depth:]
+    small = in_order(gather_seq(small))
     shared_pieces = gather_heads(small[:, :share_rows].reshape(n, layers, rows_here, both))
     step_pieces = small[:, share_rows:].reshape(n, layers, -1, depth)
     collected = [sds((layers, n, nh, rows_here, both), BF), sds((layers, LANES, width), BF)]

time: 1120 us -> 1110 us (level)
    ppermute x12 -> x15, waiting for transfers between devices: 38.5 us -> 57.1 us  [along(): return lax.ppermute(x, 'seq', pairs)]
    all_gather x6, waiting for transfers between devices: 16.7 us -> 1.05 us  [fetch(): table = lax.all_gather(table, 'seq', axis=0)]
    unnamed x337 -> x369, local copies, waits for them, and re-layouts: 35.9 us -> 37.2 us
    ppermute x12 -> x15, starting transfers between devices: 31.4 us -> 32.2 us  [along(): return lax.ppermute(x, 'seq', pairs)]
  transfers between devices with their start and end apart: 144 -> 147, of which waited for: 71 -> 70; matrix products, arithmetic and copies ran while one was open for 6% -> 6% of each run, Pallas kernels for 30% -> 30%
where the time goes in v3:
time: 1110 us; the launch traced here: 1100 us
  waiting for transfers between devices  400 us (36%)
  Pallas kernels  366 us (33%)
  starting transfers between devices  219 us (20%)
  local copies, waits for them, and re-layouts  57.6 us (5%)
  other arithmetic  43.6 us (4%)
  between operations  16.7 us (2%)
    pallas_call x59, Pallas kernels, call(): pl.pallas_call(kernel, grid=(grid,), in_specs=list(in_specs) + [anywhere(...  366 us
    ppermute x108, waiting for transfers between devices, flip(): return lax.ppermute(x, 'heads', [(i, i ^ k) for i in range(nh)])  251 us
    ppermute x108, starting transfers between devices, flip(): return lax.ppermute(x, 'heads', [(i, i ^ k) for i in range(nh)])  108 us
    all_to_all x12, waiting for transfers between devices, turn(): return lax.all_to_all(states, 'seq', 0, 0)  90.8 us
    all_to_all x12, starting transfers between devices, turn(): return lax.all_to_all(states, 'seq', 0, 0)  78.2 us
    ppermute x15, waiting for transfers between devices, along(): return lax.ppermute(x, 'seq', pairs)  57.1 us
    unnamed x369, local copies, waits for them, and re-layouts  37.2 us
    ppermute x15, starting transfers between devices, along(): return lax.ppermute(x, 'seq', pairs)  32.2 us
  transfers between devices with their start and end apart: 147, of which 70 were waited for; matrix products, arithmetic and copies ran while one was open for 6% of the time, Pallas kernels for 30%

profile of v3, /device:TPU:9, one launch (start us, length us, event | category | flops | bytes accessed | tf_op | source)
XLA Modules:
  0.0 1103.7 jit_solution(5614003482147496058)
XLA Ops:
  28.5 18.5 %collective-permute-done.10 = bf16[144,512]{1,0:T(8,128)(2,1)S(1)} collective-permute-done((bf16[144,512]{1,0:T(8,128)(2,1)S(1)}, bf16[144,512]{1,0:T(8,128)(2,1)S(1)}, u32[]{:S(2)}, u32[]{:S(2)}) %collective-permute-start.10) | collective-permute-done | bytes 147488 | tf_op jit(solution)/shard_map/ppermute | solution.py:667
  52.4 8.4 collective-permute-done.6.refs_5_
  95.4 9.3 project.3
  105.3 10.1 local.3
  127.0 21.1 %all-to-all-done.refs_0_ = bf16[4,1,144,512]{3,2,1,0:T(8,128)(2,1)S(1)} async-done(((bf16[4,1,144,512]{3,2,1,0:T(8,128)(2,1)}), bf16[4,1,144,512]{3,2,1,0:T(8,128)(2,1)S(1)}, u32[]{:S(2)}, u32[]{:S(2)}) %all-to-all-start) | async-done | bytes 589856 | tf_op jit(solution)/shard_map/all_to_all | solution.py:756
  170.1 8.2 output.3
  188.0 9.9 collective-permute-done.23.refs_4_
  197.9 13.0 %collective-permute-done.25.refs_5_ = bf16[4,32,2176]{2,1,0:T(8,128)(2,1)S(1)} collective-permute-done((bf16[4,32,2176]{2,1,0:T(8,128)(2,1)S(1)}, bf16[4,32,2176]{2,1,0:T(8,128)(2,1)S(1)}, u32[]{:S(2)}, u32[]{:S(2)}) %collective-permute-start.25) | collective-permute-done | bytes 557088 | tf_op jit(solution)/shard_map/ppermute | solution.py:663
  221.4 8.0 collective-permute-done.33.refs_7_
  233.8 8.8 collective-permute-done.31.refs_5_
  250.1 9.1 project.4
  259.9 10.3 local.4
  281.9 21.6 %all-to-all-done.2.refs_0_ = bf16[4,1,144,512]{3,2,1,0:T(8,128)(2,1)S(1)} async-done(((bf16[4,1,144,512]{3,2,1,0:T(8,128)(2,1)}), bf16[4,1,144,512]{3,2,1,0:T(8,128)(2,1)S(1)}, u32[]{:S(2)}, u32[]{:S(2)}) %all-to-all-start.2) | async-done | bytes 589856 | tf_op jit(solution)/shard_map/all_to_all | solution.py:756
  306.3 8.2 all-to-all-start.3
  327.6 8.3 output.4
  344.8 9.7 collective-permute-done.38.refs_4_
  355.7 11.6 %collective-permute-done.42.refs_6_ = bf16[4,32,2176]{2,1,0:T(8,128)(2,1)S(1)} collective-permute-done((bf16[4,32,2176]{2,1,0:T(8,128)(2,1)S(1)}, bf16[4,32,2176]{2,1,0:T(8,128)(2,1)S(1)}, u32[]{:S(2)}, u32[]{:S(2)}) %collective-permute-start.42) | collective-permute-done | bytes 557088 | tf_op jit(solution)/shard_map/ppermute | solution.py:663
  390.4 8.6 collective-permute-done.46.refs_5_
  407.9 9.1 project.5
  417.6 10.3 local.5
  439.5 20.6 %all-to-all-done.4.refs_0_ = bf16[4,1,144,512]{3,2,1,0:T(8,128)(2,1)S(1)} async-done(((bf16[4,1,144,512]{3,2,1,0:T(8,128)(2,1)}), bf16[4,1,144,512]{3,2,1,0:T(8,128)(2,1)S(1)}, u32[]{:S(2)}, u32[]{:S(2)}) %all-to-all-start.4) | async-done | bytes 589856 | tf_op jit(solution)/shard_map/all_to_all | solution.py:756
  462.9 9.6 all-to-all-start.5
  484.5 8.3 output.5
  510.3 14.9 %collective-permute-done.55.refs_5_ = bf16[4,32,2176]{2,1,0:T(8,128)(2,1)S(1)} collective-permute-done((bf16[4,32,2176]{2,1,0:T(8,128)(2,1)S(1)}, bf16[4,32,2176]{2,1,0:T(8,128)(2,1)S(1)}, u32[]{:S(2)}, u32[]{:S(2)}) %collective-permute-start.55) | collective-permute-done | bytes 557088 | tf_op jit(solution)/shard_map/ppermute | solution.py:663
  538.8 9.4 collective-permute-done.63.refs_14_
  552.0 9.7 collective-permute-done.61.refs_12_
  565.4 10.0 gate_back.3
  581.8 9.1 early_weights.3
  602.6 11.2 %mix_back.3 = (bf16[4,256,512]{2,1,0:T(8,128)(2,1)}, f32[4,256,256]{2,1,0:T(8,128)}, f32[4,256,256]{2,1,0:T(8,128)}, f32[8,128]{1,0:T(8,128)}) custom-call(bf16[4,256,512]{2,1,0:T(8,128)(2,1)} %get-tuple-element.387.refs_0_, f32[4,256,512]{2,1,0:T(8,128)} %get-tuple-element.381.refs_2_.refs_1_, ...), custom_call_target="tpu_custom_call" | custom-call | flops 1 | bytes 1 | tf_op jit(solution)/shard_map/mix_back/pallas_call | solution.py:73
  615.3 12.5 %state_back.3 = (f32[4,256,768]{2,1,0:T(8,128)}, f32[4,8,768]{2,1,0:T(8,128)}, bf16[4,256,128]{2,1,0:T(8,128)(2,1)}, f32[8,768]{1,0:T(8,128)}, f32[8,128]{1,0:T(8,128)}, /*index=5*/f32[8,128]{1,0:T(8,128)}) custom-call(s32[4]{0:T(128)} %pad_add_fusion.refs_0_, s32[4]{0:T(128)} %refs_1_.11, f32[4,256,768]{2,1,0:T(8,128)} %get-tuple-element.350.refs_2_, ...), custom_call_target="tpu_custom_call" | custom-call | flops 1 | bytes 1 | tf_op jit(solution)/shard_map/state_back/pallas_call | solution.py:73
  639.3 12.3 %spread.3 = (bf16[4,256,768]{2,1,0:T(8,128)(2,1)}, bf16[4,32,2048]{2,1,0:T(8,128)(2,1)}, bf16[4,32,2048]{2,1,0:T(8,128)(2,1)}, bf16[4,32,2048]{2,1,0:T(8,128)(2,...) custom-call(s32[4]{0:T(128)} %pad_add_fusion.refs_0_, ...), custom_call_target="tpu_custom_call" | custom-call | flops 1 | bytes 1 | tf_op jit(solution)/shard_map/spread/pallas_call | solution.py:73
  669.8 10.8 collective-permute-done.72.refs_8_
  706.0 9.2 collective-permute-done.76.refs_12_
  718.8 10.0 gate_back.4
  734.4 9.1 early_weights.4
  759.2 11.1 %mix_back.4 = (bf16[4,256,512]{2,1,0:T(8,128)(2,1)}, f32[4,256,256]{2,1,0:T(8,128)}, f32[4,256,256]{2,1,0:T(8,128)}, f32[8,128]{1,0:T(8,128)}) custom-call(bf16[4,256,512]{2,1,0:T(8,128)(2,1)} %get-tuple-element.428.refs_0_, f32[4,256,512]{2,1,0:T(8,128)} %get-tuple-element.423.refs_2_.refs_1_, ...), custom_call_target="tpu_custom_call" | custom-call | flops 1 | bytes 1 | tf_op jit(solution)/shard_map/mix_back/pallas_call | solution.py:73
  771.9 12.3 %state_back.4 = (f32[4,256,768]{2,1,0:T(8,128)}, f32[4,8,768]{2,1,0:T(8,128)}, bf16[4,256,128]{2,1,0:T(8,128)(2,1)}, f32[8,768]{1,0:T(8,128)}, f32[8,128]{1,0:T(8,128)}, /*index=5*/f32[8,128]{1,0:T(8,128)}) custom-call(s32[4]{0:T(128)} %pad_add_fusion.refs_0_, s32[4]{0:T(128)} %refs_1_.11, f32[4,256,768]{2,1,0:T(8,128)} %get-tuple-element.318.refs_2_, ...), custom_call_target="tpu_custom_call" | custom-call | flops 1 | bytes 1 | tf_op jit(solution)/shard_map/state_back/pallas_call | solution.py:73
  796.6 12.3 %spread.4 = (bf16[4,256,768]{2,1,0:T(8,128)(2,1)}, bf16[4,32,2048]{2,1,0:T(8,128)(2,1)}, bf16[4,32,2048]{2,1,0:T(8,128)(2,1)}, bf16[4,32,2048]{2,1,0:T(8,128)(2,...) custom-call(s32[4]{0:T(128)} %pad_add_fusion.refs_0_, ...), custom_call_target="tpu_custom_call" | custom-call | flops 1 | bytes 1 | tf_op jit(solution)/shard_map/spread/pallas_call | solution.py:73
  827.3 10.8 collective-permute-done.87.refs_8_
  850.6 8.0 collective-permute-done.93.refs_14_
  863.6 9.2 collective-permute-done.91.refs_12_
  876.4 10.1 gate_back.5
  892.3 9.2 early_weights.5
  917.0 11.1 %mix_back.5 = (bf16[4,256,512]{2,1,0:T(8,128)(2,1)}, f32[4,256,256]{2,1,0:T(8,128)}, f32[4,256,256]{2,1,0:T(8,128)}, f32[8,128]{1,0:T(8,128)}) custom-call(bf16[4,256,512]{2,1,0:T(8,128)(2,1)} %get-tuple-element.469.refs_0_, f32[4,256,512]{2,1,0:T(8,128)} %get-tuple-element.464.refs_2_.refs_1_, ...), custom_call_target="tpu_custom_call" | custom-call | flops 1 | bytes 1 | tf_op jit(solution)/shard_map/mix_back/pallas_call | solution.py:73
  938.4 12.8 %state_back.5 = (f32[4,256,768]{2,1,0:T(8,128)}, f32[4,8,768]{2,1,0:T(8,128)}, bf16[4,256,128]{2,1,0:T(8,128)(2,1)}, f32[8,768]{1,0:T(8,128)}, f32[8,128]{1,0:T(8,128)}, /*index=5*/f32[8,128]{1,0:T(8,128)}) custom-call(s32[4]{0:T(128)} %pad_add_fusion.refs_0_, s32[4]{0:T(128)} %refs_1_.11, f32[4,256,768]{2,1,0:T(8,128)} %get-tuple-element.287.refs_2_, ...), custom_call_target="tpu_custom_call" | custom-call | flops 1 | bytes 1 | tf_op jit(solution)/shard_map/state_back/pallas_call | solution.py:73
  964.9 12.3 %spread.5 = (bf16[4,256,768]{2,1,0:T(8,128)(2,1)}, bf16[4,32,2048]{2,1,0:T(8,128)(2,1)}, bf16[4,32,2048]{2,1,0:T(8,128)(2,1)}, bf16[4,32,2048]{2,1,0:T(8,128)(2,...) custom-call(s32[4]{0:T(128)} %pad_add_fusion.refs_0_, ...), custom_call_target="tpu_custom_call" | custom-call | flops 1 | bytes 1 | tf_op jit(solution)/shard_map/spread/pallas_call | solution.py:73
  1026.1 10.4 collective-permute-done.102.refs_8_
  1056.1 14.2 %collective-permute-done.112 = f32[3,7168]{1,0:T(4,128)S(1)} collective-permute-done((f32[3,7168]{1,0:T(4,128)S(1)}, f32[3,7168]{1,0:T(4,128)S(1)}, u32[]{:S(2)}, u32[]{:S(2)}) %collective-permute-start.112) | collective-permute-done | bytes 86048 | tf_op jit(solution)/shard_map/ppermute | solution.py:667
  (829 shorter events, 554.4 us)
Async XLA Ops:
  7.2 88.2 %all-gather.13.cloned.1.call-start = ((), (), s32[]{:S(2)}) async-start(), calls=%async_computation.24 | async-start | bytes 2621440 | tf_op jit(solution)/shard_map/all_gather | solution.py:706
  10.8 147.8 %all-gather.15.cloned.1.call-start = ((), (), s32[]{:S(2)}) async-start(), calls=%async_computation.25 | async-start | bytes 5242880 | tf_op jit(solution)/shard_map/all_gather | solution.py:706
  14.8 32.2 %collective-permute-start.12 = (bf16[144,512]{1,0:T(8,128)(2,1)S(1)}, bf16[144,512]{1,0:T(8,128)(2,1)S(1)}, u32[]{:S(2)}, u32[]{:S(2)}) collective-permute-start(bf16[144,512]{1,0:T(8,128)(2,1)S(1)} %pad_maximum_fusion.9), channel_id=1, source_target_pairs={{0,8},{8,16},{16,24},{24,0},{1,9},{9,17},{17,25},{25,1},{2,10},{10... | collective-permute-start | bytes 442376 | tf_op jit(solution)/shard_map/ppermute | solution.py:667
  14.9 32.1 %collective-permute-start.11 = (bf16[144,512]{1,0:T(8,128)(2,1)S(1)}, bf16[144,512]{1,0:T(8,128)(2,1)S(1)}, u32[]{:S(2)}, u32[]{:S(2)}) collective-permute-start(bf16[144,512]{1,0:T(8,128)(2,1)S(1)} %pad_maximum_fusion.9), channel_id=1, source_target_pairs={{0,16},{8,24},{16,0},{24,8},{1,17},{9,25},{17,1},{25,9},{2,18},{10... | collective-permute-start | bytes 442376 | tf_op jit(solution)/shard_map/ppermute | solution.py:667
  20.7 26.3 %collective-permute-start.10 = (bf16[144,512]{1,0:T(8,128)(2,1)S(1)}, bf16[144,512]{1,0:T(8,128)(2,1)S(1)}, u32[]{:S(2)}, u32[]{:S(2)}) collective-permute-start(bf16[144,512]{1,0:T(8,128)(2,1)S(1)} %pad_maximum_fusion.9), channel_id=1, source_target_pairs={{0,24},{8,0},{16,8},{24,16},{1,25},{9,1},{17,9},{25,17},{2,26},{10... | collective-permute-start | bytes 442376 | tf_op jit(solution)/shard_map/ppermute | solution.py:667
  26.1 25.1 %collective-permute-start.8 = (bf16[4,32,2048]{2,1,0:T(8,128)(2,1)}, bf16[4,32,2048]{2,1,0:T(8,128)(2,1)}, u32[]{:S(2)}, u32[]{:S(2)}) collective-permute-start(bf16[4,32,2048]{2,1,0:T(8,128)(2,1)} %get-tuple-element.282.refs_1_), channel_id=1, source_target_pairs={{0,6},{1,7},{2,4},{3,5},{4,2},{5,3},{6,0},{7,1},{8,14},{9,15},{10,... | collective-permute-start | bytes 1572872 | tf_op jit(solution)/shard_map/ppermute | solution.py:663
  28.2 32.6 %collective-permute-start.6 = (bf16[4,32,2048]{2,1,0:T(8,128)(2,1)}, bf16[4,32,2048]{2,1,0:T(8,128)(2,1)}, u32[]{:S(2)}, u32[]{:S(2)}) collective-permute-start(bf16[4,32,2048]{2,1,0:T(8,128)(2,1)} %get-tuple-element.282.refs_1_), channel_id=1, source_target_pairs={{0,4},{1,5},{2,6},{3,7},{4,0},{5,1},{6,2},{7,3},{8,12},{9,13},{10,... | collective-permute-start | bytes 1572872 | tf_op jit(solution)/shard_map/ppermute | solution.py:663
  51.2 27.3 %collective-permute-start.4 = (bf16[4,32,2048]{2,1,0:T(8,128)(2,1)}, bf16[4,32,2048]{2,1,0:T(8,128)(2,1)}, u32[]{:S(2)}, u32[]{:S(2)}) collective-permute-start(bf16[4,32,2048]{2,1,0:T(8,128)(2,1)} %get-tuple-element.282.refs_1_), channel_id=1, source_target_pairs={{0,2},{1,3},{2,0},{3,1},{4,6},{5,7},{6,4},{7,5},{8,10},{9,11},{10,... | collective-permute-start | bytes 1572872 | tf_op jit(solution)/shard_map/ppermute | solution.py:663
  115.4 32.7 %all-to-all-start = ((bf16[4,1,144,512]{3,2,1,0:T(8,128)(2,1)}), bf16[4,1,144,512]{3,2,1,0:T(8,128)(2,1)S(1)}, u32[]{:S(2)}, u32[]{:S(2)}) async-start(bf16[4,1,144,512]{3,2,1,0:T(8,128)(2,1)} %get-tuple-element.297), calls=%async_computation | async-start | bytes 1179648 | tf_op jit(solution)/shard_map/all_to_all | solution.py:756
  157.5 92.6 %all-gather.17.cloned.1.call-start = ((), (), s32[]{:S(2)}) async-start(), calls=%async_computation.26 | async-start | bytes 5242880 | tf_op jit(solution)/shard_map/all_gather | solution.py:706
  169.3 158.3 %all-gather.19.cloned.1.call-start = ((), (), s32[]{:S(2)}) async-start(), calls=%async_computation.27 | async-start | bytes 2621440 | tf_op jit(solution)/shard_map/all_gather | solution.py:706
  185.4 25.5 %collective-permute-start.25 = (bf16[4,32,2176]{2,1,0:T(8,128)(2,1)S(1)}, bf16[4,32,2176]{2,1,0:T(8,128)(2,1)S(1)}, u32[]{:S(2)}, u32[]{:S(2)}) collective-permute-start(bf16[4,32,2176]{2,1,0:T(8,128)(2,1)S(1)} %add_convert_fusion.9), channel_id=1, source_target_pairs={{0,4},{1,5},{2,6},{3,7},{4,0},{5,1},{6,2},{7,3},{8,12},{9,13},{10,... | collective-permute-start | bytes 1671176 | tf_op jit(solution)/shard_map/ppermute | solution.py:663
  185.6 25.3 %collective-permute-start.27 = (bf16[4,32,2176]{2,1,0:T(8,128)(2,1)S(1)}, bf16[4,32,2176]{2,1,0:T(8,128)(2,1)S(1)}, u32[]{:S(2)}, u32[]{:S(2)}) collective-permute-start(bf16[4,32,2176]{2,1,0:T(8,128)(2,1)S(1)} %add_convert_fusion.8), channel_id=1, source_target_pairs={{0,6},{1,7},{2,4},{3,5},{4,2},{5,3},{6,0},{7,1},{8,14},{9,15},{10,... | collective-permute-start | bytes 1671176 | tf_op jit(solution)/shard_map/ppermute | solution.py:663
  217.2 25.3 %collective-permute-start.31 = (bf16[4,32,2048]{2,1,0:T(8,128)(2,1)}, bf16[4,32,2048]{2,1,0:T(8,128)(2,1)S(1)}, u32[]{:S(2)}, u32[]{:S(2)}) collective-permute-start(bf16[4,32,2048]{2,1,0:T(8,128)(2,1)} %get-tuple-element.315.refs_1_), channel_id=1, source_target_pairs={{0,4},{1,5},{2,6},{3,7},{4,0},{5,1},{6,2},{7,3},{8,12},{9,13},{10,... | collective-permute-start | bytes 1572872 | tf_op jit(solution)/shard_map/ppermute | solution.py:663
  217.2 25.7 %collective-permute-start.29 = (bf16[4,32,2048]{2,1,0:T(8,128)(2,1)}, bf16[4,32,2048]{2,1,0:T(8,128)(2,1)S(1)}, u32[]{:S(2)}, u32[]{:S(2)}) collective-permute-start(bf16[4,32,2048]{2,1,0:T(8,128)(2,1)} %get-tuple-element.315.refs_1_), channel_id=1, source_target_pairs={{0,2},{1,3},{2,0},{3,1},{4,6},{5,7},{6,4},{7,5},{8,10},{9,11},{10,... | collective-permute-start | bytes 1572872 | tf_op jit(solution)/shard_map/ppermute | solution.py:663
  218.9 24.1 %collective-permute-start.28 = (bf16[4,32,2048]{2,1,0:T(8,128)(2,1)}, bf16[4,32,2048]{2,1,0:T(8,128)(2,1)S(1)}, u32[]{:S(2)}, u32[]{:S(2)}) collective-permute-start(bf16[4,32,2048]{2,1,0:T(8,128)(2,1)} %get-tuple-element.315.refs_1_), channel_id=1, source_target_pairs={{0,1},{1,0},{2,3},{3,2},{4,5},{5,4},{6,7},{7,6},{8,9},{9,8},{10,11... | collective-permute-start | bytes 1572872 | tf_op jit(solution)/shard_map/ppermute | solution.py:663
  270.2 33.3 %all-to-all-start.2 = ((bf16[4,1,144,512]{3,2,1,0:T(8,128)(2,1)}), bf16[4,1,144,512]{3,2,1,0:T(8,128)(2,1)S(1)}, u32[]{:S(2)}, u32[]{:S(2)}) async-start(bf16[4,1,144,512]{3,2,1,0:T(8,128)(2,1)} %get-tuple-element.328), calls=%async_computation.2 | async-start | bytes 1179648 | tf_op jit(solution)/shard_map/all_to_all | solution.py:756
  314.4 93.4 %all-gather.21.cloned.1.call-start = ((), (), s32[]{:S(2)}) async-start(), calls=%async_computation.28 | async-start | bytes 5242880 | tf_op jit(solution)/shard_map/all_gather | solution.py:706
  327.0 151.7 %all-gather.23.cloned.1.call-start = ((), (), s32[]{:S(2)}) async-start(), calls=%async_computation.29 | async-start | bytes 2621440 | tf_op jit(solution)/shard_map/all_gather | solution.py:706
  343.3 24.1 %collective-permute-start.42 = (bf16[4,32,2176]{2,1,0:T(8,128)(2,1)S(1)}, bf16[4,32,2176]{2,1,0:T(8,128)(2,1)S(1)}, u32[]{:S(2)}, u32[]{:S(2)}) collective-permute-start(bf16[4,32,2176]{2,1,0:T(8,128)(2,1)S(1)} %add_convert_fusion.4), channel_id=1, source_target_pairs={{0,6},{1,7},{2,4},{3,5},{4,2},{5,3},{6,0},{7,1},{8,14},{9,15},{10,... | collective-permute-start | bytes 1671176 | tf_op jit(solution)/shard_map/ppermute | solution.py:663
  373.8 25.1 %collective-permute-start.46 = (bf16[4,32,2048]{2,1,0:T(8,128)(2,1)}, bf16[4,32,2048]{2,1,0:T(8,128)(2,1)S(1)}, u32[]{:S(2)}, u32[]{:S(2)}) collective-permute-start(bf16[4,32,2048]{2,1,0:T(8,128)(2,1)} %get-tuple-element.347.refs_1_), channel_id=1, source_target_pairs={{0,4},{1,5},{2,6},{3,7},{4,0},{5,1},{6,2},{7,3},{8,12},{9,13},{10,... | collective-permute-start | bytes 1572872 | tf_op jit(solution)/shard_map/ppermute | solution.py:663
  375.0 24.4 %collective-permute-start.44 = (bf16[4,32,2048]{2,1,0:T(8,128)(2,1)}, bf16[4,32,2048]{2,1,0:T(8,128)(2,1)S(1)}, u32[]{:S(2)}, u32[]{:S(2)}) collective-permute-start(bf16[4,32,2048]{2,1,0:T(8,128)(2,1)} %get-tuple-element.347.refs_1_), channel_id=1, source_target_pairs={{0,2},{1,3},{2,0},{3,1},{4,6},{5,7},{6,4},{7,5},{8,10},{9,11},{10,... | collective-permute-start | bytes 1572872 | tf_op jit(solution)/shard_map/ppermute | solution.py:663
  375.4 24.3 %collective-permute-start.43 = (bf16[4,32,2048]{2,1,0:T(8,128)(2,1)}, bf16[4,32,2048]{2,1,0:T(8,128)(2,1)S(1)}, u32[]{:S(2)}, u32[]{:S(2)}) collective-permute-start(bf16[4,32,2048]{2,1,0:T(8,128)(2,1)} %get-tuple-element.347.refs_1_), channel_id=1, source_target_pairs={{0,1},{1,0},{2,3},{3,2},{4,5},{5,4},{6,7},{7,6},{8,9},{9,8},{10,11... | collective-permute-start | bytes 1572872 | tf_op jit(solution)/shard_map/ppermute | solution.py:663
  427.9 32.2 %all-to-all-start.4 = ((bf16[4,1,144,512]{3,2,1,0:T(8,128)(2,1)}), bf16[4,1,144,512]{3,2,1,0:T(8,128)(2,1)S(1)}, u32[]{:S(2)}, u32[]{:S(2)}) async-start(bf16[4,1,144,512]{3,2,1,0:T(8,128)(2,1)} %get-tuple-element.360), calls=%async_computation.4 | async-start | bytes 1179648 | tf_op jit(solution)/shard_map/all_to_all | solution.py:756
  499.4 25.8 %collective-permute-start.55 = (bf16[4,32,2176]{2,1,0:T(8,128)(2,1)S(1)}, bf16[4,32,2176]{2,1,0:T(8,128)(2,1)S(1)}, u32[]{:S(2)}, u32[]{:S(2)}) collective-permute-start(bf16[4,32,2176]{2,1,0:T(8,128)(2,1)S(1)} %add_convert_fusion.1), channel_id=1, source_target_pairs={{0,4},{1,5},{2,6},{3,7},{4,0},{5,1},{6,2},{7,3},{8,12},{9,13},{10,... | collective-permute-start | bytes 1671176 | tf_op jit(solution)/shard_map/ppermute | solution.py:663
  500.8 24.5 %collective-permute-start.57 = (bf16[4,32,2176]{2,1,0:T(8,128)(2,1)S(1)}, bf16[4,32,2176]{2,1,0:T(8,128)(2,1)S(1)}, u32[]{:S(2)}, u32[]{:S(2)}) collective-permute-start(bf16[4,32,2176]{2,1,0:T(8,128)(2,1)S(1)} %add_convert_fusion), channel_id=1, source_target_pairs={{0,6},{1,7},{2,4},{3,5},{4,2},{5,3},{6,0},{7,1},{8,14},{9,15},{10,... | collective-permute-start | bytes 1671176 | tf_op jit(solution)/shard_map/ppermute | solution.py:663
  536.2 25.5 %collective-permute-start.61 = (bf16[4,32,2176]{2,1,0:T(8,128)(2,1)}, bf16[4,32,2176]{2,1,0:T(8,128)(2,1)S(1)}, u32[]{:S(2)}, u32[]{:S(2)}) collective-permute-start(bf16[4,32,2176]{2,1,0:T(8,128)(2,1)} %get-tuple-element.385.refs_8_), channel_id=1, source_target_pairs={{0,4},{1,5},{2,6},{3,7},{4,0},{5,1},{6,2},{7,3},{8,12},{9,13},{10,... | collective-permute-start | bytes 1671176 | tf_op jit(solution)/shard_map/ppermute | solution.py:663
  536.5 25.7 %collective-permute-start.59 = (bf16[4,32,2176]{2,1,0:T(8,128)(2,1)}, bf16[4,32,2176]{2,1,0:T(8,128)(2,1)S(1)}, u32[]{:S(2)}, u32[]{:S(2)}) collective-permute-start(bf16[4,32,2176]{2,1,0:T(8,128)(2,1)} %get-tuple-element.385.refs_8_), channel_id=1, source_target_pairs={{0,2},{1,3},{2,0},{3,1},{4,6},{5,7},{6,4},{7,5},{8,10},{9,11},{10,... | collective-permute-start | bytes 1671176 | tf_op jit(solution)/shard_map/ppermute | solution.py:663
  536.8 25.5 %collective-permute-start.58 = (bf16[4,32,2176]{2,1,0:T(8,128)(2,1)}, bf16[4,32,2176]{2,1,0:T(8,128)(2,1)S(1)}, u32[]{:S(2)}, u32[]{:S(2)}) collective-permute-start(bf16[4,32,2176]{2,1,0:T(8,128)(2,1)} %get-tuple-element.385.refs_8_), channel_id=1, source_target_pairs={{0,1},{1,0},{2,3},{3,2},{4,5},{5,4},{6,7},{7,6},{8,9},{9,8},{10,11... | collective-permute-start | bytes 1671176 | tf_op jit(solution)/shard_map/ppermute | solution.py:663
  602.2 169.7 %reduce-scatter.7.cloned.1.call-start = ((), (), s32[]{:S(2)}) async-start(), calls=%async_computation.18 | async-start | bytes 5242880 | tf_op jit(solution)/shard_map/reduce_scatter | solution.py:934
  615.3 173.9 %reduce-scatter.9.cloned.1.call-start = ((), (), s32[]{:S(2)}) async-start(), calls=%async_computation.19 | async-start | bytes 2621440 | tf_op jit(solution)/shard_map/reduce_scatter | solution.py:1016
  658.0 22.5 %collective-permute-start.72 = (bf16[4,32,2048]{2,1,0:T(8,128)(2,1)S(1)}, bf16[4,32,2048]{2,1,0:T(8,128)(2,1)S(1)}, u32[]{:S(2)}, u32[]{:S(2)}) collective-permute-start(bf16[4,32,2048]{2,1,0:T(8,128)(2,1)S(1)} %add_convert_fusion.20), channel_id=1, source_target_pairs={{0,6},{1,7},{2,4},{3,5},{4,2},{5,3},{6,0},{7,1},{8,14},{9,15},{10,... | collective-permute-start | bytes 1572872 | tf_op jit(solution)/shard_map/ppermute | solution.py:663
  688.9 26.3 %collective-permute-start.76 = (bf16[4,32,2176]{2,1,0:T(8,128)(2,1)S(1)}, bf16[4,32,2176]{2,1,0:T(8,128)(2,1)S(1)}, u32[]{:S(2)}, u32[]{:S(2)}) collective-permute-start(bf16[4,32,2176]{2,1,0:T(8,128)(2,1)S(1)} %copy-done.46), channel_id=1, source_target_pairs={{0,4},{1,5},{2,6},{3,7},{4,0},{5,1},{6,2},{7,3},{8,12},{9,13},{10,... | collective-permute-start | bytes 1671176 | tf_op jit(solution)/shard_map/ppermute | solution.py:663
  690.1 25.5 %collective-permute-start.74 = (bf16[4,32,2176]{2,1,0:T(8,128)(2,1)S(1)}, bf16[4,32,2176]{2,1,0:T(8,128)(2,1)S(1)}, u32[]{:S(2)}, u32[]{:S(2)}) collective-permute-start(bf16[4,32,2176]{2,1,0:T(8,128)(2,1)S(1)} %copy-done.46), channel_id=1, source_target_pairs={{0,2},{1,3},{2,0},{3,1},{4,6},{5,7},{6,4},{7,5},{8,10},{9,11},{10,... | collective-permute-start | bytes 1671176 | tf_op jit(solution)/shard_map/ppermute | solution.py:663
  690.5 25.6 %collective-permute-start.73 = (bf16[4,32,2176]{2,1,0:T(8,128)(2,1)S(1)}, bf16[4,32,2176]{2,1,0:T(8,128)(2,1)S(1)}, u32[]{:S(2)}, u32[]{:S(2)}) collective-permute-start(bf16[4,32,2176]{2,1,0:T(8,128)(2,1)S(1)} %copy-done.46), channel_id=1, source_target_pairs={{0,1},{1,0},{2,3},{3,2},{4,5},{5,4},{6,7},{7,6},{8,9},{9,8},{10,11... | collective-permute-start | bytes 1671176 | tf_op jit(solution)/shard_map/ppermute | solution.py:663
  759.2 179.2 %reduce-scatter.11.cloned.1.call-start = ((), (), s32[]{:S(2)}) async-start(), calls=%async_computation.20 | async-start | bytes 5242880 | tf_op jit(solution)/shard_map/reduce_scatter | solution.py:934
  771.8 192.5 %reduce-scatter.13.cloned.1.call-start = ((), (), s32[]{:S(2)}) async-start(), calls=%async_computation.21 | async-start | bytes 2621440 | tf_op jit(solution)/shard_map/reduce_scatter | solution.py:1016
  815.5 22.6 %collective-permute-start.87 = (bf16[4,32,2048]{2,1,0:T(8,128)(2,1)S(1)}, bf16[4,32,2048]{2,1,0:T(8,128)(2,1)S(1)}, u32[]{:S(2)}, u32[]{:S(2)}) collective-permute-start(bf16[4,32,2048]{2,1,0:T(8,128)(2,1)S(1)} %add_convert_fusion.16), channel_id=1, source_target_pairs={{0,6},{1,7},{2,4},{3,5},{4,2},{5,3},{6,0},{7,1},{8,14},{9,15},{10,... | collective-permute-start | bytes 1572872 | tf_op jit(solution)/shard_map/ppermute | solution.py:663
  846.4 26.4 %collective-permute-start.91 = (bf16[4,32,2176]{2,1,0:T(8,128)(2,1)S(1)}, bf16[4,32,2176]{2,1,0:T(8,128)(2,1)S(1)}, u32[]{:S(2)}, u32[]{:S(2)}) collective-permute-start(bf16[4,32,2176]{2,1,0:T(8,128)(2,1)S(1)} %copy-done.47), channel_id=1, source_target_pairs={{0,4},{1,5},{2,6},{3,7},{4,0},{5,1},{6,2},{7,3},{8,12},{9,13},{10,... | collective-permute-start | bytes 1671176 | tf_op jit(solution)/shard_map/ppermute | solution.py:663
  847.6 25.6 %collective-permute-start.89 = (bf16[4,32,2176]{2,1,0:T(8,128)(2,1)S(1)}, bf16[4,32,2176]{2,1,0:T(8,128)(2,1)S(1)}, u32[]{:S(2)}, u32[]{:S(2)}) collective-permute-start(bf16[4,32,2176]{2,1,0:T(8,128)(2,1)S(1)} %copy-done.47), channel_id=1, source_target_pairs={{0,2},{1,3},{2,0},{3,1},{4,6},{5,7},{6,4},{7,5},{8,10},{9,11},{10,... | collective-permute-start | bytes 1671176 | tf_op jit(solution)/shard_map/ppermute | solution.py:663
  848.1 25.6 %collective-permute-start.88 = (bf16[4,32,2176]{2,1,0:T(8,128)(2,1)S(1)}, bf16[4,32,2176]{2,1,0:T(8,128)(2,1)S(1)}, u32[]{:S(2)}, u32[]{:S(2)}) collective-permute-start(bf16[4,32,2176]{2,1,0:T(8,128)(2,1)S(1)} %copy-done.47), channel_id=1, source_target_pairs={{0,1},{1,0},{2,3},{3,2},{4,5},{5,4},{6,7},{7,6},{8,9},{9,8},{10,11... | collective-permute-start | bytes 1671176 | tf_op jit(solution)/shard_map/ppermute | solution.py:663
  917.0 101.2 %reduce-scatter.15.cloned.1.call-start = ((), (), s32[]{:S(2)}) async-start(), calls=%async_computation.22 | async-start | bytes 5242880 | tf_op jit(solution)/shard_map/reduce_scatter | solution.py:934
  929.7 151.4 %reduce-scatter.17.cloned.1.call-start = ((), (), s32[]{:S(2)}) async-start(), calls=%async_computation.23 | async-start | bytes 3358720 | tf_op jit(solution)/shard_map/reduce_scatter | solution.py:1016
  999.4 25.8 %collective-permute-start.98 = (bf16[4,32,2048]{2,1,0:T(8,128)(2,1)}, bf16[4,32,2048]{2,1,0:T(8,128)(2,1)}, u32[]{:S(2)}, u32[]{:S(2)}) collective-permute-start(bf16[4,32,2048]{2,1,0:T(8,128)(2,1)} %add_convert_fusion.14), channel_id=1, source_target_pairs={{0,2},{1,3},{2,0},{3,1},{4,6},{5,7},{6,4},{7,5},{8,10},{9,11},{10,... | collective-permute-start | bytes 1572872 | tf_op jit(solution)/shard_map/ppermute | solution.py:663
  1000.6 25.5 %collective-permute-start.100 = (bf16[4,32,2048]{2,1,0:T(8,128)(2,1)}, bf16[4,32,2048]{2,1,0:T(8,128)(2,1)}, u32[]{:S(2)}, u32[]{:S(2)}) collective-permute-start(bf16[4,32,2048]{2,1,0:T(8,128)(2,1)} %add_convert_fusion.13), channel_id=1, source_target_pairs={{0,4},{1,5},{2,6},{3,7},{4,0},{5,1},{6,2},{7,3},{8,12},{9,13},{10,... | collective-permute-start | bytes 1572872 | tf_op jit(solution)/shard_map/ppermute | solution.py:663
  1005.4 31.0 %collective-permute-start.102 = (bf16[4,32,2048]{2,1,0:T(8,128)(2,1)}, bf16[4,32,2048]{2,1,0:T(8,128)(2,1)}, u32[]{:S(2)}, u32[]{:S(2)}) collective-permute-start(bf16[4,32,2048]{2,1,0:T(8,128)(2,1)} %add_convert_fusion.12), channel_id=1, source_target_pairs={{0,6},{1,7},{2,4},{3,5},{4,2},{5,3},{6,0},{7,1},{8,14},{9,15},{10,... | collective-permute-start | bytes 1572872 | tf_op jit(solution)/shard_map/ppermute | solution.py:663
  1042.4 27.9 %collective-permute-start.112 = (f32[3,7168]{1,0:T(4,128)S(1)}, f32[3,7168]{1,0:T(4,128)S(1)}, u32[]{:S(2)}, u32[]{:S(2)}) collective-permute-start(f32[3,7168]{1,0:T(4,128)S(1)} %pad_maximum_fusion.10), channel_id=1, source_target_pairs={{0,24},{8,0},{16,8},{24,16},{1,25},{9,1},{17,9},{25,17},{2,26},{10... | collective-permute-start | bytes 258056 | tf_op jit(solution)/shard_map/ppermute | solution.py:667
  1044.6 25.7 %collective-permute-start.110 = (f32[3,7168]{1,0:T(4,128)S(1)}, f32[3,7168]{1,0:T(4,128)S(1)}, u32[]{:S(2)}, u32[]{:S(2)}) collective-permute-start(f32[3,7168]{1,0:T(4,128)S(1)} %pad_maximum_fusion.10), channel_id=1, source_target_pairs={{0,8},{8,16},{16,24},{24,0},{1,9},{9,17},{17,25},{25,1},{2,10},{10... | collective-permute-start | bytes 258056 | tf_op jit(solution)/shard_map/ppermute | solution.py:667
  (267 other events, 2011.8 us)
Sparse Core Ops, SparseCore 0:
  10.9 51.2 all-gather.12
  64.4 92.8 all-gather.14
  169.4 80.6 all-gather.16
  251.5 56.1 all-gather.18
  327.1 80.6 all-gather.20
  409.2 56.3 all-gather.22
  615.4 80.1 reduce-scatter.6
  698.0 46.9 reduce-scatter.8
  771.9 81.2 reduce-scatter.10
  856.0 46.9 reduce-scatter.12
  929.8 81.1 reduce-scatter.14
  1018.9 62.1 reduce-scatter.16
